TPU v7x, 32 devices: a whole 2x2x4 slice. The times are simulated.
32 devices in a mesh: sn: 8 (over y, x, core), rhs: 4 (over z).
Axes of the slice: x: 2, y: 2, z: 4, core: 2. Of those that a mesh axis runs over, the one named last changes fastest.
Arguments:
- rhs_leaf: float32 [256, 256, 128], P('sn', 'rhs'), may hold values from -6 to 6
- rhs_top: float32 [8, 256, 128], P('sn', 'rhs'), may hold values from -6 to 6
- leaf_blocks: float32 [256, 3, 128, 128], P('sn', None, 'rhs'), may hold values from -0.078125 to 0.078125
- leaf_dinv: float32 [256, 128, 128], P('sn', 'rhs')
- leaf_struct: int32 [256, 3], P('sn'), may hold values from 1 to 39, as said below
- top_blocks: float32 [8, 8, 128, 128], P(None, 'sn', 'rhs'), may hold values from -0.1875 to 0.1875
- top_dinv: float32 [8, 128, 128], P('sn', 'rhs')
Outputs:
- leaf_solution: float32 [256, 256, 128], P('sn', 'rhs')
- top_solution: float32 [8, 256, 128], P('sn', 'rhs')
Inputs may be any that keep to these rules, and one draw needn't show every extreme that they name: `leaf_struct`: subtree d hangs below top supernode a = 4 * (d // 4). Row d * 32 + s names 3 distinct ancestors of leaf supernode s of subtree d: a value v < 32 is supernode v of the same subtree, with v > s; a value 32 + k is a top supernode k on a's path to the root, that is k = a or the factor holds top block (k, a). Column 0 is the elimination tree parent: s + 1, except for the subtree's last supernode, whose parent is 32 + a.
All inputs are finite; a program needn't handle non-finite values.
Results may differ from a plain program's by a relative error of at most 0.00018.
Values sent between devices are 32-bit elements; how exact they have to be, the bound alone decides.
No kernel may reach another device: no remote copies, remote signals or barrier semaphores. Data moves between devices by JAX's collectives and lax.ppermute only.
A program may use at most 64 MiB of HBM per device.

v0:
```python
import functools

import jax
import jax.numpy as jnp
import numpy as np
from jax import lax
from jax.experimental import pallas as pl
from jax.experimental.pallas import tpu as pltpu
from jax.sharding import Mesh
from jax.sharding import PartitionSpec as P

CHUNKS = 4
f32 = jnp.float32
bf16 = jnp.bfloat16
SMEM = pl.BlockSpec(memory_space=pltpu.SMEM)
VMEM = pl.BlockSpec(memory_space=pltpu.VMEM)


def params():
    return pltpu.CompilerParams(vmem_limit_bytes=40 * 2**20)


def split(value):
    high = value.astype(bf16)
    return high, (value - high.astype(f32)).astype(bf16)


def product(left, right, transposed):
    dims = (((1,), (1 if transposed else 0,)), ((), ()))

    def dot(a, b):
        return lax.dot_general(a, b, dims, preferred_element_type=f32)

    return dot(left[0], right[0]) + (dot(left[1], right[0]) + dot(left[0], right[1]))


def ancestors_of(tops):
    def level(t):
        return ((t + 1) & -(t + 1)).bit_length() - 1

    return [[t for t in range(j + 1, tops) if t + 1 - 2 ** level(t) <= j] for j in range(tops)]


def paths_of(subtrees, above):
    return [[4 * (d // 4)] + above[4 * (d // 4)] for d in range(subtrees)]


def padded(rows, width):
    return np.array([row + [row[0] if row else 0] * (width - len(row)) for row in rows], np.int32)


def forward_kernel(base, first, last, width, *refs):
    meta, pieces, sides = refs[0], refs[1:5], refs[5]
    refs = refs[6:]
    if not first:
        acc_in, refs = refs[0], refs[1:]
    acc, high, low, scaled, refs = refs[0], refs[1], refs[2], refs[3], refs[4:]
    if last:
        payload, refs = refs[0], refs[1:]
    full = refs[0]
    steps, columns, rows = scaled.shape[0], scaled.shape[1], pieces[0].shape[2]
    leafs = steps * CHUNKS
    wide = full.shape[2]
    for place, piece in enumerate(pieces):
        offset = pl.multiple_of(meta[3 * leafs + place] * rows, rows)
        full[:, :, pl.ds(offset, rows), :] = piece[...]
    if first:
        acc[...] = jnp.zeros_like(acc)
    else:
        acc[...] = acc_in[...]
    for s in range(steps):
        blocks = split(full[s, 0:3].reshape(3 * wide, wide))
        merged = split(product(blocks, split(full[s, 3]), False))
        high[s] = merged[0]
        low[s] = merged[1]
    for s in range(steps):
        at = (base + s) * columns
        source = split(sides[at : at + columns] - acc[base + s])
        outgoing = product(source, (high[s], low[s]), True)
        for r in range(3):
            target = meta[3 * (base + s) + r]
            acc[target] = acc[target] + outgoing[:, r * wide : (r + 1) * wide]
        inverse = split(full[s, 3])
        solved = split(product(source, inverse, True))
        scaled[s] = product(solved, inverse, False)
    if last:
        peers, part = payload.shape[0], payload.shape[2]
        groups = columns // part
        for i in range(width + 1):
            if i < width:
                node = acc[leafs + meta[3 * leafs + 4 + i]]
            else:
                node = sides[leafs * columns : (leafs + 1) * columns]
            for p in range(peers):
                at = (p % groups) * part
                payload[p, i] = node[at : at + part]


def backward_kernel(base, first, width, meta, high, low, scaled, state, out, z):
    steps, wide = scaled.shape[0], scaled.shape[2]
    leafs = steps * CHUNKS
    if first:
        part = state.shape[2]
        groups = scaled.shape[1] // part
        z[...] = jnp.zeros_like(z)
        for i in range(width):
            node = leafs + meta[3 * leafs + 4 + i]
            for p in range(groups):
                z[node, p * part : (p + 1) * part, :] = state[p, i]
    else:
        z[...] = state[...]
    for s in range(steps - 1, -1, -1):
        total = scaled[s]
        for r in (2, 1, 0):
            source = split(z[meta[3 * (base + s) + r]])
            at = slice(r * wide, (r + 1) * wide)
            total = total - product(source, (high[s, at], low[s, at]), False)
        z[base + s] = total
        out[s] = total


def top_prepare_kernel(meta, top, high, low, inverse_high, inverse_low, full):
    blocks, rows, wide = top.shape[2], top.shape[3], top.shape[4]
    for place in range(top.shape[1]):
        offset = pl.multiple_of(meta[place] * rows, rows)
        full[:, pl.ds(offset, rows), :] = top[0, place]
    inverse = split(full[blocks - 1])
    merged = product(split(full[: blocks - 1].reshape((blocks - 1) * wide, wide)), inverse, False)
    high[0], low[0] = split(merged)
    inverse_high[0], inverse_low[0] = inverse


def top_kernel(above, paths, incoming, high, low, inverse_high, inverse_low, outgoing):
    tops, wide = len(above), high.shape[2]
    width = outgoing.shape[1] - 1
    sources = [incoming[t, width] for t in range(tops)]
    for d, path in enumerate(paths):
        for i, t in enumerate(path):
            sources[t] = sources[t] - incoming[d, i]
    scaled = []
    for j in range(tops):
        source = split(sources[j])
        count = len(above[j])
        if count:
            rows = slice(0, count * wide)
            updates = product(source, (high[j, rows], low[j, rows]), True)
            for i, t in enumerate(above[j]):
                sources[t] = sources[t] - updates[:, i * wide : (i + 1) * wide]
        inverse = (inverse_high[j], inverse_low[j])
        scaled.append(product(split(product(source, inverse, True)), inverse, False))
    solved = [None] * tops
    parts = [None] * tops
    for j in range(tops - 1, -1, -1):
        total = scaled[j]
        for i, t in enumerate(above[j]):
            rows = slice(i * wide, (i + 1) * wide)
            total = total - product(parts[t], (high[j, rows], low[j, rows]), False)
        solved[j] = total
        parts[j] = split(total)
    for p in range(outgoing.shape[0]):
        path = paths[p]
        for i in range(width):
            outgoing[p, i] = solved[path[i] if i < len(path) else path[0]]
        outgoing[p, width] = solved[p]


def local(rhs_leaf, rhs_top, leaf_blocks, leaf_dinv, leaf_struct, top_blocks, top_dinv):
    leafs, columns, wide = rhs_leaf.shape
    tops = top_blocks.shape[0]
    steps = leafs // CHUNKS
    above = ancestors_of(tops)
    most = max(len(row) for row in above)
    width = most + 1
    paths = paths_of(tops, above)
    groups = min(tops, columns // 8)
    part = columns // groups

    core, zh, zl = lax.axis_index("core"), lax.axis_index("zh"), lax.axis_index("zl")
    xy = lax.axis_index("xy")

    def swap(value):
        return lax.ppermute(value, ("core", "zh"), [(0, 0), (1, 2), (2, 1), (3, 3)])

    def other(value, axis):
        return lax.ppermute(value, axis, [(0, 1), (1, 0)])

    def after(first, value):
        return lax.optimization_barrier((first, value))[1]

    own = []
    for k in range(CHUNKS):
        at = slice(k * steps, (k + 1) * steps)
        own.append(jnp.concatenate([leaf_blocks[at], leaf_dinv[at][:, None]], axis=1))
    names = jnp.zeros((8, wide), f32).at[:3, :leafs].set(leaf_struct.T.astype(f32))
    sides = jnp.concatenate([rhs_leaf.reshape(-1, wide), rhs_top.reshape(-1, wide), names], axis=0)

    swapped = [swap(value) for value in own]
    sides = swap(sides)
    nearby = [other(x1, "zl") for x1 in swapped]

    chosen = jnp.take(top_blocks[:, 0], jnp.asarray(padded(above, most))[2 * xy + core], axis=0)
    top = after(sides, jnp.concatenate([chosen, top_dinv], axis=0))
    top = jnp.stack([top, other(top, "zh")])
    top = jnp.concatenate([top, other(top, "zl")])
    top = lax.all_gather(top, ("xy", "core"), axis=0, tiled=False)

    names = sides[(leafs + 1) * columns :][:3, :leafs].T.astype(jnp.int32).reshape(-1)
    path = jnp.asarray(padded(paths, width))[2 * xy + zh]
    places = jnp.stack([2 * core + zl, 2 * core + 1 - zl, 2 - 2 * core + zl, 3 - 2 * core - zl])
    meta = jnp.concatenate([names, places.astype(jnp.int32), path])

    def whole(*shape):
        return pl.BlockSpec((1,) + shape, lambda t: (t,) + (0,) * len(shape))

    top_places = jnp.stack([2 * zh + zl, 2 - 2 * zh + zl, 2 * zh + 1 - zl, 3 - 2 * zh - zl])
    top_factor = pl.pallas_call(
        top_prepare_kernel,
        grid=(tops,),
        in_specs=[SMEM, whole(*top.shape[1:])],
        out_specs=[whole(most * wide, wide)] * 2 + [whole(wide, wide)] * 2,
        out_shape=[jax.ShapeDtypeStruct((tops, most * wide, wide), bf16)] * 2
        + [jax.ShapeDtypeStruct((tops, wide, wide), bf16)] * 2,
        scratch_shapes=[pltpu.VMEM((width, wide, wide), f32)],
        compiler_params=params(),
        name="top_prepare",
    )(top_places.astype(jnp.int32), top)

    vectors = jax.ShapeDtypeStruct((leafs + tops, columns, wide), f32)
    merged = jax.ShapeDtypeStruct((steps, 3 * wide, wide), bf16)
    chunk = jax.ShapeDtypeStruct((steps, columns, wide), f32)
    cost = pl.CostEstimate(flops=4 * 10**9, bytes_accessed=8 * 2**20, transcendentals=0)
    factors, state = [], None
    for k in range(CHUNKS):
        last = k == CHUNKS - 1
        shapes = [vectors, merged, merged, chunk]
        x1, x2 = after(swapped[-1], swapped[k]), after(swapped[-1], nearby[k])
        if last:
            x2 = after(state, x2)
        pieces = (x1, x2, other(x1, "core"), other(x2, "core"))
        if last:
            shapes.append(jax.ShapeDtypeStruct((tops, width + 1, part, wide), f32))
        if k == CHUNKS - 2:
            state = after(top_factor, state)
        results = pl.pallas_call(
            functools.partial(forward_kernel, k * steps, k == 0, last, width),
            in_specs=[SMEM] + [VMEM] * (5 + (k > 0)),
            out_specs=[VMEM] * len(shapes),
            out_shape=shapes,
            scratch_shapes=[pltpu.VMEM((steps, 4, wide, wide), f32)],
            compiler_params=params(),
            cost_estimate=cost,
            name="leaf_forward",
        )(meta, *pieces, sides, *(() if k == 0 else (state,)))
        state = results[0]
        factors.append(results[1:4])

    incoming = lax.all_to_all(results[4], ("xy", "zh"), split_axis=0, concat_axis=0, tiled=True)
    outgoing = pl.pallas_call(
        functools.partial(top_kernel, above, paths),
        in_specs=[VMEM] * 5,
        out_specs=VMEM,
        out_shape=jax.ShapeDtypeStruct((tops, width + 1, part, wide), f32),
        compiler_params=params(),
        name="top_solve",
    )(incoming, *top_factor)
    state = lax.all_to_all(outgoing, ("xy", "zh"), split_axis=0, concat_axis=0, tiled=True)
    own_top = state[:groups, width].reshape(1, columns, wide)

    found = [None] * CHUNKS
    for k in range(CHUNKS - 1, -1, -1):
        found[k], state = pl.pallas_call(
            functools.partial(backward_kernel, k * steps, k == CHUNKS - 1, width),
            in_specs=[SMEM] + [VMEM] * 4,
            out_specs=[VMEM] * 2,
            out_shape=[chunk, vectors],
            compiler_params=params(),
            cost_estimate=cost,
            name="leaf_backward",
        )(meta, *factors[k], state)
    late = swap(found[-1])
    middle = swap(jnp.concatenate(found[1:-1] + [own_top], axis=0))
    early = swap(after(late, found[0]))
    leaf_solution = jnp.concatenate([early, middle[:-1], late], axis=0)
    return (leaf_solution, middle[-1:])


def solution(mesh):
    subtrees, quarters = mesh.devices.shape
    fine = Mesh(
        mesh.devices.reshape(subtrees // 2, 2, 2, quarters // 2), ("xy", "core", "zh", "zl")
    )
    sn, rhs = ("xy", "core"), ("zh", "zl")
    return jax.shard_map(
        local,
        mesh=fine,
        in_specs=(
            P(sn, rhs, None),
            P(sn, rhs, None),
            P(sn, None, rhs, None),
            P(sn, rhs, None),
            P(sn, None),
            P(None, sn, rhs, None),
            P(sn, rhs, None),
        ),
        out_specs=(P(sn, rhs, None), P(sn, rhs, None)),
        check_vma=False,
    )
```

profile of v0, /device:TPU:1, one launch (start us, length us, event | category | flops | bytes accessed | tf_op | source)
XLA Modules:
  0.0 225.6 jit_solution(6295949483480593919)
XLA Ops:
  7.2 0.7 convert_bitcast_fusion
  7.9 2.3 %select_maximum_fusion = f32[2120,128]{1,0:T(8,128)} fusion(f32[3,32]{1,0:T(4,128)S(1)} %convert_bitcast_fusion, f32[64,128]{1,0:T(8,128)} %bitcast.43, f32[2048,128]{1,0:T(8,128)} %bitcast.38), kind=kLoop, calls=%fused_computation.1 | loop fusion | flops 1085440 | bytes 2167168 | tf_op jit(solution)/shard_map/concatenate | solution.py:195
  10.3 5.7 %collective-permute-start = (f32[2120,128]{1,0:T(8,128)}, f32[2120,128]{1,0:T(8,128)S(1)}, u32[]{:S(2)}, u32[]{:S(2)}) collective-permute-start(f32[2120,128]{1,0:T(8,128)} %select_maximum_fusion), channel_id=1, source_target_pairs={{0,0},{2,4},{4,2},{6,6},{1,1},{3,5},{5,3},{7,7},{8,8},{10,12},{12,... | collective-permute-start | bytes 3256328 | tf_op jit(solution)/shard_map/ppermute | solution.py:182
  18.1 22.6 %collective-permute-done.refs_5_ = f32[2120,128]{1,0:T(8,128)S(1)} collective-permute-done((f32[2120,128]{1,0:T(8,128)}, f32[2120,128]{1,0:T(8,128)S(1)}, u32[]{:S(2)}, u32[]{:S(2)}) %collective-permute-start) | collective-permute-done | bytes 1085472 | tf_op jit(solution)/shard_map/ppermute | solution.py:182
  40.7 4.7 %collective-permute-done.6 = f32[4,32,128]{2,1,0:T(8,128)S(1)} collective-permute-done((f32[4,32,128]{2,1,0:T(8,128)S(1)}, f32[4,32,128]{2,1,0:T(8,128)S(1)}, u32[]{:S(2)}, u32[]{:S(2)}) %collective-permute-start.6) | collective-permute-done | bytes 65568 | tf_op jit(solution)/shard_map/ppermute | solution.py:185
  45.5 5.1 %collective-permute-done.7 = f32[2,4,32,128]{3,2,1,0:T(8,128)S(1)} collective-permute-done((f32[2,4,32,128]{3,2,1,0:T(8,128)S(1)}, f32[2,4,32,128]{3,2,1,0:T(8,128)S(1)}, u32[]{:S(2)}, u32[]{:S(2)}) %collective-permute-start.7) | collective-permute-done | bytes 131104 | tf_op jit(solution)/shard_map/ppermute | solution.py:185
  50.6 0.7 pad_maximum_fusion.6
  51.7 4.4 %collective-permute-start.12 = (f32[8,4,32,128]{3,2,1,0:T(8,128)S(1)}, f32[8,4,32,128]{3,2,1,0:T(8,128)}, u32[]{:S(2)}, u32[]{:S(2)}) collective-permute-start(f32[8,4,32,128]{3,2,1,0:T(8,128)S(1)} %pad_maximum_fusion.5), channel_id=1, source_target_pairs={{0,0},{2,4},{4,2},{6,6},{1,1},{3,5},{5,3},{7,7},{8,8},{10,12},{12,... | collective-permute-start | bytes 1572872 | tf_op jit(solution)/shard_map/ppermute | solution.py:182
  56.1 2.1 collective-permute-start.8
  58.2 4.4 %collective-permute-start.1 = (f32[8,4,32,128]{3,2,1,0:T(8,128)S(1)}, f32[8,4,32,128]{3,2,1,0:T(8,128)S(1)}, u32[]{:S(2)}, u32[]{:S(2)}) collective-permute-start(f32[8,4,32,128]{3,2,1,0:T(8,128)S(1)} %pad_maximum_fusion.2), channel_id=1, source_target_pairs={{0,0},{2,4},{4,2},{6,6},{1,1},{3,5},{5,3},{7,7},{8,8},{10,12},{12,... | collective-permute-start | bytes 1572872 | tf_op jit(solution)/shard_map/ppermute | solution.py:182
  62.7 2.1 collective-permute-start.2
  64.8 2.7 %collective-permute-done.12.refs_1_ = f32[8,4,32,128]{3,2,1,0:T(8,128)} collective-permute-done((f32[8,4,32,128]{3,2,1,0:T(8,128)S(1)}, f32[8,4,32,128]{3,2,1,0:T(8,128)}, u32[]{:S(2)}, u32[]{:S(2)}) %collective-permute-start.12) | collective-permute-done | bytes 524320 | tf_op jit(solution)/shard_map/ppermute | solution.py:182
  67.4 3.1 %collective-permute-start.13 = (f32[8,4,32,128]{3,2,1,0:T(8,128)}, f32[8,4,32,128]{3,2,1,0:T(8,128)}, u32[]{:S(2)}, u32[]{:S(2)}) collective-permute-start(f32[8,4,32,128]{3,2,1,0:T(8,128)} %collective-permute-done.12.refs_1_), channel_id=1, source_target_pairs={{0,1},{1,0},{2,3},{3,2},{4,5},{5,4},{6,7},{7,6},{8,9},{9,8},{10,11... | collective-permute-start | bytes 1572872 | tf_op jit(solution)/shard_map/ppermute | solution.py:185
  70.5 8.1 %collective-permute-done.8.refs_1_ = f32[8,4,32,128]{3,2,1,0:T(8,128)S(1)} collective-permute-done((f32[8,4,32,128]{3,2,1,0:T(8,128)S(1)}, f32[8,4,32,128]{3,2,1,0:T(8,128)S(1)}, u32[]{:S(2)}, u32[]{:S(2)}) %collective-permute-start.8) | collective-permute-done | bytes 524320 | tf_op jit(solution)/shard_map/ppermute | solution.py:182
  78.6 3.2 %collective-permute-start.9 = (f32[8,4,32,128]{3,2,1,0:T(8,128)S(1)}, f32[8,4,32,128]{3,2,1,0:T(8,128)}, u32[]{:S(2)}, u32[]{:S(2)}) collective-permute-start(f32[8,4,32,128]{3,2,1,0:T(8,128)S(1)} %collective-permute-done.8.refs_1_), channel_id=1, source_target_pairs={{0,1},{1,0},{2,3},{3,2},{4,5},{5,4},{6,7},{7,6},{8,9},{9,8},{10,11... | collective-permute-start | bytes 1572872 | tf_op jit(solution)/shard_map/ppermute | solution.py:185
  81.8 8.0 %collective-permute-done.1.refs_1_ = f32[8,4,32,128]{3,2,1,0:T(8,128)S(1)} collective-permute-done((f32[8,4,32,128]{3,2,1,0:T(8,128)S(1)}, f32[8,4,32,128]{3,2,1,0:T(8,128)S(1)}, u32[]{:S(2)}, u32[]{:S(2)}) %collective-permute-start.1) | collective-permute-done | bytes 524320 | tf_op jit(solution)/shard_map/ppermute | solution.py:182
  89.8 3.2 %collective-permute-start.16 = (f32[8,4,32,128]{3,2,1,0:T(8,128)S(1)}, f32[8,4,32,128]{3,2,1,0:T(8,128)S(1)}, u32[]{:S(2)}, u32[]{:S(2)}) collective-permute-start(f32[8,4,32,128]{3,2,1,0:T(8,128)S(1)} %collective-permute-done.1.refs_1_), channel_id=1, source_target_pairs={{0,1},{1,0},{2,3},{3,2},{4,5},{5,4},{6,7},{7,6},{8,9},{9,8},{10,11... | collective-permute-start | bytes 1572872 | tf_op jit(solution)/shard_map/ppermute | solution.py:185
  93.0 9.5 %collective-permute-done.2.refs_1_ = f32[8,4,32,128]{3,2,1,0:T(8,128)S(1)} collective-permute-done((f32[8,4,32,128]{3,2,1,0:T(8,128)S(1)}, f32[8,4,32,128]{3,2,1,0:T(8,128)S(1)}, u32[]{:S(2)}, u32[]{:S(2)}) %collective-permute-start.2) | collective-permute-done | bytes 524320 | tf_op jit(solution)/shard_map/ppermute | solution.py:182
  102.7 4.5 %collective-permute-done.13.refs_2_ = f32[8,4,32,128]{3,2,1,0:T(8,128)} collective-permute-done((f32[8,4,32,128]{3,2,1,0:T(8,128)}, f32[8,4,32,128]{3,2,1,0:T(8,128)}, u32[]{:S(2)}, u32[]{:S(2)}) %collective-permute-start.13) | collective-permute-done | bytes 524320 | tf_op jit(solution)/shard_map/ppermute | solution.py:185
  108.0 4.7 %collective-permute-done.9.refs_2_ = f32[8,4,32,128]{3,2,1,0:T(8,128)} collective-permute-done((f32[8,4,32,128]{3,2,1,0:T(8,128)S(1)}, f32[8,4,32,128]{3,2,1,0:T(8,128)}, u32[]{:S(2)}, u32[]{:S(2)}) %collective-permute-start.9) | collective-permute-done | bytes 524320 | tf_op jit(solution)/shard_map/ppermute | solution.py:185
  112.7 6.8 %collective-permute-done.16.refs_2_ = f32[8,4,32,128]{3,2,1,0:T(8,128)S(1)} collective-permute-done((f32[8,4,32,128]{3,2,1,0:T(8,128)S(1)}, f32[8,4,32,128]{3,2,1,0:T(8,128)S(1)}, u32[]{:S(2)}, u32[]{:S(2)}) %collective-permute-start.16) | collective-permute-done | bytes 524320 | tf_op jit(solution)/shard_map/ppermute | solution.py:185
  119.5 5.7 %collective-permute-done.3.refs_2_ = f32[8,4,32,128]{3,2,1,0:T(8,128)} collective-permute-done((f32[8,4,32,128]{3,2,1,0:T(8,128)S(1)}, f32[8,4,32,128]{3,2,1,0:T(8,128)}, u32[]{:S(2)}, u32[]{:S(2)}) %collective-permute-start.3) | collective-permute-done | bytes 524320 | tf_op jit(solution)/shard_map/ppermute | solution.py:185
  126.2 5.2 %leaf_forward.4 = (f32[40,64,128]{2,1,0:T(8,128)S(1)}, bf16[8,384,128]{2,1,0:T(8,128)(2,1)S(1)}, bf16[8,384,128]{2,1,0:T(8,128)(2,1)S(1)}, f32[8,64,128]{2,1,0:T(8,128)S(1)}) custom-call(s32[104]{0:T(128)S(1)} %concatenate.34.refs_0_.meta, f32[8,4,32,128]{3,2,1,0:T(8,128)} %collective-permute-done.12.refs_1_, ...), custom_call_target="tpu_custom_call" | custom-call | flops 4000000000 | bytes 8388608 | tf_op jit(solution)/shard_map/leaf_forward/pallas_call | solution.py:244
  131.4 0.9 copy-done.8
  132.3 0.9 copy-done.10
  133.9 5.0 %leaf_forward.5 = (f32[40,64,128]{2,1,0:T(8,128)S(1)}, bf16[8,384,128]{2,1,0:T(8,128)(2,1)S(1)}, bf16[8,384,128]{2,1,0:T(8,128)(2,1)S(1)}, f32[8,64,128]{2,1,0:T(8,128)S(1)}) custom-call(s32[104]{0:T(128)S(1)} %concatenate.34.refs_0_.meta, f32[8,4,32,128]{3,2,1,0:T(8,128)S(1)} %collective-permute-done.8.refs_1_, ...), custom_call_target="tpu_custom_call" | custom-call | flops 4000000000 | bytes 8388608 | tf_op jit(solution)/shard_map/leaf_forward/pallas_call | solution.py:244
  138.9 1.1 copy-done.2
  140.0 0.9 copy-done.4
  140.9 1.0 copy-done.6
  141.8 0.7 copy-done.12
  142.6 1.6 copy-done.1
  144.1 2.8 %top_prepare.1 = (bf16[8,384,128]{2,1,0:T(8,128)(2,1)S(1)}, bf16[8,384,128]{2,1,0:T(8,128)(2,1)S(1)}, bf16[8,128,128]{2,1,0:T(8,128)(2,1)S(1)}, bf16[8,128,128]{2,1,0:T(8,128)(2,1)S(1)}) custom-call(s32[4]{0:T(128)S(1)} %pad_add_fusion.meta, f32[8,4,4,32,128]{4,3,2,1,0:T(8,128)S(1)} %bitcast.37), custom_call_target="tpu_custom_call" | custom-call | tf_op jit(solution)/shard_map/top_prepare/pallas_call | solution.py:216
  146.9 5.0 %leaf_forward.6 = (f32[40,64,128]{2,1,0:T(8,128)S(1)}, bf16[8,384,128]{2,1,0:T(8,128)(2,1)S(1)}, bf16[8,384,128]{2,1,0:T(8,128)(2,1)S(1)}, f32[8,64,128]{2,1,0:T(8,128)S(1)}) custom-call(s32[104]{0:T(128)S(1)} %concatenate.34.refs_0_.meta, f32[8,4,32,128]{3,2,1,0:T(8,128)S(1)} %collective-permute-done.2.refs_1_, ...), custom_call_target="tpu_custom_call" | custom-call | flops 4000000000 | bytes 8388608 | tf_op jit(solution)/shard_map/leaf_forward/pallas_call | solution.py:244
  152.4 1.5 collective-permute-done.18.refs_4_
  153.9 5.8 %leaf_forward.7 = (f32[40,64,128]{2,1,0:T(8,128)}, bf16[8,384,128]{2,1,0:T(8,128)(2,1)S(1)}, bf16[8,384,128]{2,1,0:T(8,128)(2,1)S(1)}, f32[8,64,128]{2,1,0:T(8,128)S(1)}, f32[8,5,8,128]{3,2,1,0:T(8,128)S(1)}) custom-call(s32[104]{0:T(128)S(1)} %concatenate.34.refs_0_.meta, f32[8,4,32,128]{3,2,1,0:T(8,128)S(1)} %collective-permute-done.1.refs_1_, ...), custom_call_target="tpu_custom_call" | custom-call | flops 4000000000 | bytes 8388608 | tf_op jit(solution)/shard_map/leaf_forward/pallas_call | solution.py:244
  159.7 11.5 %all_to_all.10.incoming = f32[8,5,8,128]{3,2,1,0:T(8,128)S(1)} all-to-all(f32[8,5,8,128]{3,2,1,0:T(8,128)S(1)} %get-tuple-element.74), channel_id=1, replica_groups=mesh['xy'=4,'core'=2,'zh'=2,'zl'=2] {'xy','zh'}, dimensions={0} | all-to-all | bytes 327680 | tf_op jit(solution)/shard_map/all_to_all | solution.py:257
  171.2 2.7 %top_solve.1 = f32[8,5,8,128]{3,2,1,0:T(8,128)S(1)} custom-call(f32[8,5,8,128]{3,2,1,0:T(8,128)S(1)} %all_to_all.10.incoming, bf16[8,384,128]{2,1,0:T(8,128)(2,1)S(1)} %get-tuple-element.57.high, bf16[8,384,128]{2,1,0:T(8,128)(2,1)S(1)} %get-tuple-element.58.low, bf16[8,128,128]{2,1,0:T(8,128)(2,1)S(1)} %get-tuple-element.59.inverse_high, ...), custom_call_target="tpu_custom_call" | custom-call | tf_op jit(solution)/shard_map/top_solve/pallas_call | solution.py:258
  173.9 9.2 %all_to_all.11.state = f32[8,5,8,128]{3,2,1,0:T(8,128)S(1)} all-to-all(f32[8,5,8,128]{3,2,1,0:T(8,128)S(1)} %top_solve.1), channel_id=1, replica_groups=mesh['xy'=4,'core'=2,'zh'=2,'zl'=2] {'xy','zh'}, dimensions={0} | all-to-all | bytes 327680 | tf_op jit(solution)/shard_map/all_to_all | solution.py:266
  183.1 2.4 %leaf_backward.4 = (f32[8,64,128]{2,1,0:T(8,128)S(1)}, f32[40,64,128]{2,1,0:T(8,128)S(1)}) custom-call(s32[104]{0:T(128)S(1)} %concatenate.34.refs_0_.meta, bf16[8,384,128]{2,1,0:T(8,128)(2,1)S(1)} %get-tuple-element.71.high, bf16[8,384,128]{2,1,0:T(8,128)(2,1)S(1)} %get-tuple-element.72.low, f32[8,64,128]{2,1,0:T(8,128)S(1)} %get-tuple-element.73.scaled, ...), custom_call_target="tpu_custom_call" | custom-call | flops 4000000000 | bytes 8388608 | tf_op jit(solution)/shard_map/leaf_backward/pallas_call | solution.py:271
  185.6 3.9 %collective-permute-start.19 = (f32[8,64,128]{2,1,0:T(8,128)S(1)}, f32[8,64,128]{2,1,0:T(8,128)S(1)}, u32[]{:S(2)}, u32[]{:S(2)}) collective-permute-start(f32[8,64,128]{2,1,0:T(8,128)S(1)} %get-tuple-element.75), channel_id=1, source_target_pairs={{0,0},{2,4},{4,2},{6,6},{1,1},{3,5},{5,3},{7,7},{8,8},{10,12},{12,... | collective-permute-start | bytes 786440 | tf_op jit(solution)/shard_map/ppermute | solution.py:182
  189.5 2.4 %leaf_backward.5 = (f32[8,64,128]{2,1,0:T(8,128)S(1)}, f32[40,64,128]{2,1,0:T(8,128)S(1)}) custom-call(s32[104]{0:T(128)S(1)} %concatenate.34.refs_0_.meta, bf16[8,384,128]{2,1,0:T(8,128)(2,1)S(1)} %get-tuple-element.82.high, bf16[8,384,128]{2,1,0:T(8,128)(2,1)S(1)} %get-tuple-element.83.low, f32[8,64,128]{2,1,0:T(8,128)S(1)} %get-tuple-element.84.scaled, ...), custom_call_target="tpu_custom_call" | custom-call | flops 4000000000 | bytes 8388608 | tf_op jit(solution)/shard_map/leaf_backward/pallas_call | solution.py:271
  191.9 2.4 %leaf_backward.6 = (f32[8,64,128]{2,1,0:T(8,128)S(1)}, f32[40,64,128]{2,1,0:T(8,128)S(1)}) custom-call(s32[104]{0:T(128)S(1)} %concatenate.34.refs_0_.meta, bf16[8,384,128]{2,1,0:T(8,128)(2,1)S(1)} %copy-done.5, bf16[8,384,128]{2,1,0:T(8,128)(2,1)S(1)} %copy-done.7, f32[8,64,128]{2,1,0:T(8,128)S(1)} %copy-done.13, f32[40,64,128]{2,1,0:T(8,128)S(1)} %get-tuple-element.86.state), custom_call_target="tpu_custom_call" | custom-call | flops 4000000000 | bytes 8388608 | tf_op jit(solution)/shard_map/leaf_backward/pallas_call | solution.py:271
  194.5 2.7 %collective-permute-start.21 = (f32[17,64,128]{2,1,0:T(8,128)S(1)}, f32[17,64,128]{2,1,0:T(8,128)S(1)}, u32[]{:S(2)}, u32[]{:S(2)}) collective-permute-start(f32[17,64,128]{2,1,0:T(8,128)S(1)} %pad_maximum_fusion.1), channel_id=1, source_target_pairs={{0,0},{2,4},{4,2},{6,6},{1,1},{3,5},{5,3},{7,7},{8,8},{10,12},{12,... | collective-permute-start | bytes 1671176 | tf_op jit(solution)/shard_map/ppermute | solution.py:182
  197.3 3.6 %leaf_backward.7 = (f32[8,64,128]{2,1,0:T(8,128)S(1)}, f32[40,64,128]{2,1,0:T(8,128)}) custom-call(s32[104]{0:T(128)S(1)} %concatenate.34.refs_0_.meta, bf16[8,384,128]{2,1,0:T(8,128)(2,1)S(1)} %copy-done.9, bf16[8,384,128]{2,1,0:T(8,128)(2,1)S(1)} %copy-done.11, f32[8,64,128]{2,1,0:T(8,128)S(1)} %copy-done.15, f32[40,64,128]{2,1,0:T(8,128)S(1)} %get-tuple-element.87.state), custom_call_target="tpu_custom_call" | custom-call | flops 4000000000 | bytes 8388608 | tf_op jit(solution)/shard_map/leaf_backward/pallas_call | solution.py:271
  200.8 3.8 %collective-permute-start.20 = (f32[8,64,128]{2,1,0:T(8,128)S(1)}, f32[8,64,128]{2,1,0:T(8,128)S(1)}, u32[]{:S(2)}, u32[]{:S(2)}) collective-permute-start(f32[8,64,128]{2,1,0:T(8,128)S(1)} %get-tuple-element.89), channel_id=1, source_target_pairs={{0,0},{2,4},{4,2},{6,6},{1,1},{3,5},{5,3},{7,7},{8,8},{10,12},{12,... | collective-permute-start | bytes 786440 | tf_op jit(solution)/shard_map/ppermute | solution.py:182
  204.7 10.2 %collective-permute-done.21 = f32[17,64,128]{2,1,0:T(8,128)S(1)} collective-permute-done((f32[17,64,128]{2,1,0:T(8,128)S(1)}, f32[17,64,128]{2,1,0:T(8,128)S(1)}, u32[]{:S(2)}, u32[]{:S(2)}) %collective-permute-start.21) | collective-permute-done | bytes 557088 | tf_op jit(solution)/shard_map/ppermute | solution.py:182
  215.5 2.1 collective-permute-done.20
  217.7 1.1 pad_maximum_fusion
  (76 shorter events, 6.4 us)
Async XLA Ops:
  7.2 9.6 %copy-start = (f32[8,1,32,128]{3,2,1,0:T(8,128)S(1)}, f32[8,1,32,128]{3,2,1,0:T(8,128)}, u32[]{:S(2)}) copy-start(f32[8,1,32,128]{3,2,1,0:T(8,128)} %param.16) | copy-start | bytes 393220
  7.2 135.4 %all-gather.3.cloned.1.call-start = ((), (), s32[]{:S(2)}) async-start(), calls=%async_computation.2 | async-start | bytes 2359296 | tf_op jit(solution)/shard_map/all_gather | solution.py:205
  7.9 10.1 %copy-start.18 = (f32[1,32,128]{2,1,0:T(8,128)S(1)}, f32[1,32,128]{2,1,0:T(8,128)}, u32[]{:S(2)}) copy-start(f32[1,32,128]{2,1,0:T(8,128)} %param.17) | copy-start | bytes 49156
  10.3 41.1 %copy-start.17 = (f32[32,32,128]{2,1,0:T(8,128)S(1)}, f32[32,32,128]{2,1,0:T(8,128)}, u32[]{:S(2)}) copy-start(f32[32,32,128]{2,1,0:T(8,128)} %param.14) | copy-start | bytes 1572868
  10.3 30.4 %collective-permute-start = (f32[2120,128]{1,0:T(8,128)}, f32[2120,128]{1,0:T(8,128)S(1)}, u32[]{:S(2)}, u32[]{:S(2)}) collective-permute-start(f32[2120,128]{1,0:T(8,128)} %select_maximum_fusion), channel_id=1, source_target_pairs={{0,0},{2,4},{4,2},{6,6},{1,1},{3,5},{5,3},{7,7},{8,8},{10,12},{12,... | collective-permute-start | bytes 3256328 | tf_op jit(solution)/shard_map/ppermute | solution.py:182
  18.1 33.4 %copy-start.16 = (f32[32,3,32,128]{3,2,1,0:T(8,128)S(1)}, f32[32,3,32,128]{3,2,1,0:T(8,128)}, u32[]{:S(2)}) copy-start(f32[32,3,32,128]{3,2,1,0:T(8,128)} %param.13) | copy-start | bytes 4718596
  40.7 4.7 %collective-permute-start.6 = (f32[4,32,128]{2,1,0:T(8,128)S(1)}, f32[4,32,128]{2,1,0:T(8,128)S(1)}, u32[]{:S(2)}, u32[]{:S(2)}) collective-permute-start(f32[4,32,128]{2,1,0:T(8,128)S(1)} %pad_maximum_fusion.8), channel_id=1, source_target_pairs={{0,2},{2,0},{1,3},{3,1},{4,6},{6,4},{5,7},{7,5},{8,10},{10,8},{9,1... | collective-permute-start | bytes 196616 | tf_op jit(solution)/shard_map/ppermute | solution.py:185
  45.5 5.2 %collective-permute-start.7 = (f32[2,4,32,128]{3,2,1,0:T(8,128)S(1)}, f32[2,4,32,128]{3,2,1,0:T(8,128)S(1)}, u32[]{:S(2)}, u32[]{:S(2)}) collective-permute-start(f32[2,4,32,128]{3,2,1,0:T(8,128)S(1)} %pad_maximum_fusion.7), channel_id=1, source_target_pairs={{0,1},{1,0},{2,3},{3,2},{4,5},{5,4},{6,7},{7,6},{8,9},{9,8},{10,11... | collective-permute-start | bytes 393224 | tf_op jit(solution)/shard_map/ppermute | solution.py:185
  51.7 15.8 %collective-permute-start.12 = (f32[8,4,32,128]{3,2,1,0:T(8,128)S(1)}, f32[8,4,32,128]{3,2,1,0:T(8,128)}, u32[]{:S(2)}, u32[]{:S(2)}) collective-permute-start(f32[8,4,32,128]{3,2,1,0:T(8,128)S(1)} %pad_maximum_fusion.5), channel_id=1, source_target_pairs={{0,0},{2,4},{4,2},{6,6},{1,1},{3,5},{5,3},{7,7},{8,8},{10,12},{12,... | collective-permute-start | bytes 1572872 | tf_op jit(solution)/shard_map/ppermute | solution.py:182
  56.1 22.5 %collective-permute-start.8 = (f32[8,4,32,128]{3,2,1,0:T(8,128)S(1)}, f32[8,4,32,128]{3,2,1,0:T(8,128)S(1)}, u32[]{:S(2)}, u32[]{:S(2)}) collective-permute-start(f32[8,4,32,128]{3,2,1,0:T(8,128)S(1)} %pad_maximum_fusion.4), channel_id=1, source_target_pairs={{0,0},{2,4},{4,2},{6,6},{1,1},{3,5},{5,3},{7,7},{8,8},{10,12},{12,... | collective-permute-start | bytes 1572872 | tf_op jit(solution)/shard_map/ppermute | solution.py:182
  58.2 31.6 %collective-permute-start.1 = (f32[8,4,32,128]{3,2,1,0:T(8,128)S(1)}, f32[8,4,32,128]{3,2,1,0:T(8,128)S(1)}, u32[]{:S(2)}, u32[]{:S(2)}) collective-permute-start(f32[8,4,32,128]{3,2,1,0:T(8,128)S(1)} %pad_maximum_fusion.2), channel_id=1, source_target_pairs={{0,0},{2,4},{4,2},{6,6},{1,1},{3,5},{5,3},{7,7},{8,8},{10,12},{12,... | collective-permute-start | bytes 1572872 | tf_op jit(solution)/shard_map/ppermute | solution.py:182
  62.7 39.8 %collective-permute-start.2 = (f32[8,4,32,128]{3,2,1,0:T(8,128)S(1)}, f32[8,4,32,128]{3,2,1,0:T(8,128)S(1)}, u32[]{:S(2)}, u32[]{:S(2)}) collective-permute-start(f32[8,4,32,128]{3,2,1,0:T(8,128)S(1)} %pad_maximum_fusion.3), channel_id=1, source_target_pairs={{0,0},{2,4},{4,2},{6,6},{1,1},{3,5},{5,3},{7,7},{8,8},{10,12},{12,... | collective-permute-start | bytes 1572872 | tf_op jit(solution)/shard_map/ppermute | solution.py:182
  67.4 39.8 %collective-permute-start.13 = (f32[8,4,32,128]{3,2,1,0:T(8,128)}, f32[8,4,32,128]{3,2,1,0:T(8,128)}, u32[]{:S(2)}, u32[]{:S(2)}) collective-permute-start(f32[8,4,32,128]{3,2,1,0:T(8,128)} %collective-permute-done.12.refs_1_), channel_id=1, source_target_pairs={{0,1},{1,0},{2,3},{3,2},{4,5},{5,4},{6,7},{7,6},{8,9},{9,8},{10,11... | collective-permute-start | bytes 1572872 | tf_op jit(solution)/shard_map/ppermute | solution.py:185
  78.6 34.1 %collective-permute-start.9 = (f32[8,4,32,128]{3,2,1,0:T(8,128)S(1)}, f32[8,4,32,128]{3,2,1,0:T(8,128)}, u32[]{:S(2)}, u32[]{:S(2)}) collective-permute-start(f32[8,4,32,128]{3,2,1,0:T(8,128)S(1)} %collective-permute-done.8.refs_1_), channel_id=1, source_target_pairs={{0,1},{1,0},{2,3},{3,2},{4,5},{5,4},{6,7},{7,6},{8,9},{9,8},{10,11... | collective-permute-start | bytes 1572872 | tf_op jit(solution)/shard_map/ppermute | solution.py:185
  89.8 29.7 %collective-permute-start.16 = (f32[8,4,32,128]{3,2,1,0:T(8,128)S(1)}, f32[8,4,32,128]{3,2,1,0:T(8,128)S(1)}, u32[]{:S(2)}, u32[]{:S(2)}) collective-permute-start(f32[8,4,32,128]{3,2,1,0:T(8,128)S(1)} %collective-permute-done.1.refs_1_), channel_id=1, source_target_pairs={{0,1},{1,0},{2,3},{3,2},{4,5},{5,4},{6,7},{7,6},{8,9},{9,8},{10,11... | collective-permute-start | bytes 1572872 | tf_op jit(solution)/shard_map/ppermute | solution.py:185
  102.5 22.7 %collective-permute-start.3 = (f32[8,4,32,128]{3,2,1,0:T(8,128)S(1)}, f32[8,4,32,128]{3,2,1,0:T(8,128)}, u32[]{:S(2)}, u32[]{:S(2)}) collective-permute-start(f32[8,4,32,128]{3,2,1,0:T(8,128)S(1)} %collective-permute-done.2.refs_1_), channel_id=1, source_target_pairs={{0,1},{1,0},{2,3},{3,2},{4,5},{5,4},{6,7},{7,6},{8,9},{9,8},{10,11... | collective-permute-start | bytes 1572872 | tf_op jit(solution)/shard_map/ppermute | solution.py:185
  102.7 22.8 %collective-permute-start.14 = (f32[8,4,32,128]{3,2,1,0:T(8,128)}, f32[8,4,32,128]{3,2,1,0:T(8,128)}, u32[]{:S(2)}, u32[]{:S(2)}) collective-permute-start(f32[8,4,32,128]{3,2,1,0:T(8,128)} %collective-permute-done.12.refs_1_), channel_id=1, source_target_pairs={{0,4},{4,0},{1,5},{5,1},{2,6},{6,2},{3,7},{7,3},{8,12},{12,8},{9,1... | collective-permute-start | bytes 1572872 | tf_op jit(solution)/shard_map/ppermute | solution.py:185
  107.2 18.9 %collective-permute-start.15 = (f32[8,4,32,128]{3,2,1,0:T(8,128)}, f32[8,4,32,128]{3,2,1,0:T(8,128)}, u32[]{:S(2)}, u32[]{:S(2)}) collective-permute-start(f32[8,4,32,128]{3,2,1,0:T(8,128)} %collective-permute-done.13.refs_2_), channel_id=1, source_target_pairs={{0,4},{4,0},{1,5},{5,1},{2,6},{6,2},{3,7},{7,3},{8,12},{12,8},{9,1... | collective-permute-start | bytes 1572872 | tf_op jit(solution)/shard_map/ppermute | solution.py:185
  112.7 39.7 %collective-permute-start.17 = (f32[8,4,32,128]{3,2,1,0:T(8,128)S(1)}, f32[8,4,32,128]{3,2,1,0:T(8,128)}, u32[]{:S(2)}, u32[]{:S(2)}) collective-permute-start(f32[8,4,32,128]{3,2,1,0:T(8,128)S(1)} %collective-permute-done.1.refs_1_), channel_id=1, source_target_pairs={{0,4},{4,0},{1,5},{5,1},{2,6},{6,2},{3,7},{7,3},{8,12},{12,8},{9,1... | collective-permute-start | bytes 1572872 | tf_op jit(solution)/shard_map/ppermute | solution.py:185
  119.5 14.4 %collective-permute-start.10 = (f32[8,4,32,128]{3,2,1,0:T(8,128)S(1)}, f32[8,4,32,128]{3,2,1,0:T(8,128)}, u32[]{:S(2)}, u32[]{:S(2)}) collective-permute-start(f32[8,4,32,128]{3,2,1,0:T(8,128)S(1)} %collective-permute-done.8.refs_1_), channel_id=1, source_target_pairs={{0,4},{4,0},{1,5},{5,1},{2,6},{6,2},{3,7},{7,3},{8,12},{12,8},{9,1... | collective-permute-start | bytes 1572872 | tf_op jit(solution)/shard_map/ppermute | solution.py:185
  125.2 8.7 %collective-permute-start.11 = (f32[8,4,32,128]{3,2,1,0:T(8,128)}, f32[8,4,32,128]{3,2,1,0:T(8,128)}, u32[]{:S(2)}, u32[]{:S(2)}) collective-permute-start(f32[8,4,32,128]{3,2,1,0:T(8,128)} %collective-permute-done.9.refs_2_), channel_id=1, source_target_pairs={{0,4},{4,0},{1,5},{5,1},{2,6},{6,2},{3,7},{7,3},{8,12},{12,8},{9,1... | collective-permute-start | bytes 1572872 | tf_op jit(solution)/shard_map/ppermute | solution.py:185
  125.5 21.4 %collective-permute-start.4 = (f32[8,4,32,128]{3,2,1,0:T(8,128)S(1)}, f32[8,4,32,128]{3,2,1,0:T(8,128)}, u32[]{:S(2)}, u32[]{:S(2)}) collective-permute-start(f32[8,4,32,128]{3,2,1,0:T(8,128)S(1)} %collective-permute-done.2.refs_1_), channel_id=1, source_target_pairs={{0,4},{4,0},{1,5},{5,1},{2,6},{6,2},{3,7},{7,3},{8,12},{12,8},{9,1... | collective-permute-start | bytes 1572872 | tf_op jit(solution)/shard_map/ppermute | solution.py:185
  126.1 20.9 %collective-permute-start.5 = (f32[8,4,32,128]{3,2,1,0:T(8,128)}, f32[8,4,32,128]{3,2,1,0:T(8,128)}, u32[]{:S(2)}, u32[]{:S(2)}) collective-permute-start(f32[8,4,32,128]{3,2,1,0:T(8,128)} %collective-permute-done.3.refs_2_), channel_id=1, source_target_pairs={{0,4},{4,0},{1,5},{5,1},{2,6},{6,2},{3,7},{7,3},{8,12},{12,8},{9,1... | collective-permute-start | bytes 1572872 | tf_op jit(solution)/shard_map/ppermute | solution.py:185
  131.4 0.9 copy-start.8
  132.3 0.9 copy-start.10
  133.2 0.7 copy-start.14
  138.9 1.1 copy-start.2
  140.0 0.9 copy-start.4
  140.9 1.0 copy-start.6
  141.8 0.7 copy-start.12
  142.6 1.6 copy-start.1
  144.1 2.8 %copy-start.3 = (f32[40,64,128]{2,1,0:T(8,128)S(1)}, f32[40,64,128]{2,1,0:T(8,128)}, u32[]{:S(2)}) copy-start(f32[40,64,128]{2,1,0:T(8,128)} %copy-done.2) | copy-start | bytes 3932164
  151.9 2.0 collective-permute-start.18
  185.6 15.3 %collective-permute-start.19 = (f32[8,64,128]{2,1,0:T(8,128)S(1)}, f32[8,64,128]{2,1,0:T(8,128)S(1)}, u32[]{:S(2)}, u32[]{:S(2)}) collective-permute-start(f32[8,64,128]{2,1,0:T(8,128)S(1)} %get-tuple-element.75), channel_id=1, source_target_pairs={{0,0},{2,4},{4,2},{6,6},{1,1},{3,5},{5,3},{7,7},{8,8},{10,12},{12,... | collective-permute-start | bytes 786440 | tf_op jit(solution)/shard_map/ppermute | solution.py:182
  189.4 2.5 %copy-start.5 = (bf16[8,384,128]{2,1,0:T(8,128)(2,1)S(1)}, bf16[8,384,128]{2,1,0:T(8,128)(2,1)}, u32[]{:S(2)}) copy-start(bf16[8,384,128]{2,1,0:T(8,128)(2,1)} %copy-done.4) | copy-start | bytes 2359300
  189.4 2.5 %copy-start.7 = (bf16[8,384,128]{2,1,0:T(8,128)(2,1)S(1)}, bf16[8,384,128]{2,1,0:T(8,128)(2,1)}, u32[]{:S(2)}) copy-start(bf16[8,384,128]{2,1,0:T(8,128)(2,1)} %copy-done.6) | copy-start | bytes 2359300
  189.5 2.5 %copy-start.13 = (f32[8,64,128]{2,1,0:T(8,128)S(1)}, f32[8,64,128]{2,1,0:T(8,128)}, u32[]{:S(2)}) copy-start(f32[8,64,128]{2,1,0:T(8,128)} %copy-done.12) | copy-start | bytes 786436
  191.9 5.3 %copy-start.11 = (bf16[8,384,128]{2,1,0:T(8,128)(2,1)S(1)}, bf16[8,384,128]{2,1,0:T(8,128)(2,1)}, u32[]{:S(2)}) copy-start(bf16[8,384,128]{2,1,0:T(8,128)(2,1)} %copy-done.10) | copy-start | bytes 2359300
  194.4 2.9 %copy-start.9 = (bf16[8,384,128]{2,1,0:T(8,128)(2,1)S(1)}, bf16[8,384,128]{2,1,0:T(8,128)(2,1)}, u32[]{:S(2)}) copy-start(bf16[8,384,128]{2,1,0:T(8,128)(2,1)} %copy-done.8) | copy-start | bytes 2359300
  194.4 2.9 %copy-start.15 = (f32[8,64,128]{2,1,0:T(8,128)S(1)}, f32[8,64,128]{2,1,0:T(8,128)}, u32[]{:S(2)}) copy-start(f32[8,64,128]{2,1,0:T(8,128)} %copy-done.14) | copy-start | bytes 786436
  194.5 20.4 %collective-permute-start.21 = (f32[17,64,128]{2,1,0:T(8,128)S(1)}, f32[17,64,128]{2,1,0:T(8,128)S(1)}, u32[]{:S(2)}, u32[]{:S(2)}) collective-permute-start(f32[17,64,128]{2,1,0:T(8,128)S(1)} %pad_maximum_fusion.1), channel_id=1, source_target_pairs={{0,0},{2,4},{4,2},{6,6},{1,1},{3,5},{5,3},{7,7},{8,8},{10,12},{12,... | collective-permute-start | bytes 1671176 | tf_op jit(solution)/shard_map/ppermute | solution.py:182
  200.8 16.8 %collective-permute-start.20 = (f32[8,64,128]{2,1,0:T(8,128)S(1)}, f32[8,64,128]{2,1,0:T(8,128)S(1)}, u32[]{:S(2)}, u32[]{:S(2)}) collective-permute-start(f32[8,64,128]{2,1,0:T(8,128)S(1)} %get-tuple-element.89), channel_id=1, source_target_pairs={{0,0},{2,4},{4,2},{6,6},{1,1},{3,5},{5,3},{7,7},{8,8},{10,12},{12,... | collective-permute-start | bytes 786440 | tf_op jit(solution)/shard_map/ppermute | solution.py:182
Sparse Core Ops, SparseCore 0:
  51.5 29.6 all-gather.2
where the time goes:
time: 226 us
  waiting for transfers between devices  96.3 us (43%)
  starting transfers between devices  40 us (18%)
  Pallas kernels  37.3 us (17%)
  blocking collectives  20.7 us (9%)
  between operations  14.4 us (6%)
  local copies, waits for them, and re-layouts  10.2 us (5%)
  other arithmetic  6.65 us (3%)
    ppermute x8, waiting for transfers between devices, swap(): return lax.ppermute(value, ('core', 'zh'), [(0, 0), (1, 2), (2, 1), (3, 3)])  63.2 us
    ppermute x14, waiting for transfers between devices, other(): return lax.ppermute(value, axis, [(0, 1), (1, 0)])  33.1 us
    ppermute x8, starting transfers between devices, swap(): return lax.ppermute(value, ('core', 'zh'), [(0, 0), (1, 2), (2, 1), (3, 3)])  29.1 us
    pallas_call x4, Pallas kernels, local(): pl.pallas_call(functools.partial(forward_kernel, k * steps, k == 0, last,...  20.9 us
    all_to_all x1, blocking collectives, local(): lax.all_to_all(results[4], ('xy', 'zh'), split_axis=0, concat_axis=0, til...  11.5 us
    pallas_call x4, Pallas kernels, local(): pl.pallas_call(functools.partial(backward_kernel, k * steps, k == CHUNKS...  10.9 us
    ppermute x14, starting transfers between devices, other(): return lax.ppermute(value, axis, [(0, 1), (1, 0)])  10.9 us
    all_to_all x1, blocking collectives, local(): lax.all_to_all(outgoing, ('xy', 'zh'), split_axis=0, concat_axis=0, tiled...  9.24 us
  transfers between devices with their start and end apart: 23, of which 14 were waited for; matrix products, arithmetic and copies ran while one was open for 2% of the time, Pallas kernels for 12%

commit v1 on v0

--- a/solution.py
+++ b/solution.py
@@ -199,7 +199,7 @@
     nearby = [other(x1, "zl") for x1 in swapped]
 
     chosen = jnp.take(top_blocks[:, 0], jnp.asarray(padded(above, most))[2 * xy + core], axis=0)
-    top = after(sides, jnp.concatenate([chosen, top_dinv], axis=0))
+    top = jnp.concatenate([chosen, top_dinv], axis=0)
     top = jnp.stack([top, other(top, "zh")])
     top = jnp.concatenate([top, other(top, "zl")])
     top = lax.all_gather(top, ("xy", "core"), axis=0, tiled=False)
@@ -239,8 +239,6 @@
         pieces = (x1, x2, other(x1, "core"), other(x2, "core"))
         if last:
             shapes.append(jax.ShapeDtypeStruct((tops, width + 1, part, wide), f32))
-        if k == CHUNKS - 2:
-            state = after(top_factor, state)
         results = pl.pallas_call(
             functools.partial(forward_kernel, k * steps, k == 0, last, width),
             in_specs=[SMEM] + [VMEM] * (5 + (k > 0)),

time: 226 us -> 224 us (level)
  blocking collectives: 20.7 us -> 9.72 us
  starting transfers between devices: 40 us -> 46.9 us
  waiting for transfers between devices: 96.3 us -> 91.6 us
  local copies, waits for them, and re-layouts: 10.2 us -> 14.9 us
  other arithmetic: 6.65 us -> 9.13 us
    ppermute x8, waiting for transfers between devices: 63.2 us -> 38 us  [swap(): return lax.ppermute(value, ('core', 'zh'), [(0, 0), (1, 2), (2, 1), (3, 3)])]
    ppermute x14, waiting for transfers between devices: 33.1 us -> 51.9 us  [other(): return lax.ppermute(value, axis, [(0, 1), (1, 0)])]
    all_to_all x1 -> x0, blocking collectives: 11.5 us -> none  [local(): lax.all_to_all(results[4], ('xy', 'zh'), split_axis=0, concat_axis=0, til...]
    ppermute x14, starting transfers between devices: 10.9 us -> 16 us  [other(): return lax.ppermute(value, axis, [(0, 1), (1, 0)])]
    unnamed x38 -> x62, local copies, waits for them, and re-layouts: 7.85 us -> 12.5 us
    all_to_all x0 -> x1, starting transfers between devices: none -> 3.62 us  [local(): lax.all_to_all(results[4], ('xy', 'zh'), split_axis=0, concat_axis=0, til...]
    concatenate x4, other arithmetic: 0.15 us -> 2.56 us  [local(): jnp.concatenate([leaf_blocks[at], leaf_dinv[at][:, None]], axis=1)]
  transfers between devices with their start and end apart: 23 -> 24, of which waited for: 14 -> 13; matrix products, arithmetic and copies ran while one was open for 2% -> 3% of each run, Pallas kernels for 12% -> 14%
where the time goes in v1:
time: 224 us
  waiting for transfers between devices  91.6 us (41%)
  starting transfers between devices  46.9 us (21%)
  Pallas kernels  36.8 us (16%)
  local copies, waits for them, and re-layouts  14.9 us (7%)
  between operations  14.5 us (6%)
  blocking collectives  9.72 us (4%)
  other arithmetic  9.13 us (4%)
    ppermute x14, waiting for transfers between devices, other(): return lax.ppermute(value, axis, [(0, 1), (1, 0)])  51.9 us
    ppermute x8, waiting for transfers between devices, swap(): return lax.ppermute(value, ('core', 'zh'), [(0, 0), (1, 2), (2, 1), (3, 3)])  38 us
    ppermute x8, starting transfers between devices, swap(): return lax.ppermute(value, ('core', 'zh'), [(0, 0), (1, 2), (2, 1), (3, 3)])  27.3 us
    pallas_call x4, Pallas kernels, local(): pl.pallas_call(functools.partial(forward_kernel, k * steps, k == 0, last,...  20.5 us
    ppermute x14, starting transfers between devices, other(): return lax.ppermute(value, axis, [(0, 1), (1, 0)])  16 us
    unnamed x62, local copies, waits for them, and re-layouts  12.5 us
    pallas_call x4, Pallas kernels, local(): pl.pallas_call(functools.partial(backward_kernel, k * steps, k == CHUNKS...  10.8 us
    all_to_all x1, blocking collectives, local(): lax.all_to_all(outgoing, ('xy', 'zh'), split_axis=0, concat_axis=0, tiled...  9.72 us
  transfers between devices with their start and end apart: 24, of which 13 were waited for; matrix products, arithmetic and copies ran while one was open for 3% of the time, Pallas kernels for 14%

profile of v1, /device:TPU:1, one launch (start us, length us, event | category | flops | bytes accessed | tf_op | source)
XLA Modules:
  0.0 223.5 jit_solution(9049331922407998061)
XLA Ops:
  7.9 2.4 %select_maximum_fusion = f32[2120,128]{1,0:T(8,128)} fusion(f32[3,32]{1,0:T(4,128)S(1)} %convert_bitcast_fusion, f32[64,128]{1,0:T(8,128)} %bitcast.42, f32[2048,128]{1,0:T(8,128)} %bitcast.39), kind=kLoop, calls=%fused_computation.1 | loop fusion | flops 1085440 | bytes 2167168 | tf_op jit(solution)/shard_map/concatenate | solution.py:195
  10.4 5.6 %collective-permute-start = (f32[2120,128]{1,0:T(8,128)}, f32[2120,128]{1,0:T(8,128)S(1)}, u32[]{:S(2)}, u32[]{:S(2)}) collective-permute-start(f32[2120,128]{1,0:T(8,128)} %select_maximum_fusion), channel_id=1, source_target_pairs={{0,0},{2,4},{4,2},{6,6},{1,1},{3,5},{5,3},{7,7},{8,8},{10,12},{12,... | collective-permute-start | bytes 3256328 | tf_op jit(solution)/shard_map/ppermute | solution.py:182
  19.1 0.8 pad_maximum_fusion.5
  20.0 1.9 collective-permute-start.10
  21.9 16.8 %collective-permute-done.17 = f32[4,32,128]{2,1,0:T(8,128)S(1)} collective-permute-done((f32[4,32,128]{2,1,0:T(8,128)S(1)}, f32[4,32,128]{2,1,0:T(8,128)S(1)}, u32[]{:S(2)}, u32[]{:S(2)}) %collective-permute-start.17) | collective-permute-done | bytes 65568 | tf_op jit(solution)/shard_map/ppermute | solution.py:185
  38.7 11.0 %collective-permute-start.18 = (f32[2,4,32,128]{3,2,1,0:T(8,128)S(1)}, f32[2,4,32,128]{3,2,1,0:T(8,128)S(1)}, u32[]{:S(2)}, u32[]{:S(2)}) collective-permute-start(f32[2,4,32,128]{3,2,1,0:T(8,128)S(1)} %pad_maximum_fusion.7), channel_id=1, source_target_pairs={{0,1},{1,0},{2,3},{3,2},{4,5},{5,4},{6,7},{7,6},{8,9},{9,8},{10,11... | collective-permute-start | bytes 393224 | tf_op jit(solution)/shard_map/ppermute | solution.py:185
  49.6 0.9 pad_maximum_fusion.4
  50.5 1.9 collective-permute-start.6
  53.2 4.5 %collective-permute-start.2 = (f32[8,4,32,128]{3,2,1,0:T(8,128)}, f32[8,4,32,128]{3,2,1,0:T(8,128)S(1)}, u32[]{:S(2)}, u32[]{:S(2)}) collective-permute-start(f32[8,4,32,128]{3,2,1,0:T(8,128)} %pad_maximum_fusion.3), channel_id=1, source_target_pairs={{0,0},{2,4},{4,2},{6,6},{1,1},{3,5},{5,3},{7,7},{8,8},{10,12},{12,... | collective-permute-start | bytes 1572872 | tf_op jit(solution)/shard_map/ppermute | solution.py:182
  58.6 2.3 %collective-permute-start.1 = (f32[8,4,32,128]{3,2,1,0:T(8,128)S(1)}, f32[8,4,32,128]{3,2,1,0:T(8,128)S(1)}, u32[]{:S(2)}, u32[]{:S(2)}) collective-permute-start(f32[8,4,32,128]{3,2,1,0:T(8,128)S(1)} %pad_maximum_fusion.2), channel_id=1, source_target_pairs={{0,0},{2,4},{4,2},{6,6},{1,1},{3,5},{5,3},{7,7},{8,8},{10,12},{12,... | collective-permute-start | bytes 1572872 | tf_op jit(solution)/shard_map/ppermute | solution.py:182
  60.9 2.7 %collective-permute-start.11 = (f32[8,4,32,128]{3,2,1,0:T(8,128)S(1)}, f32[8,4,32,128]{3,2,1,0:T(8,128)}, u32[]{:S(2)}, u32[]{:S(2)}) collective-permute-start(f32[8,4,32,128]{3,2,1,0:T(8,128)S(1)} %collective-permute-done.10.refs_1_), channel_id=1, source_target_pairs={{0,1},{1,0},{2,3},{3,2},{4,5},{5,4},{6,7},{7,6},{8,9},{9,8},{10,11... | collective-permute-start | bytes 1572872 | tf_op jit(solution)/shard_map/ppermute | solution.py:185
  63.6 10.1 %collective-permute-done.6.refs_1_ = f32[8,4,32,128]{3,2,1,0:T(8,128)S(1)} collective-permute-done((f32[8,4,32,128]{3,2,1,0:T(8,128)}, f32[8,4,32,128]{3,2,1,0:T(8,128)S(1)}, u32[]{:S(2)}, u32[]{:S(2)}) %collective-permute-start.6) | collective-permute-done | bytes 524320 | tf_op jit(solution)/shard_map/ppermute | solution.py:182
  73.7 1.1 collective-permute-start.7
  74.8 9.6 %collective-permute-done.2.refs_1_ = f32[8,4,32,128]{3,2,1,0:T(8,128)S(1)} collective-permute-done((f32[8,4,32,128]{3,2,1,0:T(8,128)}, f32[8,4,32,128]{3,2,1,0:T(8,128)S(1)}, u32[]{:S(2)}, u32[]{:S(2)}) %collective-permute-start.2) | collective-permute-done | bytes 524320 | tf_op jit(solution)/shard_map/ppermute | solution.py:182
  84.4 5.6 %collective-permute-done.1.refs_1_ = f32[8,4,32,128]{3,2,1,0:T(8,128)S(1)} collective-permute-done((f32[8,4,32,128]{3,2,1,0:T(8,128)S(1)}, f32[8,4,32,128]{3,2,1,0:T(8,128)S(1)}, u32[]{:S(2)}, u32[]{:S(2)}) %collective-permute-start.1) | collective-permute-done | bytes 524320 | tf_op jit(solution)/shard_map/ppermute | solution.py:182
  90.0 1.9 collective-permute-done.11.refs_2_
  91.9 11.3 %collective-permute-done.7.refs_2_ = f32[8,4,32,128]{3,2,1,0:T(8,128)S(1)} collective-permute-done((f32[8,4,32,128]{3,2,1,0:T(8,128)S(1)}, f32[8,4,32,128]{3,2,1,0:T(8,128)S(1)}, u32[]{:S(2)}, u32[]{:S(2)}) %collective-permute-start.7) | collective-permute-done | bytes 524320 | tf_op jit(solution)/shard_map/ppermute | solution.py:185
  104.8 9.7 %collective-permute-done.3.refs_2_ = f32[8,4,32,128]{3,2,1,0:T(8,128)} collective-permute-done((f32[8,4,32,128]{3,2,1,0:T(8,128)S(1)}, f32[8,4,32,128]{3,2,1,0:T(8,128)}, u32[]{:S(2)}, u32[]{:S(2)}) %collective-permute-start.3) | collective-permute-done | bytes 524320 | tf_op jit(solution)/shard_map/ppermute | solution.py:185
  114.5 10.0 %collective-permute-done.14.refs_2_ = f32[8,4,32,128]{3,2,1,0:T(8,128)} collective-permute-done((f32[8,4,32,128]{3,2,1,0:T(8,128)S(1)}, f32[8,4,32,128]{3,2,1,0:T(8,128)}, u32[]{:S(2)}, u32[]{:S(2)}) %collective-permute-start.14) | collective-permute-done | bytes 524320 | tf_op jit(solution)/shard_map/ppermute | solution.py:185
  125.9 5.1 %leaf_forward.4 = (f32[40,64,128]{2,1,0:T(8,128)S(1)}, bf16[8,384,128]{2,1,0:T(8,128)(2,1)S(1)}, bf16[8,384,128]{2,1,0:T(8,128)(2,1)S(1)}, f32[8,64,128]{2,1,0:T(8,128)S(1)}) custom-call(s32[104]{0:T(128)S(1)} %concatenate.34.refs_0_.meta, f32[8,4,32,128]{3,2,1,0:T(8,128)S(1)} %collective-permute-done.10.refs_1_, ...), custom_call_target="tpu_custom_call" | custom-call | flops 4000000000 | bytes 8388608 | tf_op jit(solution)/shard_map/leaf_forward/pallas_call | solution.py:242
  131.0 0.9 copy-done.16
  131.9 0.9 copy-done.18
  133.5 4.8 %leaf_forward.5 = (f32[40,64,128]{2,1,0:T(8,128)S(1)}, bf16[8,384,128]{2,1,0:T(8,128)(2,1)S(1)}, bf16[8,384,128]{2,1,0:T(8,128)(2,1)S(1)}, f32[8,64,128]{2,1,0:T(8,128)S(1)}) custom-call(s32[104]{0:T(128)S(1)} %concatenate.34.refs_0_.meta, f32[8,4,32,128]{3,2,1,0:T(8,128)S(1)} %collective-permute-done.6.refs_1_, f32[8,4,32,128]{3,2,1,0:T(8,128)S(1)} %copy-done.3, ...), custom_call_target="tpu_custom_call" | custom-call | flops 4000000000 | bytes 8388608 | tf_op jit(solution)/shard_map/leaf_forward/pallas_call | solution.py:242
  138.3 0.9 copy-done.4
  139.2 0.9 copy-done.6
  140.1 4.9 %leaf_forward.6 = (f32[40,64,128]{2,1,0:T(8,128)S(1)}, bf16[8,384,128]{2,1,0:T(8,128)(2,1)S(1)}, bf16[8,384,128]{2,1,0:T(8,128)(2,1)S(1)}, f32[8,64,128]{2,1,0:T(8,128)S(1)}) custom-call(s32[104]{0:T(128)S(1)} %concatenate.34.refs_0_.meta, f32[8,4,32,128]{3,2,1,0:T(8,128)S(1)} %collective-permute-done.2.refs_1_, ...), custom_call_target="tpu_custom_call" | custom-call | flops 4000000000 | bytes 8388608 | tf_op jit(solution)/shard_map/leaf_forward/pallas_call | solution.py:242
  145.0 0.9 copy-done.8
  145.9 0.9 copy-done.10
  147.6 2.0 collective-permute-done.16.refs_4_
  149.7 5.8 %leaf_forward.7 = (f32[40,64,128]{2,1,0:T(8,128)}, bf16[8,384,128]{2,1,0:T(8,128)(2,1)S(1)}, bf16[8,384,128]{2,1,0:T(8,128)(2,1)S(1)}, f32[8,64,128]{2,1,0:T(8,128)S(1)}, f32[8,5,8,128]{3,2,1,0:T(8,128)}) custom-call(s32[104]{0:T(128)S(1)} %concatenate.34.refs_0_.meta, f32[8,4,32,128]{3,2,1,0:T(8,128)S(1)} %collective-permute-done.1.refs_1_, ...), custom_call_target="tpu_custom_call" | custom-call | flops 4000000000 | bytes 8388608 | tf_op jit(solution)/shard_map/leaf_forward/pallas_call | solution.py:242
  155.4 0.9 copy-done.12
  156.3 0.9 copy-done.14
  157.9 3.6 %all-to-all-start = ((f32[8,5,8,128]{3,2,1,0:T(8,128)}), f32[8,5,8,128]{3,2,1,0:T(8,128)S(1)}, u32[]{:S(2)}, u32[]{:S(2)}) async-start(f32[8,5,8,128]{3,2,1,0:T(8,128)} %get-tuple-element.66), calls=%async_computation | async-start | bytes 327680 | tf_op jit(solution)/shard_map/all_to_all | solution.py:255
  161.6 1.6 copy-done.1
  163.1 2.8 %top_prepare.1 = (bf16[8,384,128]{2,1,0:T(8,128)(2,1)S(1)}, bf16[8,384,128]{2,1,0:T(8,128)(2,1)S(1)}, bf16[8,128,128]{2,1,0:T(8,128)(2,1)S(1)}, bf16[8,128,128]{2,1,0:T(8,128)(2,1)S(1)}) custom-call(s32[4]{0:T(128)S(1)} %pad_add_fusion.meta, f32[8,4,4,32,128]{4,3,2,1,0:T(8,128)S(1)} %bitcast.38), custom_call_target="tpu_custom_call" | custom-call | tf_op jit(solution)/shard_map/top_prepare/pallas_call | solution.py:216
  165.9 1.8 all-to-all-done.incoming
  167.7 2.7 %top_solve.1 = f32[8,5,8,128]{3,2,1,0:T(8,128)S(1)} custom-call(f32[8,5,8,128]{3,2,1,0:T(8,128)S(1)} %all-to-all-done.incoming, bf16[8,384,128]{2,1,0:T(8,128)(2,1)S(1)} %get-tuple-element.67.high, bf16[8,384,128]{2,1,0:T(8,128)(2,1)S(1)} %get-tuple-element.68.low, bf16[8,128,128]{2,1,0:T(8,128)(2,1)S(1)} %get-tuple-element.69.inverse_high, ...), custom_call_target="tpu_custom_call" | custom-call | tf_op jit(solution)/shard_map/top_solve/pallas_call | solution.py:256
  170.4 9.7 %all_to_all.10.state = f32[8,5,8,128]{3,2,1,0:T(8,128)S(1)} all-to-all(f32[8,5,8,128]{3,2,1,0:T(8,128)S(1)} %top_solve.1), channel_id=1, replica_groups=mesh['xy'=4,'core'=2,'zh'=2,'zl'=2] {'xy','zh'}, dimensions={0} | all-to-all | bytes 327680 | tf_op jit(solution)/shard_map/all_to_all | solution.py:264
  180.2 2.4 %leaf_backward.4 = (f32[8,64,128]{2,1,0:T(8,128)S(1)}, f32[40,64,128]{2,1,0:T(8,128)S(1)}) custom-call(s32[104]{0:T(128)S(1)} %concatenate.34.refs_0_.meta, bf16[8,384,128]{2,1,0:T(8,128)(2,1)S(1)} %copy-done.13, bf16[8,384,128]{2,1,0:T(8,128)(2,1)S(1)} %copy-done.15, f32[8,64,128]{2,1,0:T(8,128)S(1)} %copy-done.25, f32[8,5,8,128]{3,2,1,0:T(8,128)S(1)} %all_to_all.10.state), custom_call_target="tpu_custom_call" | custom-call | flops 4000000000 | bytes 8388608 | tf_op jit(solution)/shard_map/leaf_backward/pallas_call | solution.py:269
  182.6 4.4 %collective-permute-start.19 = (f32[8,64,128]{2,1,0:T(8,128)S(1)}, f32[8,64,128]{2,1,0:T(8,128)S(1)}, u32[]{:S(2)}, u32[]{:S(2)}) collective-permute-start(f32[8,64,128]{2,1,0:T(8,128)S(1)} %get-tuple-element.71), channel_id=1, source_target_pairs={{0,0},{2,4},{4,2},{6,6},{1,1},{3,5},{5,3},{7,7},{8,8},{10,12},{12,... | collective-permute-start | bytes 786440 | tf_op jit(solution)/shard_map/ppermute | solution.py:182
  187.1 2.4 %leaf_backward.5 = (f32[8,64,128]{2,1,0:T(8,128)S(1)}, f32[40,64,128]{2,1,0:T(8,128)S(1)}) custom-call(s32[104]{0:T(128)S(1)} %concatenate.34.refs_0_.meta, bf16[8,384,128]{2,1,0:T(8,128)(2,1)S(1)} %copy-done.9, bf16[8,384,128]{2,1,0:T(8,128)(2,1)S(1)} %copy-done.11, f32[8,64,128]{2,1,0:T(8,128)S(1)} %copy-done.23, f32[40,64,128]{2,1,0:T(8,128)S(1)} %get-tuple-element.81.state), custom_call_target="tpu_custom_call" | custom-call | flops 4000000000 | bytes 8388608 | tf_op jit(solution)/shard_map/leaf_backward/pallas_call | solution.py:269
  189.6 2.4 %leaf_backward.6 = (f32[8,64,128]{2,1,0:T(8,128)S(1)}, f32[40,64,128]{2,1,0:T(8,128)S(1)}) custom-call(s32[104]{0:T(128)S(1)} %concatenate.34.refs_0_.meta, bf16[8,384,128]{2,1,0:T(8,128)(2,1)S(1)} %copy-done.5, bf16[8,384,128]{2,1,0:T(8,128)(2,1)S(1)} %copy-done.7, f32[8,64,128]{2,1,0:T(8,128)S(1)} %copy-done.21, f32[40,64,128]{2,1,0:T(8,128)S(1)} %get-tuple-element.82.state), custom_call_target="tpu_custom_call" | custom-call | flops 4000000000 | bytes 8388608 | tf_op jit(solution)/shard_map/leaf_backward/pallas_call | solution.py:269
  192.1 2.1 collective-permute-start.21
  194.3 3.5 %leaf_backward.7 = (f32[8,64,128]{2,1,0:T(8,128)S(1)}, f32[40,64,128]{2,1,0:T(8,128)}) custom-call(s32[104]{0:T(128)S(1)} %concatenate.34.refs_0_.meta, bf16[8,384,128]{2,1,0:T(8,128)(2,1)S(1)} %copy-done.17, bf16[8,384,128]{2,1,0:T(8,128)(2,1)S(1)} %copy-done.19, f32[8,64,128]{2,1,0:T(8,128)S(1)} %copy-done.27, f32[40,64,128]{2,1,0:T(8,128)S(1)} %get-tuple-element.83.state), custom_call_target="tpu_custom_call" | custom-call | flops 4000000000 | bytes 8388608 | tf_op jit(solution)/shard_map/leaf_backward/pallas_call | solution.py:269
  197.8 4.4 %collective-permute-start.20 = (f32[8,64,128]{2,1,0:T(8,128)S(1)}, f32[8,64,128]{2,1,0:T(8,128)S(1)}, u32[]{:S(2)}, u32[]{:S(2)}) collective-permute-start(f32[8,64,128]{2,1,0:T(8,128)S(1)} %get-tuple-element.85), channel_id=1, source_target_pairs={{0,0},{2,4},{4,2},{6,6},{1,1},{3,5},{5,3},{7,7},{8,8},{10,12},{12,... | collective-permute-start | bytes 786440 | tf_op jit(solution)/shard_map/ppermute | solution.py:182
  202.3 10.5 %collective-permute-done.21 = f32[17,64,128]{2,1,0:T(8,128)S(1)} collective-permute-done((f32[17,64,128]{2,1,0:T(8,128)S(1)}, f32[17,64,128]{2,1,0:T(8,128)S(1)}, u32[]{:S(2)}, u32[]{:S(2)}) %collective-permute-start.21) | collective-permute-done | bytes 557088 | tf_op jit(solution)/shard_map/ppermute | solution.py:182
  213.4 2.1 collective-permute-done.20
  215.6 1.1 pad_maximum_fusion
  (101 shorter events, 11.5 us)
Async XLA Ops:
  7.2 10.2 %copy-start = (f32[8,1,32,128]{3,2,1,0:T(8,128)S(1)}, f32[8,1,32,128]{3,2,1,0:T(8,128)}, u32[]{:S(2)}) copy-start(f32[8,1,32,128]{3,2,1,0:T(8,128)} %param.16) | copy-start | bytes 393220
  7.2 154.4 %all-gather.3.cloned.1.call-start = ((), (), s32[]{:S(2)}) async-start(), calls=%async_computation.2 | async-start | bytes 2359296 | tf_op jit(solution)/shard_map/all_gather | solution.py:205
  7.9 10.1 %copy-start.30 = (f32[1,32,128]{2,1,0:T(8,128)S(1)}, f32[1,32,128]{2,1,0:T(8,128)}, u32[]{:S(2)}) copy-start(f32[1,32,128]{2,1,0:T(8,128)} %param.17) | copy-start | bytes 49156
  7.9 10.2 %copy-start.28 = (f32[32,3,32,128]{3,2,1,0:T(8,128)S(1)}, f32[32,3,32,128]{3,2,1,0:T(8,128)}, u32[]{:S(2)}) copy-start(f32[32,3,32,128]{3,2,1,0:T(8,128)} %param.13) | copy-start | bytes 4718596
  10.4 114.1 %collective-permute-start = (f32[2120,128]{1,0:T(8,128)}, f32[2120,128]{1,0:T(8,128)S(1)}, u32[]{:S(2)}, u32[]{:S(2)}) collective-permute-start(f32[2120,128]{1,0:T(8,128)} %select_maximum_fusion), channel_id=1, source_target_pairs={{0,0},{2,4},{4,2},{6,6},{1,1},{3,5},{5,3},{7,7},{8,8},{10,12},{12,... | collective-permute-start | bytes 3256328 | tf_op jit(solution)/shard_map/ppermute | solution.py:182
  18.1 1.0 copy-start.29
  18.1 20.6 %collective-permute-start.17 = (f32[4,32,128]{2,1,0:T(8,128)S(1)}, f32[4,32,128]{2,1,0:T(8,128)S(1)}, u32[]{:S(2)}, u32[]{:S(2)}) collective-permute-start(f32[4,32,128]{2,1,0:T(8,128)S(1)} %get-tuple-element.97), channel_id=1, source_target_pairs={{0,2},{2,0},{1,3},{3,1},{4,6},{6,4},{5,7},{7,5},{8,10},{10,8},{9,1... | collective-permute-start | bytes 196616 | tf_op jit(solution)/shard_map/ppermute | solution.py:185
  20.0 40.9 %collective-permute-start.10 = (f32[8,4,32,128]{3,2,1,0:T(8,128)}, f32[8,4,32,128]{3,2,1,0:T(8,128)S(1)}, u32[]{:S(2)}, u32[]{:S(2)}) collective-permute-start(f32[8,4,32,128]{3,2,1,0:T(8,128)} %pad_maximum_fusion.5), channel_id=1, source_target_pairs={{0,0},{2,4},{4,2},{6,6},{1,1},{3,5},{5,3},{7,7},{8,8},{10,12},{12,... | collective-permute-start | bytes 1572872 | tf_op jit(solution)/shard_map/ppermute | solution.py:182
  38.7 19.2 %collective-permute-start.18 = (f32[2,4,32,128]{3,2,1,0:T(8,128)S(1)}, f32[2,4,32,128]{3,2,1,0:T(8,128)S(1)}, u32[]{:S(2)}, u32[]{:S(2)}) collective-permute-start(f32[2,4,32,128]{3,2,1,0:T(8,128)S(1)} %pad_maximum_fusion.7), channel_id=1, source_target_pairs={{0,1},{1,0},{2,3},{3,2},{4,5},{5,4},{6,7},{7,6},{8,9},{9,8},{10,11... | collective-permute-start | bytes 393224 | tf_op jit(solution)/shard_map/ppermute | solution.py:185
  50.5 23.2 %collective-permute-start.6 = (f32[8,4,32,128]{3,2,1,0:T(8,128)}, f32[8,4,32,128]{3,2,1,0:T(8,128)S(1)}, u32[]{:S(2)}, u32[]{:S(2)}) collective-permute-start(f32[8,4,32,128]{3,2,1,0:T(8,128)} %pad_maximum_fusion.4), channel_id=1, source_target_pairs={{0,0},{2,4},{4,2},{6,6},{1,1},{3,5},{5,3},{7,7},{8,8},{10,12},{12,... | collective-permute-start | bytes 1572872 | tf_op jit(solution)/shard_map/ppermute | solution.py:182
  53.2 31.1 %collective-permute-start.2 = (f32[8,4,32,128]{3,2,1,0:T(8,128)}, f32[8,4,32,128]{3,2,1,0:T(8,128)S(1)}, u32[]{:S(2)}, u32[]{:S(2)}) collective-permute-start(f32[8,4,32,128]{3,2,1,0:T(8,128)} %pad_maximum_fusion.3), channel_id=1, source_target_pairs={{0,0},{2,4},{4,2},{6,6},{1,1},{3,5},{5,3},{7,7},{8,8},{10,12},{12,... | collective-permute-start | bytes 1572872 | tf_op jit(solution)/shard_map/ppermute | solution.py:182
  58.6 31.4 %collective-permute-start.1 = (f32[8,4,32,128]{3,2,1,0:T(8,128)S(1)}, f32[8,4,32,128]{3,2,1,0:T(8,128)S(1)}, u32[]{:S(2)}, u32[]{:S(2)}) collective-permute-start(f32[8,4,32,128]{3,2,1,0:T(8,128)S(1)} %pad_maximum_fusion.2), channel_id=1, source_target_pairs={{0,0},{2,4},{4,2},{6,6},{1,1},{3,5},{5,3},{7,7},{8,8},{10,12},{12,... | collective-permute-start | bytes 1572872 | tf_op jit(solution)/shard_map/ppermute | solution.py:182
  60.9 31.0 %collective-permute-start.11 = (f32[8,4,32,128]{3,2,1,0:T(8,128)S(1)}, f32[8,4,32,128]{3,2,1,0:T(8,128)}, u32[]{:S(2)}, u32[]{:S(2)}) collective-permute-start(f32[8,4,32,128]{3,2,1,0:T(8,128)S(1)} %collective-permute-done.10.refs_1_), channel_id=1, source_target_pairs={{0,1},{1,0},{2,3},{3,2},{4,5},{5,4},{6,7},{7,6},{8,9},{9,8},{10,11... | collective-permute-start | bytes 1572872 | tf_op jit(solution)/shard_map/ppermute | solution.py:185
  73.7 29.6 %collective-permute-start.7 = (f32[8,4,32,128]{3,2,1,0:T(8,128)S(1)}, f32[8,4,32,128]{3,2,1,0:T(8,128)S(1)}, u32[]{:S(2)}, u32[]{:S(2)}) collective-permute-start(f32[8,4,32,128]{3,2,1,0:T(8,128)S(1)} %collective-permute-done.6.refs_1_), channel_id=1, source_target_pairs={{0,1},{1,0},{2,3},{3,2},{4,5},{5,4},{6,7},{7,6},{8,9},{9,8},{10,11... | collective-permute-start | bytes 1572872 | tf_op jit(solution)/shard_map/ppermute | solution.py:185
  84.4 30.1 %collective-permute-start.3 = (f32[8,4,32,128]{3,2,1,0:T(8,128)S(1)}, f32[8,4,32,128]{3,2,1,0:T(8,128)}, u32[]{:S(2)}, u32[]{:S(2)}) collective-permute-start(f32[8,4,32,128]{3,2,1,0:T(8,128)S(1)} %collective-permute-done.2.refs_1_), channel_id=1, source_target_pairs={{0,1},{1,0},{2,3},{3,2},{4,5},{5,4},{6,7},{7,6},{8,9},{9,8},{10,11... | collective-permute-start | bytes 1572872 | tf_op jit(solution)/shard_map/ppermute | solution.py:185
  90.0 34.5 %collective-permute-start.14 = (f32[8,4,32,128]{3,2,1,0:T(8,128)S(1)}, f32[8,4,32,128]{3,2,1,0:T(8,128)}, u32[]{:S(2)}, u32[]{:S(2)}) collective-permute-start(f32[8,4,32,128]{3,2,1,0:T(8,128)S(1)} %collective-permute-done.1.refs_1_), channel_id=1, source_target_pairs={{0,1},{1,0},{2,3},{3,2},{4,5},{5,4},{6,7},{7,6},{8,9},{9,8},{10,11... | collective-permute-start | bytes 1572872 | tf_op jit(solution)/shard_map/ppermute | solution.py:185
  91.9 33.4 %collective-permute-start.12 = (f32[8,4,32,128]{3,2,1,0:T(8,128)S(1)}, f32[8,4,32,128]{3,2,1,0:T(8,128)}, u32[]{:S(2)}, u32[]{:S(2)}) collective-permute-start(f32[8,4,32,128]{3,2,1,0:T(8,128)S(1)} %collective-permute-done.10.refs_1_), channel_id=1, source_target_pairs={{0,4},{4,0},{1,5},{5,1},{2,6},{6,2},{3,7},{7,3},{8,12},{12,8},{9,1... | collective-permute-start | bytes 1572872 | tf_op jit(solution)/shard_map/ppermute | solution.py:185
  104.1 21.3 %collective-permute-start.13 = (f32[8,4,32,128]{3,2,1,0:T(8,128)}, f32[8,4,32,128]{3,2,1,0:T(8,128)}, u32[]{:S(2)}, u32[]{:S(2)}) collective-permute-start(f32[8,4,32,128]{3,2,1,0:T(8,128)} %collective-permute-done.11.refs_2_), channel_id=1, source_target_pairs={{0,4},{4,0},{1,5},{5,1},{2,6},{6,2},{3,7},{7,3},{8,12},{12,8},{9,1... | collective-permute-start | bytes 1572872 | tf_op jit(solution)/shard_map/ppermute | solution.py:185
  114.5 19.0 %collective-permute-start.8 = (f32[8,4,32,128]{3,2,1,0:T(8,128)S(1)}, f32[8,4,32,128]{3,2,1,0:T(8,128)}, u32[]{:S(2)}, u32[]{:S(2)}) collective-permute-start(f32[8,4,32,128]{3,2,1,0:T(8,128)S(1)} %collective-permute-done.6.refs_1_), channel_id=1, source_target_pairs={{0,4},{4,0},{1,5},{5,1},{2,6},{6,2},{3,7},{7,3},{8,12},{12,8},{9,1... | collective-permute-start | bytes 1572872 | tf_op jit(solution)/shard_map/ppermute | solution.py:185
  124.5 15.6 %collective-permute-start.4 = (f32[8,4,32,128]{3,2,1,0:T(8,128)S(1)}, f32[8,4,32,128]{3,2,1,0:T(8,128)}, u32[]{:S(2)}, u32[]{:S(2)}) collective-permute-start(f32[8,4,32,128]{3,2,1,0:T(8,128)S(1)} %collective-permute-done.2.refs_1_), channel_id=1, source_target_pairs={{0,4},{4,0},{1,5},{5,1},{2,6},{6,2},{3,7},{7,3},{8,12},{12,8},{9,1... | collective-permute-start | bytes 1572872 | tf_op jit(solution)/shard_map/ppermute | solution.py:185
  124.5 9.0 %collective-permute-start.9 = (f32[8,4,32,128]{3,2,1,0:T(8,128)}, f32[8,4,32,128]{3,2,1,0:T(8,128)}, u32[]{:S(2)}, u32[]{:S(2)}) collective-permute-start(f32[8,4,32,128]{3,2,1,0:T(8,128)} %copy-done.2), channel_id=1, source_target_pairs={{0,4},{4,0},{1,5},{5,1},{2,6},{6,2},{3,7},{7,3},{8,12},{12,8},{9,1... | collective-permute-start | bytes 1572872 | tf_op jit(solution)/shard_map/ppermute | solution.py:185
  125.3 8.2 %copy-start.3 = (f32[8,4,32,128]{3,2,1,0:T(8,128)S(1)}, f32[8,4,32,128]{3,2,1,0:T(8,128)}, u32[]{:S(2)}) copy-start(f32[8,4,32,128]{3,2,1,0:T(8,128)} %copy-done.2) | copy-start | bytes 1572868
  125.3 22.3 %collective-permute-start.15 = (f32[8,4,32,128]{3,2,1,0:T(8,128)S(1)}, f32[8,4,32,128]{3,2,1,0:T(8,128)S(1)}, u32[]{:S(2)}, u32[]{:S(2)}) collective-permute-start(f32[8,4,32,128]{3,2,1,0:T(8,128)S(1)} %collective-permute-done.1.refs_1_), channel_id=1, source_target_pairs={{0,4},{4,0},{1,5},{5,1},{2,6},{6,2},{3,7},{7,3},{8,12},{12,8},{9,1... | collective-permute-start | bytes 1572872 | tf_op jit(solution)/shard_map/ppermute | solution.py:185
  125.4 14.7 %collective-permute-start.5 = (f32[8,4,32,128]{3,2,1,0:T(8,128)}, f32[8,4,32,128]{3,2,1,0:T(8,128)S(1)}, u32[]{:S(2)}, u32[]{:S(2)}) collective-permute-start(f32[8,4,32,128]{3,2,1,0:T(8,128)} %collective-permute-done.3.refs_2_), channel_id=1, source_target_pairs={{0,4},{4,0},{1,5},{5,1},{2,6},{6,2},{3,7},{7,3},{8,12},{12,8},{9,1... | collective-permute-start | bytes 1572872 | tf_op jit(solution)/shard_map/ppermute | solution.py:185
  131.0 0.9 copy-start.16
  131.8 0.9 copy-start.18
  138.3 0.9 copy-start.4
  140.1 4.9 %copy-start.20 = (f32[8,64,128]{2,1,0:T(8,128)}, f32[8,64,128]{2,1,0:T(8,128)S(1)}, u32[]{:S(2)}) copy-start(f32[8,64,128]{2,1,0:T(8,128)S(1)} %get-tuple-element.77.scaled) | copy-start | bytes 786436
  145.0 0.9 copy-start.8
  145.9 0.9 copy-start.10
  147.5 2.1 collective-permute-start.16
  157.9 9.8 %all-to-all-start = ((f32[8,5,8,128]{3,2,1,0:T(8,128)}), f32[8,5,8,128]{3,2,1,0:T(8,128)S(1)}, u32[]{:S(2)}, u32[]{:S(2)}) async-start(f32[8,5,8,128]{3,2,1,0:T(8,128)} %get-tuple-element.66), calls=%async_computation | async-start | bytes 327680 | tf_op jit(solution)/shard_map/all_to_all | solution.py:255
  161.6 1.6 copy-start.1
  167.7 12.4 %copy-start.13 = (bf16[8,384,128]{2,1,0:T(8,128)(2,1)S(1)}, bf16[8,384,128]{2,1,0:T(8,128)(2,1)}, u32[]{:S(2)}) copy-start(bf16[8,384,128]{2,1,0:T(8,128)(2,1)} %copy-done.12) | copy-start | bytes 2359300
  167.7 12.4 %copy-start.15 = (bf16[8,384,128]{2,1,0:T(8,128)(2,1)S(1)}, bf16[8,384,128]{2,1,0:T(8,128)(2,1)}, u32[]{:S(2)}) copy-start(bf16[8,384,128]{2,1,0:T(8,128)(2,1)} %copy-done.14) | copy-start | bytes 2359300
  167.7 12.4 %copy-start.25 = (f32[8,64,128]{2,1,0:T(8,128)S(1)}, f32[8,64,128]{2,1,0:T(8,128)}, u32[]{:S(2)}) copy-start(f32[8,64,128]{2,1,0:T(8,128)} %copy-done.24) | copy-start | bytes 786436
  180.1 6.9 %copy-start.9 = (bf16[8,384,128]{2,1,0:T(8,128)(2,1)S(1)}, bf16[8,384,128]{2,1,0:T(8,128)(2,1)}, u32[]{:S(2)}) copy-start(bf16[8,384,128]{2,1,0:T(8,128)(2,1)} %copy-done.8) | copy-start | bytes 2359300
  180.1 6.9 %copy-start.11 = (bf16[8,384,128]{2,1,0:T(8,128)(2,1)S(1)}, bf16[8,384,128]{2,1,0:T(8,128)(2,1)}, u32[]{:S(2)}) copy-start(bf16[8,384,128]{2,1,0:T(8,128)(2,1)} %copy-done.10) | copy-start | bytes 2359300
  180.1 6.9 %copy-start.23 = (f32[8,64,128]{2,1,0:T(8,128)S(1)}, f32[8,64,128]{2,1,0:T(8,128)}, u32[]{:S(2)}) copy-start(f32[8,64,128]{2,1,0:T(8,128)} %copy-done.22) | copy-start | bytes 786436
  182.6 15.2 %collective-permute-start.19 = (f32[8,64,128]{2,1,0:T(8,128)S(1)}, f32[8,64,128]{2,1,0:T(8,128)S(1)}, u32[]{:S(2)}, u32[]{:S(2)}) collective-permute-start(f32[8,64,128]{2,1,0:T(8,128)S(1)} %get-tuple-element.71), channel_id=1, source_target_pairs={{0,0},{2,4},{4,2},{6,6},{1,1},{3,5},{5,3},{7,7},{8,8},{10,12},{12,... | collective-permute-start | bytes 786440 | tf_op jit(solution)/shard_map/ppermute | solution.py:182
  187.1 2.5 %copy-start.5 = (bf16[8,384,128]{2,1,0:T(8,128)(2,1)S(1)}, bf16[8,384,128]{2,1,0:T(8,128)(2,1)}, u32[]{:S(2)}) copy-start(bf16[8,384,128]{2,1,0:T(8,128)(2,1)} %copy-done.4) | copy-start | bytes 2359300
  187.1 2.5 %copy-start.7 = (bf16[8,384,128]{2,1,0:T(8,128)(2,1)S(1)}, bf16[8,384,128]{2,1,0:T(8,128)(2,1)}, u32[]{:S(2)}) copy-start(bf16[8,384,128]{2,1,0:T(8,128)(2,1)} %copy-done.6) | copy-start | bytes 2359300
  187.1 2.5 %copy-start.21 = (f32[8,64,128]{2,1,0:T(8,128)S(1)}, f32[8,64,128]{2,1,0:T(8,128)}, u32[]{:S(2)}) copy-start(f32[8,64,128]{2,1,0:T(8,128)} %copy-done.20) | copy-start | bytes 786436
  189.6 4.7 %copy-start.19 = (bf16[8,384,128]{2,1,0:T(8,128)(2,1)S(1)}, bf16[8,384,128]{2,1,0:T(8,128)(2,1)}, u32[]{:S(2)}) copy-start(bf16[8,384,128]{2,1,0:T(8,128)(2,1)} %copy-done.18) | copy-start | bytes 2359300
  192.0 2.3 %copy-start.17 = (bf16[8,384,128]{2,1,0:T(8,128)(2,1)S(1)}, bf16[8,384,128]{2,1,0:T(8,128)(2,1)}, u32[]{:S(2)}) copy-start(bf16[8,384,128]{2,1,0:T(8,128)(2,1)} %copy-done.16) | copy-start | bytes 2359300
  192.0 2.2 %copy-start.27 = (f32[8,64,128]{2,1,0:T(8,128)S(1)}, f32[8,64,128]{2,1,0:T(8,128)}, u32[]{:S(2)}) copy-start(f32[8,64,128]{2,1,0:T(8,128)} %copy-done.26) | copy-start | bytes 786436
  192.1 20.7 %collective-permute-start.21 = (f32[17,64,128]{2,1,0:T(8,128)S(1)}, f32[17,64,128]{2,1,0:T(8,128)S(1)}, u32[]{:S(2)}, u32[]{:S(2)}) collective-permute-start(f32[17,64,128]{2,1,0:T(8,128)S(1)} %pad_maximum_fusion.1), channel_id=1, source_target_pairs={{0,0},{2,4},{4,2},{6,6},{1,1},{3,5},{5,3},{7,7},{8,8},{10,12},{12,... | collective-permute-start | bytes 1671176 | tf_op jit(solution)/shard_map/ppermute | solution.py:182
  197.8 17.8 %collective-permute-start.20 = (f32[8,64,128]{2,1,0:T(8,128)S(1)}, f32[8,64,128]{2,1,0:T(8,128)S(1)}, u32[]{:S(2)}, u32[]{:S(2)}) collective-permute-start(f32[8,64,128]{2,1,0:T(8,128)S(1)} %get-tuple-element.85), channel_id=1, source_target_pairs={{0,0},{2,4},{4,2},{6,6},{1,1},{3,5},{5,3},{7,7},{8,8},{10,12},{12,... | collective-permute-start | bytes 786440 | tf_op jit(solution)/shard_map/ppermute | solution.py:182
  (7 other events, 5.5 us)
Sparse Core Ops, SparseCore 0:
  58.7 27.9 all-gather.2

commit v2 on v1

--- a/solution.py
+++ b/solution.py
@@ -50,20 +50,26 @@
 
 
 def forward_kernel(base, first, last, width, *refs):
-    meta, pieces, sides = refs[0], refs[1:5], refs[5]
-    refs = refs[6:]
+    meta, kept, passed, sides = refs[0], refs[1:5], refs[5:9], refs[9]
+    refs = refs[10:]
     if not first:
         acc_in, refs = refs[0], refs[1:]
     acc, high, low, scaled, refs = refs[0], refs[1], refs[2], refs[3], refs[4:]
     if last:
         payload, refs = refs[0], refs[1:]
     full = refs[0]
-    steps, columns, rows = scaled.shape[0], scaled.shape[1], pieces[0].shape[2]
+    steps, columns, rows = scaled.shape[0], scaled.shape[1], kept[0].shape[2]
     leafs = steps * CHUNKS
     wide = full.shape[2]
-    for place, piece in enumerate(pieces):
-        offset = pl.multiple_of(meta[3 * leafs + place] * rows, rows)
-        full[:, :, pl.ds(offset, rows), :] = piece[...]
+
+    def assemble(pieces):
+        for place, piece in enumerate(pieces):
+            offset = pl.multiple_of(meta[3 * leafs + place] * rows, rows)
+            full[:, :, pl.ds(offset, rows), :] = piece[...]
+
+    keeps = meta[3 * leafs + 4 + width]
+    pl.when(keeps == 1)(lambda: assemble(kept))
+    pl.when(keeps == 0)(lambda: assemble(passed))
     if first:
         acc[...] = jnp.zeros_like(acc)
     else:
@@ -181,33 +187,49 @@
     def swap(value):
         return lax.ppermute(value, ("core", "zh"), [(0, 0), (1, 2), (2, 1), (3, 3)])
 
-    def other(value, axis):
-        return lax.ppermute(value, axis, [(0, 1), (1, 0)])
+    def to_keeper(value):
+        return lax.ppermute(value, ("core", "zh"), [(1, 0), (2, 3)])
+
+    def to_trader(value):
+        return lax.ppermute(value, ("core", "zh"), [(0, 2), (3, 1)])
+
+    def keepers(value):
+        return lax.ppermute(value, ("core", "zh", "zl"), [(0, 1), (1, 0), (6, 7), (7, 6)])
+
+    def other(value, *axes):
+        last = 2 ** len(axes) - 1
+        return lax.ppermute(value, axes, [(i, last - i) for i in range(last + 1)])
 
     def after(first, value):
         return lax.optimization_barrier((first, value))[1]
 
-    own = []
-    for k in range(CHUNKS):
-        at = slice(k * steps, (k + 1) * steps)
-        own.append(jnp.concatenate([leaf_blocks[at], leaf_dinv[at][:, None]], axis=1))
+    chosen = jnp.take(top_blocks[:, 0], jnp.asarray(padded(above, most))[2 * xy + core], axis=0)
+    top = jnp.concatenate([chosen, top_dinv], axis=0)
+    top = jnp.stack([top, other(top, "zh"), other(top, "zl"), other(top, "zh", "zl")])
+
     names = jnp.zeros((8, wide), f32).at[:3, :leafs].set(leaf_struct.T.astype(f32))
     sides = jnp.concatenate([rhs_leaf.reshape(-1, wide), rhs_top.reshape(-1, wide), names], axis=0)
-
-    swapped = [swap(value) for value in own]
+    blocks, inverses, sides = after(top, (leaf_blocks, leaf_dinv, sides))
+    top = lax.all_gather(top, ("xy", "core"), axis=0, tiled=False)
+
+    def joined(at):
+        return jnp.concatenate([blocks[at], inverses[at][:, None]], axis=1)
+
+    own = joined(slice(None))
+    near = keepers(own)
     sides = swap(sides)
-    nearby = [other(x1, "zl") for x1 in swapped]
-
-    chosen = jnp.take(top_blocks[:, 0], jnp.asarray(padded(above, most))[2 * xy + core], axis=0)
-    top = jnp.concatenate([chosen, top_dinv], axis=0)
-    top = jnp.stack([top, other(top, "zh")])
-    top = jnp.concatenate([top, other(top, "zl")])
-    top = lax.all_gather(top, ("xy", "core"), axis=0, tiled=False)
+    far, across = [], []
+    for k in range(CHUNKS):
+        value = joined(slice(k * steps, (k + 1) * steps))
+        far.append(to_keeper(after(across[k - 2], value) if k > 1 else value))
+        across.append(keepers(after(sides, far[0]) if k == 0 else far[k]))
+    own_passed, near_passed = [to_trader(value) for value in after(across[1], (own, near))]
 
     names = sides[(leafs + 1) * columns :][:3, :leafs].T.astype(jnp.int32).reshape(-1)
     path = jnp.asarray(padded(paths, width))[2 * xy + zh]
-    places = jnp.stack([2 * core + zl, 2 * core + 1 - zl, 2 - 2 * core + zl, 3 - 2 * core - zl])
-    meta = jnp.concatenate([names, places.astype(jnp.int32), path])
+    places = jnp.stack([2 * zh + zl, 2 * zh + 1 - zl, 2 - 2 * zh + zl, 3 - 2 * zh - zl])
+    keeps = (core == zh).astype(jnp.int32)
+    meta = jnp.concatenate([names, places.astype(jnp.int32), path, keeps[None]])
 
     def whole(*shape):
         return pl.BlockSpec((1,) + shape, lambda t: (t,) + (0,) * len(shape))
@@ -233,22 +255,23 @@
     for k in range(CHUNKS):
         last = k == CHUNKS - 1
         shapes = [vectors, merged, merged, chunk]
-        x1, x2 = after(swapped[-1], swapped[k]), after(swapped[-1], nearby[k])
-        if last:
-            x2 = after(state, x2)
-        pieces = (x1, x2, other(x1, "core"), other(x2, "core"))
+        passed = (to_trader(far[k]), to_trader(after(state, across[k]) if last else across[k]))
+        part_of = pl.BlockSpec((steps, 4) + own.shape[2:], functools.partial(lambda k, i: (k, 0, 0, 0), k))
+        specs = [SMEM, part_of, part_of, VMEM, VMEM, part_of, part_of, VMEM, VMEM, VMEM]
         if last:
             shapes.append(jax.ShapeDtypeStruct((tops, width + 1, part, wide), f32))
+        before = () if k == 0 else (state,)
         results = pl.pallas_call(
             functools.partial(forward_kernel, k * steps, k == 0, last, width),
-            in_specs=[SMEM] + [VMEM] * (5 + (k > 0)),
+            grid=(1,),
+            in_specs=specs + [VMEM] * (k > 0),
             out_specs=[VMEM] * len(shapes),
             out_shape=shapes,
             scratch_shapes=[pltpu.VMEM((steps, 4, wide, wide), f32)],
             compiler_params=params(),
             cost_estimate=cost,
             name="leaf_forward",
-        )(meta, *pieces, sides, *(() if k == 0 else (state,)))
+        )(meta, own, near, far[k], across[k], own_passed, near_passed, *passed, sides, *before)
         state = results[0]
         factors.append(results[1:4])
 

time: 224 us -> 239 us (1.067)
  starting transfers between devices: 46.9 us -> 74.2 us
  waiting for transfers between devices: 91.6 us -> 74.4 us
    ppermute x14 -> x22, starting transfers between devices: 16 us -> 54.6 us  [the longest x4 30.7 us: to_keeper(): return lax.ppermute(value, ('core', 'zh'), [(1, 0), (2, 3)])]
    ppermute x8 -> x4, waiting for transfers between devices: 38 us -> 12.7 us  [swap(): return lax.ppermute(value, ('core', 'zh'), [(0, 0), (1, 2), (2, 1), (3, 3)])]
    ppermute x8 -> x4, starting transfers between devices: 27.3 us -> 16.2 us  [swap(): return lax.ppermute(value, ('core', 'zh'), [(0, 0), (1, 2), (2, 1), (3, 3)])]
    ppermute x14 -> x22, waiting for transfers between devices: 51.9 us -> 60 us  [the longest x4 34.4 us: to_keeper(): return lax.ppermute(value, ('core', 'zh'), [(1, 0), (2, 3)])]
    unnamed x62 -> x72, local copies, waits for them, and re-layouts: 12.5 us -> 11 us
  transfers between devices with their start and end apart: 24 -> 28, of which waited for: 13 -> 12; matrix products, arithmetic and copies ran while one was open for 3% -> 4% of each run, Pallas kernels for 14% -> 14%
where the time goes in v2:
time: 239 us; the launch traced here: 238 us
  waiting for transfers between devices  74.4 us (31%)
  starting transfers between devices  74.2 us (31%)
  Pallas kernels  39.1 us (16%)
  local copies, waits for them, and re-layouts  15 us (6%)
  between operations  14.6 us (6%)
  other arithmetic  10.9 us (5%)
  blocking collectives  9.72 us (4%)
    ppermute x4, waiting for transfers between devices, to_keeper(): return lax.ppermute(value, ('core', 'zh'), [(1, 0), (2, 3)])  34.4 us
    ppermute x4, starting transfers between devices, to_keeper(): return lax.ppermute(value, ('core', 'zh'), [(1, 0), (2, 3)])  30.7 us
    ppermute x10, waiting for transfers between devices, to_trader(): return lax.ppermute(value, ('core', 'zh'), [(0, 2), (3, 1)])  23.7 us
    pallas_call x4, Pallas kernels, local(): pl.pallas_call(functools.partial(forward_kernel, k * steps, k == 0, last,...  22.8 us
    ppermute x4, starting transfers between devices, swap(): return lax.ppermute(value, ('core', 'zh'), [(0, 0), (1, 2), (2, 1), (3, 3)])  16.2 us
    ppermute x10, starting transfers between devices, to_trader(): return lax.ppermute(value, ('core', 'zh'), [(0, 2), (3, 1)])  13 us
    ppermute x4, waiting for transfers between devices, swap(): return lax.ppermute(value, ('core', 'zh'), [(0, 0), (1, 2), (2, 1), (3, 3)])  12.7 us
    unnamed x72, local copies, waits for them, and re-layouts  11 us
  transfers between devices with their start and end apart: 28, of which 12 were waited for; matrix products, arithmetic and copies ran while one was open for 4% of the time, Pallas kernels for 14%

profile of v2, /device:TPU:1, one launch (start us, length us, event | category | flops | bytes accessed | tf_op | source)
XLA Modules:
  0.0 238.0 jit_solution(11145697897309581482)
XLA Ops:
  10.0 3.2 %collective-permute-start = (f32[4,32,128]{2,1,0:T(8,128)S(1)}, f32[4,32,128]{2,1,0:T(8,128)S(1)}, u32[]{:S(2)}, u32[]{:S(2)}) collective-permute-start(f32[4,32,128]{2,1,0:T(8,128)S(1)} %get-tuple-element.97), channel_id=1, source_target_pairs={{0,2},{2,0},{1,3},{3,1},{4,6},{6,4},{5,7},{7,5},{8,10},{10,8},{9,1... | collective-permute-start | bytes 196616 | tf_op jit(solution)/shard_map/ppermute | solution.py:201
  13.2 1.3 collective-permute-start.1
  15.2 2.4 select_maximum_fusion
  17.6 2.0 collective-permute-done.2
  20.3 1.7 pad_maximum_fusion.refs_1_
  22.0 2.0 collective-permute-start.4
  25.9 4.3 %collective-permute-start.5 = (f32[8,4,32,128]{3,2,1,0:T(8,128)S(1)}, f32[8,4,32,128]{3,2,1,0:T(8,128)S(1)}, u32[]{:S(2)}, u32[]{:S(2)}) collective-permute-start(f32[8,4,32,128]{3,2,1,0:T(8,128)S(1)} %pad_maximum_fusion.3), channel_id=1, source_target_pairs={{2,0},{4,6},{3,1},{5,7},{10,8},{12,14},{11,9},{13,15},{18,16},{20,... | collective-permute-start | bytes 1572872 | tf_op jit(solution)/shard_map/ppermute | solution.py:191
  30.2 4.3 %collective-permute-start.3 = (f32[2120,128]{1,0:T(8,128)S(1)}, f32[2120,128]{1,0:T(8,128)S(1)}, u32[]{:S(2)}, u32[]{:S(2)}) collective-permute-start(f32[2120,128]{1,0:T(8,128)S(1)} %copy-done.35), channel_id=1, source_target_pairs={{0,0},{2,4},{4,2},{6,6},{1,1},{3,5},{5,3},{7,7},{8,8},{10,12},{12,... | collective-permute-start | bytes 3256328 | tf_op jit(solution)/shard_map/ppermute | solution.py:188
  34.4 7.5 %collective-permute-done.5.refs_3_ = f32[8,4,32,128]{3,2,1,0:T(8,128)S(1)} collective-permute-done((f32[8,4,32,128]{3,2,1,0:T(8,128)S(1)}, f32[8,4,32,128]{3,2,1,0:T(8,128)S(1)}, u32[]{:S(2)}, u32[]{:S(2)}) %collective-permute-start.5) | collective-permute-done | bytes 524320 | tf_op jit(solution)/shard_map/ppermute | solution.py:191
  42.7 8.2 %collective-permute-start.12 = (f32[8,4,32,128]{3,2,1,0:T(8,128)S(1)}, f32[8,4,32,128]{3,2,1,0:T(8,128)}, u32[]{:S(2)}, u32[]{:S(2)}) collective-permute-start(f32[8,4,32,128]{3,2,1,0:T(8,128)S(1)} %pad_maximum_fusion.5), channel_id=1, source_target_pairs={{2,0},{4,6},{3,1},{5,7},{10,8},{12,14},{11,9},{13,15},{18,16},{20,... | collective-permute-start | bytes 1572872 | tf_op jit(solution)/shard_map/ppermute | solution.py:191
  50.8 1.3 collective-permute-start.10
  52.1 1.3 collective-permute-start.9
  53.4 23.0 %collective-permute-done.12.refs_3_ = f32[8,4,32,128]{3,2,1,0:T(8,128)} collective-permute-done((f32[8,4,32,128]{3,2,1,0:T(8,128)S(1)}, f32[8,4,32,128]{3,2,1,0:T(8,128)}, u32[]{:S(2)}, u32[]{:S(2)}) %collective-permute-start.12) | collective-permute-done | bytes 524320 | tf_op jit(solution)/shard_map/ppermute | solution.py:191
  76.4 1.5 collective-permute-start.13
  77.9 1.4 collective-permute-start.20
  79.3 1.1 pad_maximum_fusion.6
  80.5 16.1 %collective-permute-start.14 = (f32[8,4,32,128]{3,2,1,0:T(8,128)S(1)}, f32[8,4,32,128]{3,2,1,0:T(8,128)}, u32[]{:S(2)}, u32[]{:S(2)}) collective-permute-start(f32[8,4,32,128]{3,2,1,0:T(8,128)S(1)} %pad_maximum_fusion.6), channel_id=1, source_target_pairs={{2,0},{4,6},{3,1},{5,7},{10,8},{12,14},{11,9},{13,15},{18,16},{20,... | collective-permute-start | bytes 1572872 | tf_op jit(solution)/shard_map/ppermute | solution.py:191
  97.4 2.1 collective-permute-start.7
  100.3 1.3 collective-permute-start.21
  101.9 1.4 collective-permute-start.15
  104.1 3.6 %collective-permute-done.7.refs_3_ = f32[8,4,32,128]{3,2,1,0:T(8,128)} collective-permute-done((f32[8,4,32,128]{3,2,1,0:T(8,128)}, f32[8,4,32,128]{3,2,1,0:T(8,128)}, u32[]{:S(2)}, u32[]{:S(2)}) %collective-permute-start.7) | collective-permute-done | bytes 524320 | tf_op jit(solution)/shard_map/ppermute | solution.py:191
  107.7 1.3 collective-permute-start.18
  109.0 1.3 collective-permute-start.19
  111.4 1.3 collective-permute-start.16
  112.7 1.3 collective-permute-start.17
  115.1 5.5 %leaf_forward.4 = (f32[40,64,128]{2,1,0:T(8,128)S(1)}, bf16[8,384,128]{2,1,0:T(8,128)(2,1)S(1)}, bf16[8,384,128]{2,1,0:T(8,128)(2,1)S(1)}, f32[8,64,128]{2,1,0:T(8,128)S(1)}) custom-call(s32[105]{0:T(128)S(1)} %concatenate.34.refs_0_.meta, f32[32,4,32,128]{3,2,1,0:T(8,128)S(1)} %pad_maximum_fusion.refs_1_, ...), custom_call_target="tpu_custom_call" | custom-call | flops 4000000000 | bytes 8388608 | tf_op jit(solution)/shard_map/leaf_forward/pallas_call | solution.py:264
  122.2 6.6 %collective-permute-done.18.refs_7_ = f32[8,4,32,128]{3,2,1,0:T(8,128)} collective-permute-done((f32[8,4,32,128]{3,2,1,0:T(8,128)}, f32[8,4,32,128]{3,2,1,0:T(8,128)}, u32[]{:S(2)}, u32[]{:S(2)}) %collective-permute-start.18) | collective-permute-done | bytes 524320 | tf_op jit(solution)/shard_map/ppermute | solution.py:194
  128.9 1.3 collective-permute-start.11
  131.0 5.3 %leaf_forward.5 = (f32[40,64,128]{2,1,0:T(8,128)S(1)}, bf16[8,384,128]{2,1,0:T(8,128)(2,1)S(1)}, bf16[8,384,128]{2,1,0:T(8,128)(2,1)S(1)}, f32[8,64,128]{2,1,0:T(8,128)S(1)}) custom-call(s32[105]{0:T(128)S(1)} %concatenate.34.refs_0_.meta, f32[32,4,32,128]{3,2,1,0:T(8,128)S(1)} %pad_maximum_fusion.refs_1_, ...), custom_call_target="tpu_custom_call" | custom-call | flops 4000000000 | bytes 8388608 | tf_op jit(solution)/shard_map/leaf_forward/pallas_call | solution.py:264
  137.9 5.6 %leaf_forward.6 = (f32[40,64,128]{2,1,0:T(8,128)S(1)}, bf16[8,384,128]{2,1,0:T(8,128)(2,1)S(1)}, bf16[8,384,128]{2,1,0:T(8,128)(2,1)S(1)}, f32[8,64,128]{2,1,0:T(8,128)S(1)}) custom-call(s32[105]{0:T(128)S(1)} %concatenate.34.refs_0_.meta, f32[32,4,32,128]{3,2,1,0:T(8,128)S(1)} %pad_maximum_fusion.refs_1_, ...), custom_call_target="tpu_custom_call" | custom-call | flops 4000000000 | bytes 8388608 | tf_op jit(solution)/shard_map/leaf_forward/pallas_call | solution.py:264
  145.3 1.3 collective-permute-start.22
  147.3 15.4 %collective-permute-done.22.refs_8_ = f32[8,4,32,128]{3,2,1,0:T(8,128)S(1)} collective-permute-done((f32[8,4,32,128]{3,2,1,0:T(8,128)S(1)}, f32[8,4,32,128]{3,2,1,0:T(8,128)S(1)}, u32[]{:S(2)}, u32[]{:S(2)}) %collective-permute-start.22) | collective-permute-done | bytes 524320 | tf_op jit(solution)/shard_map/ppermute | solution.py:194
  162.8 6.5 %leaf_forward.7 = (f32[40,64,128]{2,1,0:T(8,128)}, bf16[8,384,128]{2,1,0:T(8,128)(2,1)S(1)}, bf16[8,384,128]{2,1,0:T(8,128)(2,1)S(1)}, f32[8,64,128]{2,1,0:T(8,128)S(1)}, f32[8,5,8,128]{3,2,1,0:T(8,128)}) custom-call(s32[105]{0:T(128)S(1)} %concatenate.34.refs_0_.meta, f32[32,4,32,128]{3,2,1,0:T(8,128)S(1)} %pad_maximum_fusion.refs_1_, ...), custom_call_target="tpu_custom_call" | custom-call | flops 4000000000 | bytes 8388608 | tf_op jit(solution)/shard_map/leaf_forward/pallas_call | solution.py:264
  171.7 3.4 %all-to-all-start = ((f32[8,5,8,128]{3,2,1,0:T(8,128)}), f32[8,5,8,128]{3,2,1,0:T(8,128)S(1)}, u32[]{:S(2)}, u32[]{:S(2)}) async-start(f32[8,5,8,128]{3,2,1,0:T(8,128)} %get-tuple-element.66), calls=%async_computation | async-start | bytes 327680 | tf_op jit(solution)/shard_map/all_to_all | solution.py:278
  175.2 1.6 copy-done.1
  176.8 2.8 %top_prepare.1 = (bf16[8,384,128]{2,1,0:T(8,128)(2,1)S(1)}, bf16[8,384,128]{2,1,0:T(8,128)(2,1)S(1)}, bf16[8,128,128]{2,1,0:T(8,128)(2,1)S(1)}, bf16[8,128,128]{2,1,0:T(8,128)(2,1)S(1)}) custom-call(s32[4]{0:T(128)S(1)} %pad_add_fusion.meta, f32[8,4,4,32,128]{4,3,2,1,0:T(8,128)S(1)} %bitcast.38), custom_call_target="tpu_custom_call" | custom-call | tf_op jit(solution)/shard_map/top_prepare/pallas_call | solution.py:238
  179.6 1.8 all-to-all-done.incoming
  181.3 2.7 %top_solve.1 = f32[8,5,8,128]{3,2,1,0:T(8,128)S(1)} custom-call(f32[8,5,8,128]{3,2,1,0:T(8,128)S(1)} %all-to-all-done.incoming, bf16[8,384,128]{2,1,0:T(8,128)(2,1)S(1)} %get-tuple-element.67.high, bf16[8,384,128]{2,1,0:T(8,128)(2,1)S(1)} %get-tuple-element.68.low, bf16[8,128,128]{2,1,0:T(8,128)(2,1)S(1)} %get-tuple-element.69.inverse_high, ...), custom_call_target="tpu_custom_call" | custom-call | tf_op jit(solution)/shard_map/top_solve/pallas_call | solution.py:279
  184.1 9.7 %all_to_all.10.state = f32[8,5,8,128]{3,2,1,0:T(8,128)S(1)} all-to-all(f32[8,5,8,128]{3,2,1,0:T(8,128)S(1)} %top_solve.1), channel_id=1, replica_groups=mesh['xy'=4,'core'=2,'zh'=2,'zl'=2] {'xy','zh'}, dimensions={0} | all-to-all | bytes 327680 | tf_op jit(solution)/shard_map/all_to_all | solution.py:287
  193.8 2.4 %leaf_backward.4 = (f32[8,64,128]{2,1,0:T(8,128)S(1)}, f32[40,64,128]{2,1,0:T(8,128)S(1)}) custom-call(s32[105]{0:T(128)S(1)} %concatenate.34.refs_0_.meta, bf16[8,384,128]{2,1,0:T(8,128)(2,1)S(1)} %copy-done.17, bf16[8,384,128]{2,1,0:T(8,128)(2,1)S(1)} %copy-done.19, f32[8,64,128]{2,1,0:T(8,128)S(1)} %copy-done.29, f32[8,5,8,128]{3,2,1,0:T(8,128)S(1)} %all_to_all.10.state), custom_call_target="tpu_custom_call" | custom-call | flops 4000000000 | bytes 8388608 | tf_op jit(solution)/shard_map/leaf_backward/pallas_call | solution.py:292
  196.3 5.4 %collective-permute-start.23 = (f32[8,64,128]{2,1,0:T(8,128)S(1)}, f32[8,64,128]{2,1,0:T(8,128)S(1)}, u32[]{:S(2)}, u32[]{:S(2)}) collective-permute-start(f32[8,64,128]{2,1,0:T(8,128)S(1)} %get-tuple-element.71), channel_id=1, source_target_pairs={{0,0},{2,4},{4,2},{6,6},{1,1},{3,5},{5,3},{7,7},{8,8},{10,12},{12,... | collective-permute-start | bytes 786440 | tf_op jit(solution)/shard_map/ppermute | solution.py:188
  201.8 2.4 %leaf_backward.5 = (f32[8,64,128]{2,1,0:T(8,128)S(1)}, f32[40,64,128]{2,1,0:T(8,128)S(1)}) custom-call(s32[105]{0:T(128)S(1)} %concatenate.34.refs_0_.meta, bf16[8,384,128]{2,1,0:T(8,128)(2,1)S(1)} %copy-done.13, bf16[8,384,128]{2,1,0:T(8,128)(2,1)S(1)} %copy-done.15, f32[8,64,128]{2,1,0:T(8,128)S(1)} %copy-done.27, f32[40,64,128]{2,1,0:T(8,128)S(1)} %get-tuple-element.81.state), custom_call_target="tpu_custom_call" | custom-call | flops 4000000000 | bytes 8388608 | tf_op jit(solution)/shard_map/leaf_backward/pallas_call | solution.py:292
  204.3 2.4 %leaf_backward.6 = (f32[8,64,128]{2,1,0:T(8,128)S(1)}, f32[40,64,128]{2,1,0:T(8,128)S(1)}) custom-call(s32[105]{0:T(128)S(1)} %concatenate.34.refs_0_.meta, bf16[8,384,128]{2,1,0:T(8,128)(2,1)S(1)} %copy-done.9, bf16[8,384,128]{2,1,0:T(8,128)(2,1)S(1)} %copy-done.11, f32[8,64,128]{2,1,0:T(8,128)S(1)} %copy-done.25, f32[40,64,128]{2,1,0:T(8,128)S(1)} %get-tuple-element.82.state), custom_call_target="tpu_custom_call" | custom-call | flops 4000000000 | bytes 8388608 | tf_op jit(solution)/shard_map/leaf_backward/pallas_call | solution.py:292
  206.8 1.9 collective-permute-start.25
  208.7 3.5 %leaf_backward.7 = (f32[8,64,128]{2,1,0:T(8,128)S(1)}, f32[40,64,128]{2,1,0:T(8,128)}) custom-call(s32[105]{0:T(128)S(1)} %concatenate.34.refs_0_.meta, bf16[8,384,128]{2,1,0:T(8,128)(2,1)S(1)} %copy-done.21, bf16[8,384,128]{2,1,0:T(8,128)(2,1)S(1)} %copy-done.23, f32[8,64,128]{2,1,0:T(8,128)S(1)} %copy-done.31, f32[40,64,128]{2,1,0:T(8,128)S(1)} %get-tuple-element.83.state), custom_call_target="tpu_custom_call" | custom-call | flops 4000000000 | bytes 8388608 | tf_op jit(solution)/shard_map/leaf_backward/pallas_call | solution.py:292
  212.3 4.5 %collective-permute-start.24 = (f32[8,64,128]{2,1,0:T(8,128)S(1)}, f32[8,64,128]{2,1,0:T(8,128)S(1)}, u32[]{:S(2)}, u32[]{:S(2)}) collective-permute-start(f32[8,64,128]{2,1,0:T(8,128)S(1)} %get-tuple-element.85), channel_id=1, source_target_pairs={{0,0},{2,4},{4,2},{6,6},{1,1},{3,5},{5,3},{7,7},{8,8},{10,12},{12,... | collective-permute-start | bytes 786440 | tf_op jit(solution)/shard_map/ppermute | solution.py:188
  216.8 10.5 %collective-permute-done.25 = f32[17,64,128]{2,1,0:T(8,128)S(1)} collective-permute-done((f32[17,64,128]{2,1,0:T(8,128)S(1)}, f32[17,64,128]{2,1,0:T(8,128)S(1)}, u32[]{:S(2)}, u32[]{:S(2)}) %collective-permute-start.25) | collective-permute-done | bytes 557088 | tf_op jit(solution)/shard_map/ppermute | solution.py:188
  228.0 2.2 collective-permute-done.24
  (119 shorter events, 22.6 us)
Async XLA Ops:
  7.2 168.0 %all-gather.3.cloned.1.call-start = ((), (), s32[]{:S(2)}) async-start(), calls=%async_computation.2 | async-start | bytes 2359296 | tf_op jit(solution)/shard_map/all_gather | solution.py:213
  10.0 7.6 %collective-permute-start = (f32[4,32,128]{2,1,0:T(8,128)S(1)}, f32[4,32,128]{2,1,0:T(8,128)S(1)}, u32[]{:S(2)}, u32[]{:S(2)}) collective-permute-start(f32[4,32,128]{2,1,0:T(8,128)S(1)} %get-tuple-element.97), channel_id=1, source_target_pairs={{0,2},{2,0},{1,3},{3,1},{4,6},{6,4},{5,7},{7,5},{8,10},{10,8},{9,1... | collective-permute-start | bytes 196616 | tf_op jit(solution)/shard_map/ppermute | solution.py:201
  13.2 4.4 %collective-permute-start.1 = (f32[4,32,128]{2,1,0:T(8,128)S(1)}, f32[4,32,128]{2,1,0:T(8,128)S(1)}, u32[]{:S(2)}, u32[]{:S(2)}) collective-permute-start(f32[4,32,128]{2,1,0:T(8,128)S(1)} %get-tuple-element.97), channel_id=1, source_target_pairs={{0,1},{1,0},{2,3},{3,2},{4,5},{5,4},{6,7},{7,6},{8,9},{9,8},{10,11... | collective-permute-start | bytes 196616 | tf_op jit(solution)/shard_map/ppermute | solution.py:201
  14.5 5.0 %collective-permute-start.2 = (f32[4,32,128]{2,1,0:T(8,128)S(1)}, f32[4,32,128]{2,1,0:T(8,128)S(1)}, u32[]{:S(2)}, u32[]{:S(2)}) collective-permute-start(f32[4,32,128]{2,1,0:T(8,128)S(1)} %get-tuple-element.97), channel_id=1, source_target_pairs={{0,3},{1,2},{2,1},{3,0},{4,7},{5,6},{6,5},{7,4},{8,11},{9,10},{10,... | collective-permute-start | bytes 196616 | tf_op jit(solution)/shard_map/ppermute | solution.py:201
  15.2 5.1 %copy-start.33 = (f32[32,32,128]{2,1,0:T(8,128)S(1)}, f32[32,32,128]{2,1,0:T(8,128)}, u32[]{:S(2)}) copy-start(f32[32,32,128]{2,1,0:T(8,128)} %param.14) | copy-start | bytes 1572868
  20.3 4.5 %copy-start.32 = (f32[32,3,32,128]{3,2,1,0:T(8,128)S(1)}, f32[32,3,32,128]{3,2,1,0:T(8,128)}, u32[]{:S(2)}) copy-start(f32[32,3,32,128]{3,2,1,0:T(8,128)} %param.13) | copy-start | bytes 4718596
  22.0 28.8 %collective-permute-start.4 = (f32[32,4,32,128]{3,2,1,0:T(8,128)S(1)}, f32[32,4,32,128]{3,2,1,0:T(8,128)}, u32[]{:S(2)}, u32[]{:S(2)}) collective-permute-start(f32[32,4,32,128]{3,2,1,0:T(8,128)S(1)} %pad_maximum_fusion.refs_1_), channel_id=1, source_target_pairs={{0,1},{1,0},{6,7},{7,6},{8,9},{9,8},{14,15},{15,14},{16,17},{17,16... | collective-permute-start | bytes 6291464 | tf_op jit(solution)/shard_map/ppermute | solution.py:197
  24.8 5.4 %copy-start.35 = (f32[2120,128]{1,0:T(8,128)S(1)}, f32[2120,128]{1,0:T(8,128)}, u32[]{:S(2)}) copy-start(f32[2120,128]{1,0:T(8,128)} %select_maximum_fusion) | copy-start | bytes 3256324
  25.9 16.1 %collective-permute-start.5 = (f32[8,4,32,128]{3,2,1,0:T(8,128)S(1)}, f32[8,4,32,128]{3,2,1,0:T(8,128)S(1)}, u32[]{:S(2)}, u32[]{:S(2)}) collective-permute-start(f32[8,4,32,128]{3,2,1,0:T(8,128)S(1)} %pad_maximum_fusion.3), channel_id=1, source_target_pairs={{2,0},{4,6},{3,1},{5,7},{10,8},{12,14},{11,9},{13,15},{18,16},{20,... | collective-permute-start | bytes 1572872 | tf_op jit(solution)/shard_map/ppermute | solution.py:191
  30.2 46.2 %collective-permute-start.3 = (f32[2120,128]{1,0:T(8,128)S(1)}, f32[2120,128]{1,0:T(8,128)S(1)}, u32[]{:S(2)}, u32[]{:S(2)}) collective-permute-start(f32[2120,128]{1,0:T(8,128)S(1)} %copy-done.35), channel_id=1, source_target_pairs={{0,0},{2,4},{4,2},{6,6},{1,1},{3,5},{5,3},{7,7},{8,8},{10,12},{12,... | collective-permute-start | bytes 3256328 | tf_op jit(solution)/shard_map/ppermute | solution.py:188
  41.9 34.5 %copy-start.2 = (f32[8,4,32,128]{3,2,1,0:T(8,128)}, f32[8,4,32,128]{3,2,1,0:T(8,128)S(1)}, u32[]{:S(2)}) copy-start(f32[8,4,32,128]{3,2,1,0:T(8,128)S(1)} %collective-permute-done.5.refs_3_) | copy-start | bytes 1572868
  41.9 8.9 %collective-permute-start.6 = (f32[8,4,32,128]{3,2,1,0:T(8,128)S(1)}, f32[8,4,32,128]{3,2,1,0:T(8,128)S(1)}, u32[]{:S(2)}, u32[]{:S(2)}) collective-permute-start(f32[8,4,32,128]{3,2,1,0:T(8,128)S(1)} %collective-permute-done.5.refs_3_), channel_id=1, source_target_pairs={{0,1},{1,0},{6,7},{7,6},{8,9},{9,8},{14,15},{15,14},{16,17},{17,16... | collective-permute-start | bytes 1572872 | tf_op jit(solution)/shard_map/ppermute | solution.py:197
  42.7 33.8 %collective-permute-start.12 = (f32[8,4,32,128]{3,2,1,0:T(8,128)S(1)}, f32[8,4,32,128]{3,2,1,0:T(8,128)}, u32[]{:S(2)}, u32[]{:S(2)}) collective-permute-start(f32[8,4,32,128]{3,2,1,0:T(8,128)S(1)} %pad_maximum_fusion.5), channel_id=1, source_target_pairs={{2,0},{4,6},{3,1},{5,7},{10,8},{12,14},{11,9},{13,15},{18,16},{20,... | collective-permute-start | bytes 1572872 | tf_op jit(solution)/shard_map/ppermute | solution.py:191
  50.8 25.6 %copy-start.4 = (f32[8,4,32,128]{3,2,1,0:T(8,128)}, f32[8,4,32,128]{3,2,1,0:T(8,128)S(1)}, u32[]{:S(2)}) copy-start(f32[8,4,32,128]{3,2,1,0:T(8,128)S(1)} %collective-permute-done.6.refs_4_) | copy-start | bytes 1572868
  50.8 60.6 %collective-permute-start.10 = (f32[32,4,32,128]{3,2,1,0:T(8,128)}, f32[32,4,32,128]{3,2,1,0:T(8,128)}, u32[]{:S(2)}, u32[]{:S(2)}) collective-permute-start(f32[32,4,32,128]{3,2,1,0:T(8,128)} %collective-permute-done.4.refs_2_), channel_id=1, source_target_pairs={{0,4},{6,2},{1,5},{7,3},{8,12},{14,10},{9,13},{15,11},{16,20},{22,... | collective-permute-start | bytes 6291464 | tf_op jit(solution)/shard_map/ppermute | solution.py:194
  52.1 60.6 %collective-permute-start.9 = (f32[32,4,32,128]{3,2,1,0:T(8,128)S(1)}, f32[32,4,32,128]{3,2,1,0:T(8,128)}, u32[]{:S(2)}, u32[]{:S(2)}) collective-permute-start(f32[32,4,32,128]{3,2,1,0:T(8,128)S(1)} %pad_maximum_fusion.refs_1_), channel_id=1, source_target_pairs={{0,4},{6,2},{1,5},{7,3},{8,12},{14,10},{9,13},{15,11},{16,20},{22,... | collective-permute-start | bytes 6291464 | tf_op jit(solution)/shard_map/ppermute | solution.py:194
  76.4 4.0 %collective-permute-start.13 = (f32[8,4,32,128]{3,2,1,0:T(8,128)}, f32[8,4,32,128]{3,2,1,0:T(8,128)}, u32[]{:S(2)}, u32[]{:S(2)}) collective-permute-start(f32[8,4,32,128]{3,2,1,0:T(8,128)} %collective-permute-done.12.refs_3_), channel_id=1, source_target_pairs={{0,1},{1,0},{6,7},{7,6},{8,9},{9,8},{14,15},{15,14},{16,17},{17,16... | collective-permute-start | bytes 1572872 | tf_op jit(solution)/shard_map/ppermute | solution.py:197
  77.9 18.7 %copy-start.34 = (f32[8,3,32,128]{3,2,1,0:T(8,128)S(1)}, f32[8,3,32,128]{3,2,1,0:T(8,128)}, u32[]{:S(2)}) copy-start(f32[8,3,32,128]{3,2,1,0:T(8,128)} %get-tuple-element.90) | copy-start | bytes 1179652
  77.9 21.6 %collective-permute-start.20 = (f32[8,4,32,128]{3,2,1,0:T(8,128)}, f32[8,4,32,128]{3,2,1,0:T(8,128)S(1)}, u32[]{:S(2)}, u32[]{:S(2)}) collective-permute-start(f32[8,4,32,128]{3,2,1,0:T(8,128)} %collective-permute-done.12.refs_3_), channel_id=1, source_target_pairs={{0,4},{6,2},{1,5},{7,3},{8,12},{14,10},{9,13},{15,11},{16,20},{22,... | collective-permute-start | bytes 1572872 | tf_op jit(solution)/shard_map/ppermute | solution.py:194
  80.5 21.5 %collective-permute-start.14 = (f32[8,4,32,128]{3,2,1,0:T(8,128)S(1)}, f32[8,4,32,128]{3,2,1,0:T(8,128)}, u32[]{:S(2)}, u32[]{:S(2)}) collective-permute-start(f32[8,4,32,128]{3,2,1,0:T(8,128)S(1)} %pad_maximum_fusion.6), channel_id=1, source_target_pairs={{2,0},{4,6},{3,1},{5,7},{10,8},{12,14},{11,9},{13,15},{18,16},{20,... | collective-permute-start | bytes 1572872 | tf_op jit(solution)/shard_map/ppermute | solution.py:191
  97.4 10.2 %collective-permute-start.7 = (f32[8,4,32,128]{3,2,1,0:T(8,128)}, f32[8,4,32,128]{3,2,1,0:T(8,128)}, u32[]{:S(2)}, u32[]{:S(2)}) collective-permute-start(f32[8,4,32,128]{3,2,1,0:T(8,128)} %pad_maximum_fusion.4), channel_id=1, source_target_pairs={{2,0},{4,6},{3,1},{5,7},{10,8},{12,14},{11,9},{13,15},{18,16},{20,... | collective-permute-start | bytes 1572872 | tf_op jit(solution)/shard_map/ppermute | solution.py:191
  100.3 8.7 %collective-permute-start.21 = (f32[8,4,32,128]{3,2,1,0:T(8,128)}, f32[8,4,32,128]{3,2,1,0:T(8,128)}, u32[]{:S(2)}, u32[]{:S(2)}) collective-permute-start(f32[8,4,32,128]{3,2,1,0:T(8,128)} %collective-permute-done.13.refs_4_), channel_id=1, source_target_pairs={{0,4},{6,2},{1,5},{7,3},{8,12},{14,10},{9,13},{15,11},{16,20},{22,... | collective-permute-start | bytes 1572872 | tf_op jit(solution)/shard_map/ppermute | solution.py:194
  101.9 8.6 %collective-permute-start.15 = (f32[8,4,32,128]{3,2,1,0:T(8,128)}, f32[8,4,32,128]{3,2,1,0:T(8,128)}, u32[]{:S(2)}, u32[]{:S(2)}) collective-permute-start(f32[8,4,32,128]{3,2,1,0:T(8,128)} %collective-permute-done.14.refs_3_), channel_id=1, source_target_pairs={{0,1},{1,0},{6,7},{7,6},{8,9},{9,8},{14,15},{15,14},{16,17},{17,16... | collective-permute-start | bytes 1572872 | tf_op jit(solution)/shard_map/ppermute | solution.py:197
  107.7 21.2 %collective-permute-start.18 = (f32[8,4,32,128]{3,2,1,0:T(8,128)}, f32[8,4,32,128]{3,2,1,0:T(8,128)}, u32[]{:S(2)}, u32[]{:S(2)}) collective-permute-start(f32[8,4,32,128]{3,2,1,0:T(8,128)} %copy-done.2), channel_id=1, source_target_pairs={{0,4},{6,2},{1,5},{7,3},{8,12},{14,10},{9,13},{15,11},{16,20},{22,... | collective-permute-start | bytes 1572872 | tf_op jit(solution)/shard_map/ppermute | solution.py:194
  109.0 22.0 %collective-permute-start.19 = (f32[8,4,32,128]{3,2,1,0:T(8,128)}, f32[8,4,32,128]{3,2,1,0:T(8,128)}, u32[]{:S(2)}, u32[]{:S(2)}) collective-permute-start(f32[8,4,32,128]{3,2,1,0:T(8,128)} %copy-done.4), channel_id=1, source_target_pairs={{0,4},{6,2},{1,5},{7,3},{8,12},{14,10},{9,13},{15,11},{16,20},{22,... | collective-permute-start | bytes 1572872 | tf_op jit(solution)/shard_map/ppermute | solution.py:194
  110.6 20.4 %copy-start.3 = (f32[8,4,32,128]{3,2,1,0:T(8,128)S(1)}, f32[8,4,32,128]{3,2,1,0:T(8,128)}, u32[]{:S(2)}) copy-start(f32[8,4,32,128]{3,2,1,0:T(8,128)} %copy-done.2) | copy-start | bytes 1572868
  110.6 20.4 %copy-start.5 = (f32[8,4,32,128]{3,2,1,0:T(8,128)S(1)}, f32[8,4,32,128]{3,2,1,0:T(8,128)}, u32[]{:S(2)}) copy-start(f32[8,4,32,128]{3,2,1,0:T(8,128)} %copy-done.4) | copy-start | bytes 1572868
  110.6 34.7 %collective-permute-start.8 = (f32[8,4,32,128]{3,2,1,0:T(8,128)}, f32[8,4,32,128]{3,2,1,0:T(8,128)S(1)}, u32[]{:S(2)}, u32[]{:S(2)}) collective-permute-start(f32[8,4,32,128]{3,2,1,0:T(8,128)} %collective-permute-done.7.refs_3_), channel_id=1, source_target_pairs={{0,1},{1,0},{6,7},{7,6},{8,9},{9,8},{14,15},{15,14},{16,17},{17,16... | collective-permute-start | bytes 1572872 | tf_op jit(solution)/shard_map/ppermute | solution.py:197
  111.4 26.5 %collective-permute-start.16 = (f32[8,4,32,128]{3,2,1,0:T(8,128)}, f32[8,4,32,128]{3,2,1,0:T(8,128)S(1)}, u32[]{:S(2)}, u32[]{:S(2)}) collective-permute-start(f32[8,4,32,128]{3,2,1,0:T(8,128)} %collective-permute-done.14.refs_3_), channel_id=1, source_target_pairs={{0,4},{6,2},{1,5},{7,3},{8,12},{14,10},{9,13},{15,11},{16,20},{22,... | collective-permute-start | bytes 1572872 | tf_op jit(solution)/shard_map/ppermute | solution.py:194
  112.7 25.2 %collective-permute-start.17 = (f32[8,4,32,128]{3,2,1,0:T(8,128)}, f32[8,4,32,128]{3,2,1,0:T(8,128)S(1)}, u32[]{:S(2)}, u32[]{:S(2)}) collective-permute-start(f32[8,4,32,128]{3,2,1,0:T(8,128)} %collective-permute-done.15.refs_4_), channel_id=1, source_target_pairs={{0,4},{6,2},{1,5},{7,3},{8,12},{14,10},{9,13},{15,11},{16,20},{22,... | collective-permute-start | bytes 1572872 | tf_op jit(solution)/shard_map/ppermute | solution.py:194
  122.2 14.0 %copy-start.22 = (bf16[8,384,128]{2,1,0:T(8,128)(2,1)}, bf16[8,384,128]{2,1,0:T(8,128)(2,1)S(1)}, u32[]{:S(2)}) copy-start(bf16[8,384,128]{2,1,0:T(8,128)(2,1)S(1)} %get-tuple-element.73.low) | copy-start | bytes 2359300
  128.9 18.4 %collective-permute-start.11 = (f32[8,4,32,128]{3,2,1,0:T(8,128)}, f32[8,4,32,128]{3,2,1,0:T(8,128)S(1)}, u32[]{:S(2)}, u32[]{:S(2)}) collective-permute-start(f32[8,4,32,128]{3,2,1,0:T(8,128)} %collective-permute-done.7.refs_3_), channel_id=1, source_target_pairs={{0,4},{6,2},{1,5},{7,3},{8,12},{14,10},{9,13},{15,11},{16,20},{22,... | collective-permute-start | bytes 1572872 | tf_op jit(solution)/shard_map/ppermute | solution.py:194
  137.9 5.6 %copy-start.10 = (bf16[8,384,128]{2,1,0:T(8,128)(2,1)}, bf16[8,384,128]{2,1,0:T(8,128)(2,1)S(1)}, u32[]{:S(2)}) copy-start(bf16[8,384,128]{2,1,0:T(8,128)(2,1)S(1)} %get-tuple-element.76.low) | copy-start | bytes 2359300
  145.3 23.9 %copy-start.26 = (f32[8,64,128]{2,1,0:T(8,128)}, f32[8,64,128]{2,1,0:T(8,128)S(1)}, u32[]{:S(2)}) copy-start(f32[8,64,128]{2,1,0:T(8,128)S(1)} %get-tuple-element.80.scaled) | copy-start | bytes 786436
  145.3 17.5 %collective-permute-start.22 = (f32[8,4,32,128]{3,2,1,0:T(8,128)S(1)}, f32[8,4,32,128]{3,2,1,0:T(8,128)S(1)}, u32[]{:S(2)}, u32[]{:S(2)}) collective-permute-start(f32[8,4,32,128]{3,2,1,0:T(8,128)S(1)} %collective-permute-done.8.refs_4_), channel_id=1, source_target_pairs={{0,4},{6,2},{1,5},{7,3},{8,12},{14,10},{9,13},{15,11},{16,20},{22,... | collective-permute-start | bytes 1572872 | tf_op jit(solution)/shard_map/ppermute | solution.py:194
  171.7 9.6 %all-to-all-start = ((f32[8,5,8,128]{3,2,1,0:T(8,128)}), f32[8,5,8,128]{3,2,1,0:T(8,128)S(1)}, u32[]{:S(2)}, u32[]{:S(2)}) async-start(f32[8,5,8,128]{3,2,1,0:T(8,128)} %get-tuple-element.66), calls=%async_computation | async-start | bytes 327680 | tf_op jit(solution)/shard_map/all_to_all | solution.py:278
  181.3 12.4 %copy-start.17 = (bf16[8,384,128]{2,1,0:T(8,128)(2,1)S(1)}, bf16[8,384,128]{2,1,0:T(8,128)(2,1)}, u32[]{:S(2)}) copy-start(bf16[8,384,128]{2,1,0:T(8,128)(2,1)} %copy-done.16) | copy-start | bytes 2359300
  181.3 12.4 %copy-start.19 = (bf16[8,384,128]{2,1,0:T(8,128)(2,1)S(1)}, bf16[8,384,128]{2,1,0:T(8,128)(2,1)}, u32[]{:S(2)}) copy-start(bf16[8,384,128]{2,1,0:T(8,128)(2,1)} %copy-done.18) | copy-start | bytes 2359300
  181.3 12.4 %copy-start.29 = (f32[8,64,128]{2,1,0:T(8,128)S(1)}, f32[8,64,128]{2,1,0:T(8,128)}, u32[]{:S(2)}) copy-start(f32[8,64,128]{2,1,0:T(8,128)} %copy-done.28) | copy-start | bytes 786436
  193.8 7.9 %copy-start.13 = (bf16[8,384,128]{2,1,0:T(8,128)(2,1)S(1)}, bf16[8,384,128]{2,1,0:T(8,128)(2,1)}, u32[]{:S(2)}) copy-start(bf16[8,384,128]{2,1,0:T(8,128)(2,1)} %copy-done.12) | copy-start | bytes 2359300
  193.8 7.9 %copy-start.15 = (bf16[8,384,128]{2,1,0:T(8,128)(2,1)S(1)}, bf16[8,384,128]{2,1,0:T(8,128)(2,1)}, u32[]{:S(2)}) copy-start(bf16[8,384,128]{2,1,0:T(8,128)(2,1)} %copy-done.14) | copy-start | bytes 2359300
  193.8 7.9 %copy-start.27 = (f32[8,64,128]{2,1,0:T(8,128)S(1)}, f32[8,64,128]{2,1,0:T(8,128)}, u32[]{:S(2)}) copy-start(f32[8,64,128]{2,1,0:T(8,128)} %copy-done.26) | copy-start | bytes 786436
  196.3 16.0 %collective-permute-start.23 = (f32[8,64,128]{2,1,0:T(8,128)S(1)}, f32[8,64,128]{2,1,0:T(8,128)S(1)}, u32[]{:S(2)}, u32[]{:S(2)}) collective-permute-start(f32[8,64,128]{2,1,0:T(8,128)S(1)} %get-tuple-element.71), channel_id=1, source_target_pairs={{0,0},{2,4},{4,2},{6,6},{1,1},{3,5},{5,3},{7,7},{8,8},{10,12},{12,... | collective-permute-start | bytes 786440 | tf_op jit(solution)/shard_map/ppermute | solution.py:188
  204.2 4.5 %copy-start.21 = (bf16[8,384,128]{2,1,0:T(8,128)(2,1)S(1)}, bf16[8,384,128]{2,1,0:T(8,128)(2,1)}, u32[]{:S(2)}) copy-start(bf16[8,384,128]{2,1,0:T(8,128)(2,1)} %copy-done.20) | copy-start | bytes 2359300
  204.2 4.5 %copy-start.23 = (bf16[8,384,128]{2,1,0:T(8,128)(2,1)S(1)}, bf16[8,384,128]{2,1,0:T(8,128)(2,1)}, u32[]{:S(2)}) copy-start(bf16[8,384,128]{2,1,0:T(8,128)(2,1)} %copy-done.22) | copy-start | bytes 2359300
  204.3 4.5 %copy-start.31 = (f32[8,64,128]{2,1,0:T(8,128)S(1)}, f32[8,64,128]{2,1,0:T(8,128)}, u32[]{:S(2)}) copy-start(f32[8,64,128]{2,1,0:T(8,128)} %copy-done.30) | copy-start | bytes 786436
  206.8 20.5 %collective-permute-start.25 = (f32[17,64,128]{2,1,0:T(8,128)S(1)}, f32[17,64,128]{2,1,0:T(8,128)S(1)}, u32[]{:S(2)}, u32[]{:S(2)}) collective-permute-start(f32[17,64,128]{2,1,0:T(8,128)S(1)} %pad_maximum_fusion.2), channel_id=1, source_target_pairs={{0,0},{2,4},{4,2},{6,6},{1,1},{3,5},{5,3},{7,7},{8,8},{10,12},{12,... | collective-permute-start | bytes 1671176 | tf_op jit(solution)/shard_map/ppermute | solution.py:188
  212.3 17.8 %collective-permute-start.24 = (f32[8,64,128]{2,1,0:T(8,128)S(1)}, f32[8,64,128]{2,1,0:T(8,128)S(1)}, u32[]{:S(2)}, u32[]{:S(2)}) collective-permute-start(f32[8,64,128]{2,1,0:T(8,128)S(1)} %get-tuple-element.85), channel_id=1, source_target_pairs={{0,0},{2,4},{4,2},{6,6},{1,1},{3,5},{5,3},{7,7},{8,8},{10,12},{12,... | collective-permute-start | bytes 786440 | tf_op jit(solution)/shard_map/ppermute | solution.py:188
  (16 other events, 19.8 us)
Sparse Core Ops, SparseCore 0:
  78.0 37.4 all-gather.2

commit v3 on v2

--- a/solution.py
+++ b/solution.py
@@ -9,7 +9,8 @@
 from jax.sharding import Mesh
 from jax.sharding import PartitionSpec as P
 
-CHUNKS = 4
+CHUNKS = 2
+TURNS = 4
 f32 = jnp.float32
 bf16 = jnp.bfloat16
 SMEM = pl.BlockSpec(memory_space=pltpu.SMEM)
@@ -17,7 +18,7 @@
 
 
 def params():
-    return pltpu.CompilerParams(vmem_limit_bytes=40 * 2**20)
+    return pltpu.CompilerParams(vmem_limit_bytes=48 * 2**20)
 
 
 def split(value):
@@ -104,7 +105,7 @@
 
 def backward_kernel(base, first, width, meta, high, low, scaled, state, out, z):
     steps, wide = scaled.shape[0], scaled.shape[2]
-    leafs = steps * CHUNKS
+    leafs = steps * TURNS
     if first:
         part = state.shape[2]
         groups = scaled.shape[1] // part
@@ -205,47 +206,28 @@
 
     chosen = jnp.take(top_blocks[:, 0], jnp.asarray(padded(above, most))[2 * xy + core], axis=0)
     top = jnp.concatenate([chosen, top_dinv], axis=0)
-    top = jnp.stack([top, other(top, "zh"), other(top, "zl"), other(top, "zh", "zl")])
-
     names = jnp.zeros((8, wide), f32).at[:3, :leafs].set(leaf_struct.T.astype(f32))
     sides = jnp.concatenate([rhs_leaf.reshape(-1, wide), rhs_top.reshape(-1, wide), names], axis=0)
-    blocks, inverses, sides = after(top, (leaf_blocks, leaf_dinv, sides))
-    top = lax.all_gather(top, ("xy", "core"), axis=0, tiled=False)
-
     def joined(at):
-        return jnp.concatenate([blocks[at], inverses[at][:, None]], axis=1)
+        return jnp.concatenate([leaf_blocks[at], leaf_dinv[at][:, None]], axis=1)
 
     own = joined(slice(None))
+    parts = [joined(slice(k * steps, (k + 1) * steps)) for k in range(CHUNKS)]
     near = keepers(own)
     sides = swap(sides)
-    far, across = [], []
-    for k in range(CHUNKS):
-        value = joined(slice(k * steps, (k + 1) * steps))
-        far.append(to_keeper(after(across[k - 2], value) if k > 1 else value))
-        across.append(keepers(after(sides, far[0]) if k == 0 else far[k]))
-    own_passed, near_passed = [to_trader(value) for value in after(across[1], (own, near))]
+    far = [to_keeper(part) for part in parts]
+    across = [keepers(after(sides, far[0]))] + [keepers(value) for value in far[1:]]
+    top, own_late, near_late = after(across[0], (top, own, near))
+    own_passed, near_passed = to_trader(own_late), to_trader(near_late)
+    top = jnp.stack([top, other(top, "zh")])
+    top = jnp.concatenate([top, other(top, "zl")])
+    top = lax.all_gather(top, ("xy", "core"), axis=0, tiled=False)
 
     names = sides[(leafs + 1) * columns :][:3, :leafs].T.astype(jnp.int32).reshape(-1)
     path = jnp.asarray(padded(paths, width))[2 * xy + zh]
     places = jnp.stack([2 * zh + zl, 2 * zh + 1 - zl, 2 - 2 * zh + zl, 3 - 2 * zh - zl])
     keeps = (core == zh).astype(jnp.int32)
     meta = jnp.concatenate([names, places.astype(jnp.int32), path, keeps[None]])
-
-    def whole(*shape):
-        return pl.BlockSpec((1,) + shape, lambda t: (t,) + (0,) * len(shape))
-
-    top_places = jnp.stack([2 * zh + zl, 2 - 2 * zh + zl, 2 * zh + 1 - zl, 3 - 2 * zh - zl])
-    top_factor = pl.pallas_call(
-        top_prepare_kernel,
-        grid=(tops,),
-        in_specs=[SMEM, whole(*top.shape[1:])],
-        out_specs=[whole(most * wide, wide)] * 2 + [whole(wide, wide)] * 2,
-        out_shape=[jax.ShapeDtypeStruct((tops, most * wide, wide), bf16)] * 2
-        + [jax.ShapeDtypeStruct((tops, wide, wide), bf16)] * 2,
-        scratch_shapes=[pltpu.VMEM((width, wide, wide), f32)],
-        compiler_params=params(),
-        name="top_prepare",
-    )(top_places.astype(jnp.int32), top)
 
     vectors = jax.ShapeDtypeStruct((leafs + tops, columns, wide), f32)
     merged = jax.ShapeDtypeStruct((steps, 3 * wide, wide), bf16)
@@ -255,7 +237,7 @@
     for k in range(CHUNKS):
         last = k == CHUNKS - 1
         shapes = [vectors, merged, merged, chunk]
-        passed = (to_trader(far[k]), to_trader(after(state, across[k]) if last else across[k]))
+        passed = (to_trader(far[k]), to_trader(across[k]))
         part_of = pl.BlockSpec((steps, 4) + own.shape[2:], functools.partial(lambda k, i: (k, 0, 0, 0), k))
         specs = [SMEM, part_of, part_of, VMEM, VMEM, part_of, part_of, VMEM, VMEM, VMEM]
         if last:
@@ -275,6 +257,22 @@
         state = results[0]
         factors.append(results[1:4])
 
+    def whole(*shape):
+        return pl.BlockSpec((1,) + shape, lambda t: (t,) + (0,) * len(shape))
+
+    top_places = jnp.stack([2 * zh + zl, 2 - 2 * zh + zl, 2 * zh + 1 - zl, 3 - 2 * zh - zl])
+    top_factor = pl.pallas_call(
+        top_prepare_kernel,
+        grid=(tops,),
+        in_specs=[SMEM, whole(*top.shape[1:])],
+        out_specs=[whole(most * wide, wide)] * 2 + [whole(wide, wide)] * 2,
+        out_shape=[jax.ShapeDtypeStruct((tops, most * wide, wide), bf16)] * 2
+        + [jax.ShapeDtypeStruct((tops, wide, wide), bf16)] * 2,
+        scratch_shapes=[pltpu.VMEM((width, wide, wide), f32)],
+        compiler_params=params(),
+        name="top_prepare",
+    )(top_places.astype(jnp.int32), after(results[4], top))
+
     incoming = lax.all_to_all(results[4], ("xy", "zh"), split_axis=0, concat_axis=0, tiled=True)
     outgoing = pl.pallas_call(
         functools.partial(top_kernel, above, paths),
@@ -287,17 +285,25 @@
     state = lax.all_to_all(outgoing, ("xy", "zh"), split_axis=0, concat_axis=0, tiled=True)
     own_top = state[:groups, width].reshape(1, columns, wide)
 
-    found = [None] * CHUNKS
-    for k in range(CHUNKS - 1, -1, -1):
+    found = [None] * TURNS
+    steps = leafs // TURNS
+    share = TURNS // CHUNKS
+    chunk = jax.ShapeDtypeStruct((steps, columns, wide), f32)
+    for k in range(TURNS - 1, -1, -1):
+        part_of = [
+            pl.BlockSpec((steps,) + shape, functools.partial(lambda k, i: (k, 0, 0), k % share))
+            for shape in ((3 * wide, wide), (3 * wide, wide), (columns, wide))
+        ]
         found[k], state = pl.pallas_call(
-            functools.partial(backward_kernel, k * steps, k == CHUNKS - 1, width),
-            in_specs=[SMEM] + [VMEM] * 4,
+            functools.partial(backward_kernel, k * steps, k == TURNS - 1, width),
+            grid=(1,),
+            in_specs=[SMEM] + part_of + [VMEM],
             out_specs=[VMEM] * 2,
             out_shape=[chunk, vectors],
             compiler_params=params(),
             cost_estimate=cost,
             name="leaf_backward",
-        )(meta, *factors[k], state)
+        )(meta, *factors[k // share], state)
     late = swap(found[-1])
     middle = swap(jnp.concatenate(found[1:-1] + [own_top], axis=0))
     early = swap(after(late, found[0]))

time: 239 us -> 235 us (0.983)
  local copies, waits for them, and re-layouts: 15 us -> 12.5 us
  Pallas kernels: 39.1 us -> 41.5 us
    ppermute x4 -> x2, starting transfers between devices: 30.7 us -> 6.12 us  [to_keeper(): return lax.ppermute(value, ('core', 'zh'), [(1, 0), (2, 3)])]
    ppermute x3 -> x2, starting transfers between devices: 4.5 us -> 22.8 us  [other(): return lax.ppermute(value, axes, [(i, last - i) for i in range(last + 1)])]
    all_to_all x1, starting transfers between devices: 3.44 us -> 15.1 us  [local(): lax.all_to_all(results[4], ('xy', 'zh'), split_axis=0, concat_axis=0, til...]
    ppermute x10 -> x6, waiting for transfers between devices: 23.7 us -> 14.8 us  [to_trader(): return lax.ppermute(value, ('core', 'zh'), [(0, 2), (3, 1)])]
    ppermute x4 -> x2, waiting for transfers between devices: 34.4 us -> 42.8 us  [to_keeper(): return lax.ppermute(value, ('core', 'zh'), [(1, 0), (2, 3)])]
    ppermute x10 -> x6, starting transfers between devices: 13 us -> 7.74 us  [to_trader(): return lax.ppermute(value, ('core', 'zh'), [(0, 2), (3, 1)])]
    ppermute x5 -> x3, starting transfers between devices: 6.45 us -> 3.45 us  [keepers(): lax.ppermute(value, ('core', 'zh', 'zl'), [(0, 1), (1, 0), (6, 7), (7, 6)])]
    ppermute x4, starting transfers between devices: 16.2 us -> 18.9 us  [swap(): return lax.ppermute(value, ('core', 'zh'), [(0, 0), (1, 2), (2, 1), (3, 3)])]
  transfers between devices with their start and end apart: 28 -> 19, of which waited for: 12 -> 7; matrix products, arithmetic and copies ran while one was open for 4% -> 4% of each run, Pallas kernels for 14% -> 16%
where the time goes in v3:
time: 235 us; the launch traced here: 234 us
  starting transfers between devices  74.1 us (32%)
  waiting for transfers between devices  72.5 us (31%)
  Pallas kernels  41.5 us (18%)
  between operations  14.4 us (6%)
  local copies, waits for them, and re-layouts  12.5 us (5%)
  blocking collectives  9.7 us (4%)
  other arithmetic  9.57 us (4%)
    ppermute x2, waiting for transfers between devices, to_keeper(): return lax.ppermute(value, ('core', 'zh'), [(1, 0), (2, 3)])  42.8 us
    pallas_call x2, Pallas kernels, local(): pl.pallas_call(functools.partial(forward_kernel, k * steps, k == 0, last,...  23.2 us
    ppermute x2, starting transfers between devices, other(): return lax.ppermute(value, axes, [(i, last - i) for i in range(last + 1)])  22.8 us
    ppermute x4, starting transfers between devices, swap(): return lax.ppermute(value, ('core', 'zh'), [(0, 0), (1, 2), (2, 1), (3, 3)])  18.9 us
    all_to_all x1, starting transfers between devices, local(): lax.all_to_all(results[4], ('xy', 'zh'), split_axis=0, concat_axis=0, til...  15.1 us
    ppermute x6, waiting for transfers between devices, to_trader(): return lax.ppermute(value, ('core', 'zh'), [(0, 2), (3, 1)])  14.8 us
    pallas_call x4, Pallas kernels, local(): pl.pallas_call(functools.partial(backward_kernel, k * steps, k == TURNS -...  12.8 us
    ppermute x4, waiting for transfers between devices, swap(): return lax.ppermute(value, ('core', 'zh'), [(0, 0), (1, 2), (2, 1), (3, 3)])  11.5 us
  transfers between devices with their start and end apart: 19, of which 7 were waited for; matrix products, arithmetic and copies ran while one was open for 4% of the time, Pallas kernels for 16%

profile of v3, /device:TPU:1, one launch (start us, length us, event | category | flops | bytes accessed | tf_op | source)
XLA Modules:
  0.0 234.2 jit_solution(16686773732105569390)
XLA Ops:
  7.2 0.8 convert_bitcast_fusion
  8.0 1.4 select_maximum_fusion
  9.4 5.6 %collective-permute-start = (f32[2120,128]{1,0:T(8,128)S(1)}, f32[2120,128]{1,0:T(8,128)S(1)}, u32[]{:S(2)}, u32[]{:S(2)}) collective-permute-start(f32[2120,128]{1,0:T(8,128)S(1)} %select_maximum_fusion), channel_id=1, source_target_pairs={{0,0},{2,4},{4,2},{6,6},{1,1},{3,5},{5,3},{7,7},{8,8},{10,12},{12,... | collective-permute-start | bytes 3256328 | tf_op jit(solution)/shard_map/ppermute | solution.py:189
  15.1 0.7 slice_bitcast_fusion
  15.8 1.0 fusion.2
  16.9 1.4 collective-permute-start.4
  18.3 1.6 pad_maximum_fusion.refs_1_
  19.9 2.0 collective-permute-start.1
  21.9 34.1 %collective-permute-done.4.refs_3_ = f32[16,4,32,128]{3,2,1,0:T(8,128)S(1)} collective-permute-done((f32[16,4,32,128]{3,2,1,0:T(8,128)S(1)}, f32[16,4,32,128]{3,2,1,0:T(8,128)S(1)}, u32[]{:S(2)}, u32[]{:S(2)}) %collective-permute-start.4) | collective-permute-done | bytes 1048608 | tf_op jit(solution)/shard_map/ppermute | solution.py:192
  56.0 0.7 collective-permute-start.5
  58.8 20.6 %collective-permute-start.12 = (f32[4,32,128]{2,1,0:T(8,128)S(1)}, f32[4,32,128]{2,1,0:T(8,128)S(1)}, u32[]{:S(2)}, u32[]{:S(2)}) collective-permute-start(f32[4,32,128]{2,1,0:T(8,128)S(1)} %pad_maximum_fusion.7), channel_id=1, source_target_pairs={{0,2},{2,0},{1,3},{3,1},{4,6},{6,4},{5,7},{7,5},{8,10},{10,8},{9,1... | collective-permute-start | bytes 196616 | tf_op jit(solution)/shard_map/ppermute | solution.py:202
  79.4 1.7 collective-permute-done.12
  81.1 2.2 collective-permute-start.13
  83.3 2.3 pad_maximum_fusion.1
  85.6 4.8 %collective-permute-start.2 = (f32[16,4,32,128]{3,2,1,0:T(8,128)}, f32[16,4,32,128]{3,2,1,0:T(8,128)S(1)}, u32[]{:S(2)}, u32[]{:S(2)}) collective-permute-start(f32[16,4,32,128]{3,2,1,0:T(8,128)} %pad_maximum_fusion.1), channel_id=1, source_target_pairs={{2,0},{4,6},{3,1},{5,7},{10,8},{12,14},{11,9},{13,15},{18,16},{20,... | collective-permute-start | bytes 3145736 | tf_op jit(solution)/shard_map/ppermute | solution.py:192
  90.4 0.7 pad_maximum_fusion.5
  91.1 1.3 collective-permute-start.6
  92.4 1.3 collective-permute-start.7
  93.7 8.6 %collective-permute-done.2.refs_3_ = f32[16,4,32,128]{3,2,1,0:T(8,128)S(1)} collective-permute-done((f32[16,4,32,128]{3,2,1,0:T(8,128)}, f32[16,4,32,128]{3,2,1,0:T(8,128)S(1)}, u32[]{:S(2)}, u32[]{:S(2)}) %collective-permute-start.2) | collective-permute-done | bytes 1048608 | tf_op jit(solution)/shard_map/ppermute | solution.py:192
  103.1 1.3 collective-permute-start.10
  104.4 1.3 collective-permute-start.11
  105.7 1.3 collective-permute-start.8
  107.0 14.8 %collective-permute-done.10.refs_7_ = f32[16,4,32,128]{3,2,1,0:T(8,128)S(1)} collective-permute-done((f32[16,4,32,128]{3,2,1,0:T(8,128)}, f32[16,4,32,128]{3,2,1,0:T(8,128)S(1)}, u32[]{:S(2)}, u32[]{:S(2)}) %collective-permute-start.10) | collective-permute-done | bytes 1048608 | tf_op jit(solution)/shard_map/ppermute | solution.py:195
  121.8 1.0 copy-done.8
  122.7 1.3 collective-permute-start.9
  125.1 1.2 copy-done.5
  126.3 1.2 copy-done.7
  127.5 1.2 copy-done.9
  128.7 11.5 %leaf_forward.2 = (f32[40,64,128]{2,1,0:T(8,128)}, bf16[16,384,128]{2,1,0:T(8,128)(2,1)}, bf16[16,384,128]{2,1,0:T(8,128)(2,1)}, f32[16,64,128]{2,1,0:T(8,128)S(1)}) custom-call(s32[105]{0:T(128)S(1)} %concatenate.31.refs_0_.meta, f32[32,4,32,128]{3,2,1,0:T(8,128)} %pad_maximum_fusion.refs_1_, f32[32,4,32,128]{3,2,1,0:T(8,128)} %collective-permute-done.1.refs_2_, ...), custom_call_target="tpu_custom_call" | custom-call | flops 4000000000 | bytes 8388608 | tf_op jit(solution)/shard_map/leaf_forward/pallas_call | solution.py:246
  140.3 11.7 %leaf_forward.3 = (f32[40,64,128]{2,1,0:T(8,128)}, bf16[16,384,128]{2,1,0:T(8,128)(2,1)}, bf16[16,384,128]{2,1,0:T(8,128)(2,1)}, f32[16,64,128]{2,1,0:T(8,128)S(1)}, f32[8,5,8,128]{3,2,1,0:T(8,128)}) custom-call(s32[105]{0:T(128)S(1)} %concatenate.31.refs_0_.meta, f32[32,4,32,128]{3,2,1,0:T(8,128)} %pad_maximum_fusion.refs_1_, ...), custom_call_target="tpu_custom_call" | custom-call | flops 4000000000 | bytes 8388608 | tf_op jit(solution)/shard_map/leaf_forward/pallas_call | solution.py:246
  152.0 0.8 copy-done.10
  152.7 15.1 %all-to-all-start = ((f32[8,5,8,128]{3,2,1,0:T(8,128)}), f32[8,5,8,128]{3,2,1,0:T(8,128)S(1)}, u32[]{:S(2)}, u32[]{:S(2)}) async-start(f32[8,5,8,128]{3,2,1,0:T(8,128)} %get-tuple-element.46), calls=%async_computation | async-start | bytes 327680 | tf_op jit(solution)/shard_map/all_to_all | solution.py:276
  167.9 1.6 copy-done.1
  169.5 2.8 %top_prepare.1 = (bf16[8,384,128]{2,1,0:T(8,128)(2,1)S(1)}, bf16[8,384,128]{2,1,0:T(8,128)(2,1)S(1)}, bf16[8,128,128]{2,1,0:T(8,128)(2,1)S(1)}, bf16[8,128,128]{2,1,0:T(8,128)(2,1)S(1)}) custom-call(s32[4]{0:T(128)S(1)} %pad_add_fusion.meta, f32[8,4,4,32,128]{4,3,2,1,0:T(8,128)S(1)} %bitcast.31), custom_call_target="tpu_custom_call" | custom-call | tf_op jit(solution)/shard_map/top_prepare/pallas_call | solution.py:264
  172.3 1.8 all-to-all-done.incoming
  174.0 2.7 %top_solve.1 = f32[8,5,8,128]{3,2,1,0:T(8,128)S(1)} custom-call(f32[8,5,8,128]{3,2,1,0:T(8,128)S(1)} %all-to-all-done.incoming, bf16[8,384,128]{2,1,0:T(8,128)(2,1)S(1)} %get-tuple-element.49.high, bf16[8,384,128]{2,1,0:T(8,128)(2,1)S(1)} %get-tuple-element.50.low, bf16[8,128,128]{2,1,0:T(8,128)(2,1)S(1)} %get-tuple-element.51.inverse_high, ...), custom_call_target="tpu_custom_call" | custom-call | tf_op jit(solution)/shard_map/top_solve/pallas_call | solution.py:277
  176.7 9.7 %all_to_all.10.state = f32[8,5,8,128]{3,2,1,0:T(8,128)S(1)} all-to-all(f32[8,5,8,128]{3,2,1,0:T(8,128)S(1)} %top_solve.1), channel_id=1, replica_groups=mesh['xy'=4,'core'=2,'zh'=2,'zl'=2] {'xy','zh'}, dimensions={0} | all-to-all | bytes 327680 | tf_op jit(solution)/shard_map/all_to_all | solution.py:285
  186.5 1.4 copy-done.3
  187.9 2.4 %leaf_backward.4 = (f32[8,64,128]{2,1,0:T(8,128)S(1)}, f32[40,64,128]{2,1,0:T(8,128)S(1)}) custom-call(s32[105]{0:T(128)S(1)} %concatenate.31.refs_0_.meta, bf16[16,384,128]{2,1,0:T(8,128)(2,1)S(1)} %copy-done.2, bf16[16,384,128]{2,1,0:T(8,128)(2,1)S(1)} %copy-done.3, f32[16,64,128]{2,1,0:T(8,128)S(1)} %copy-done.11, f32[8,5,8,128]{3,2,1,0:T(8,128)S(1)} %all_to_all.10.state), custom_call_target="tpu_custom_call" | custom-call | flops 4000000000 | bytes 8388608 | tf_op jit(solution)/shard_map/leaf_backward/pallas_call | solution.py:297
  190.3 6.8 %collective-permute-start.14 = (f32[8,64,128]{2,1,0:T(8,128)S(1)}, f32[8,64,128]{2,1,0:T(8,128)S(1)}, u32[]{:S(2)}, u32[]{:S(2)}) collective-permute-start(f32[8,64,128]{2,1,0:T(8,128)S(1)} %get-tuple-element.53), channel_id=1, source_target_pairs={{0,0},{2,4},{4,2},{6,6},{1,1},{3,5},{5,3},{7,7},{8,8},{10,12},{12,... | collective-permute-start | bytes 786440 | tf_op jit(solution)/shard_map/ppermute | solution.py:189
  197.2 3.2 %leaf_backward.5 = (f32[8,64,128]{2,1,0:T(8,128)S(1)}, f32[40,64,128]{2,1,0:T(8,128)S(1)}) custom-call(s32[105]{0:T(128)S(1)} %concatenate.31.refs_0_.meta, bf16[16,384,128]{2,1,0:T(8,128)(2,1)S(1)} %copy-done.2, bf16[16,384,128]{2,1,0:T(8,128)(2,1)} %get-tuple-element.44.low, f32[16,64,128]{2,1,0:T(8,128)S(1)} %copy-done.11, ...), custom_call_target="tpu_custom_call" | custom-call | flops 4000000000 | bytes 8388608 | tf_op jit(solution)/shard_map/leaf_backward/pallas_call | solution.py:297
  200.4 3.0 %leaf_backward.6 = (f32[8,64,128]{2,1,0:T(8,128)S(1)}, f32[40,64,128]{2,1,0:T(8,128)S(1)}) custom-call(s32[105]{0:T(128)S(1)} %concatenate.31.refs_0_.meta, bf16[16,384,128]{2,1,0:T(8,128)(2,1)S(1)} %copy-done.12, bf16[16,384,128]{2,1,0:T(8,128)(2,1)} %get-tuple-element.55.low, f32[16,64,128]{2,1,0:T(8,128)S(1)} %copy-done.14, ...), custom_call_target="tpu_custom_call" | custom-call | flops 4000000000 | bytes 8388608 | tf_op jit(solution)/shard_map/leaf_backward/pallas_call | solution.py:297
  203.5 1.9 collective-permute-start.16
  205.4 4.2 %leaf_backward.7 = (f32[8,64,128]{2,1,0:T(8,128)S(1)}, f32[40,64,128]{2,1,0:T(8,128)}) custom-call(s32[105]{0:T(128)S(1)} %concatenate.31.refs_0_.meta, bf16[16,384,128]{2,1,0:T(8,128)(2,1)S(1)} %copy-done.12, bf16[16,384,128]{2,1,0:T(8,128)(2,1)} %get-tuple-element.55.low, f32[16,64,128]{2,1,0:T(8,128)S(1)} %copy-done.14, ...), custom_call_target="tpu_custom_call" | custom-call | flops 4000000000 | bytes 8388608 | tf_op jit(solution)/shard_map/leaf_backward/pallas_call | solution.py:297
  209.6 4.5 %collective-permute-start.15 = (f32[8,64,128]{2,1,0:T(8,128)S(1)}, f32[8,64,128]{2,1,0:T(8,128)S(1)}, u32[]{:S(2)}, u32[]{:S(2)}) collective-permute-start(f32[8,64,128]{2,1,0:T(8,128)S(1)} %get-tuple-element.61), channel_id=1, source_target_pairs={{0,0},{2,4},{4,2},{6,6},{1,1},{3,5},{5,3},{7,7},{8,8},{10,12},{12,... | collective-permute-start | bytes 786440 | tf_op jit(solution)/shard_map/ppermute | solution.py:189
  214.1 9.4 %collective-permute-done.16 = f32[17,64,128]{2,1,0:T(8,128)S(1)} collective-permute-done((f32[17,64,128]{2,1,0:T(8,128)S(1)}, f32[17,64,128]{2,1,0:T(8,128)S(1)}, u32[]{:S(2)}, u32[]{:S(2)}) %collective-permute-start.16) | collective-permute-done | bytes 557088 | tf_op jit(solution)/shard_map/ppermute | solution.py:189
  224.1 2.1 collective-permute-done.15
  226.3 1.1 pad_maximum_fusion.3
  (62 shorter events, 4.8 us)
Async XLA Ops:
  7.2 50.3 %copy-start = (f32[8,1,32,128]{3,2,1,0:T(8,128)S(1)}, f32[8,1,32,128]{3,2,1,0:T(8,128)}, u32[]{:S(2)}) copy-start(f32[8,1,32,128]{3,2,1,0:T(8,128)} %param.16) | copy-start | bytes 393220
  7.2 7.9 %copy-start.16 = (f32[32,32,128]{2,1,0:T(8,128)S(1)}, f32[32,32,128]{2,1,0:T(8,128)}, u32[]{:S(2)}) copy-start(f32[32,32,128]{2,1,0:T(8,128)} %param.14) | copy-start | bytes 1572868
  7.2 160.7 %all-gather.3.cloned.1.call-start = ((), (), s32[]{:S(2)}) async-start(), calls=%async_computation.2 | async-start | bytes 2359296 | tf_op jit(solution)/shard_map/all_gather | solution.py:224
  8.0 7.8 %copy-start.15 = (f32[32,3,32,128]{3,2,1,0:T(8,128)S(1)}, f32[32,3,32,128]{3,2,1,0:T(8,128)}, u32[]{:S(2)}) copy-start(f32[32,3,32,128]{3,2,1,0:T(8,128)} %param.13) | copy-start | bytes 4718596
  9.4 46.6 %collective-permute-start = (f32[2120,128]{1,0:T(8,128)S(1)}, f32[2120,128]{1,0:T(8,128)S(1)}, u32[]{:S(2)}, u32[]{:S(2)}) collective-permute-start(f32[2120,128]{1,0:T(8,128)S(1)} %select_maximum_fusion), channel_id=1, source_target_pairs={{0,0},{2,4},{4,2},{6,6},{1,1},{3,5},{5,3},{7,7},{8,8},{10,12},{12,... | collective-permute-start | bytes 3256328 | tf_op jit(solution)/shard_map/ppermute | solution.py:189
  16.9 39.1 %collective-permute-start.4 = (f32[16,4,32,128]{3,2,1,0:T(8,128)S(1)}, f32[16,4,32,128]{3,2,1,0:T(8,128)S(1)}, u32[]{:S(2)}, u32[]{:S(2)}) collective-permute-start(f32[16,4,32,128]{3,2,1,0:T(8,128)S(1)} %pad_maximum_fusion.2), channel_id=1, source_target_pairs={{2,0},{4,6},{3,1},{5,7},{10,8},{12,14},{11,9},{13,15},{18,16},{20,... | collective-permute-start | bytes 3145736 | tf_op jit(solution)/shard_map/ppermute | solution.py:192
  18.3 40.5 %copy-start.17 = (f32[1,32,128]{2,1,0:T(8,128)S(1)}, f32[1,32,128]{2,1,0:T(8,128)}, u32[]{:S(2)}) copy-start(f32[1,32,128]{2,1,0:T(8,128)} %param.17) | copy-start | bytes 49156
  19.9 38.9 %collective-permute-start.1 = (f32[32,4,32,128]{3,2,1,0:T(8,128)}, f32[32,4,32,128]{3,2,1,0:T(8,128)}, u32[]{:S(2)}, u32[]{:S(2)}) collective-permute-start(f32[32,4,32,128]{3,2,1,0:T(8,128)} %pad_maximum_fusion.refs_1_), channel_id=1, source_target_pairs={{0,1},{1,0},{6,7},{7,6},{8,9},{9,8},{14,15},{15,14},{16,17},{17,16... | collective-permute-start | bytes 6291464 | tf_op jit(solution)/shard_map/ppermute | solution.py:198
  56.0 27.3 %copy-start.4 = (f32[16,4,32,128]{3,2,1,0:T(8,128)}, f32[16,4,32,128]{3,2,1,0:T(8,128)S(1)}, u32[]{:S(2)}) copy-start(f32[16,4,32,128]{3,2,1,0:T(8,128)S(1)} %collective-permute-done.4.refs_3_) | copy-start | bytes 3145732
  56.0 2.8 %collective-permute-start.5 = (f32[16,4,32,128]{3,2,1,0:T(8,128)S(1)}, f32[16,4,32,128]{3,2,1,0:T(8,128)S(1)}, u32[]{:S(2)}, u32[]{:S(2)}) collective-permute-start(f32[16,4,32,128]{3,2,1,0:T(8,128)S(1)} %collective-permute-done.4.refs_3_), channel_id=1, source_target_pairs={{0,1},{1,0},{6,7},{7,6},{8,9},{9,8},{14,15},{15,14},{16,17},{17,16... | collective-permute-start | bytes 3145736 | tf_op jit(solution)/shard_map/ppermute | solution.py:198
  58.8 32.3 %copy-start.6 = (f32[16,4,32,128]{3,2,1,0:T(8,128)}, f32[16,4,32,128]{3,2,1,0:T(8,128)S(1)}, u32[]{:S(2)}) copy-start(f32[16,4,32,128]{3,2,1,0:T(8,128)S(1)} %collective-permute-done.5.refs_4_) | copy-start | bytes 3145732
  58.8 22.3 %collective-permute-start.12 = (f32[4,32,128]{2,1,0:T(8,128)S(1)}, f32[4,32,128]{2,1,0:T(8,128)S(1)}, u32[]{:S(2)}, u32[]{:S(2)}) collective-permute-start(f32[4,32,128]{2,1,0:T(8,128)S(1)} %pad_maximum_fusion.7), channel_id=1, source_target_pairs={{0,2},{2,0},{1,3},{3,1},{4,6},{6,4},{5,7},{7,5},{8,10},{10,8},{9,1... | collective-permute-start | bytes 196616 | tf_op jit(solution)/shard_map/ppermute | solution.py:202
  81.1 9.2 %collective-permute-start.13 = (f32[2,4,32,128]{3,2,1,0:T(8,128)S(1)}, f32[2,4,32,128]{3,2,1,0:T(8,128)S(1)}, u32[]{:S(2)}, u32[]{:S(2)}) collective-permute-start(f32[2,4,32,128]{3,2,1,0:T(8,128)S(1)} %pad_maximum_fusion.6), channel_id=1, source_target_pairs={{0,1},{1,0},{2,3},{3,2},{4,5},{5,4},{6,7},{7,6},{8,9},{9,8},{10,11... | collective-permute-start | bytes 393224 | tf_op jit(solution)/shard_map/ppermute | solution.py:202
  85.6 16.8 %collective-permute-start.2 = (f32[16,4,32,128]{3,2,1,0:T(8,128)}, f32[16,4,32,128]{3,2,1,0:T(8,128)S(1)}, u32[]{:S(2)}, u32[]{:S(2)}) collective-permute-start(f32[16,4,32,128]{3,2,1,0:T(8,128)} %pad_maximum_fusion.1), channel_id=1, source_target_pairs={{2,0},{4,6},{3,1},{5,7},{10,8},{12,14},{11,9},{13,15},{18,16},{20,... | collective-permute-start | bytes 3145736 | tf_op jit(solution)/shard_map/ppermute | solution.py:192
  91.1 33.9 %collective-permute-start.6 = (f32[32,4,32,128]{3,2,1,0:T(8,128)}, f32[32,4,32,128]{3,2,1,0:T(8,128)}, u32[]{:S(2)}, u32[]{:S(2)}) collective-permute-start(f32[32,4,32,128]{3,2,1,0:T(8,128)} %pad_maximum_fusion.refs_1_), channel_id=1, source_target_pairs={{0,4},{6,2},{1,5},{7,3},{8,12},{14,10},{9,13},{15,11},{16,20},{22,... | collective-permute-start | bytes 6291464 | tf_op jit(solution)/shard_map/ppermute | solution.py:195
  92.4 32.6 %collective-permute-start.7 = (f32[32,4,32,128]{3,2,1,0:T(8,128)}, f32[32,4,32,128]{3,2,1,0:T(8,128)}, u32[]{:S(2)}, u32[]{:S(2)}) collective-permute-start(f32[32,4,32,128]{3,2,1,0:T(8,128)} %collective-permute-done.1.refs_2_), channel_id=1, source_target_pairs={{0,4},{6,2},{1,5},{7,3},{8,12},{14,10},{9,13},{15,11},{16,20},{22,... | collective-permute-start | bytes 6291464 | tf_op jit(solution)/shard_map/ppermute | solution.py:195
  102.4 3.3 %collective-permute-start.3 = (f32[16,4,32,128]{3,2,1,0:T(8,128)S(1)}, f32[16,4,32,128]{3,2,1,0:T(8,128)S(1)}, u32[]{:S(2)}, u32[]{:S(2)}) collective-permute-start(f32[16,4,32,128]{3,2,1,0:T(8,128)S(1)} %collective-permute-done.2.refs_3_), channel_id=1, source_target_pairs={{0,1},{1,0},{6,7},{7,6},{8,9},{9,8},{14,15},{15,14},{16,17},{17,16... | collective-permute-start | bytes 3145736 | tf_op jit(solution)/shard_map/ppermute | solution.py:198
  103.1 18.7 %collective-permute-start.10 = (f32[16,4,32,128]{3,2,1,0:T(8,128)}, f32[16,4,32,128]{3,2,1,0:T(8,128)S(1)}, u32[]{:S(2)}, u32[]{:S(2)}) collective-permute-start(f32[16,4,32,128]{3,2,1,0:T(8,128)} %copy-done.4), channel_id=1, source_target_pairs={{0,4},{6,2},{1,5},{7,3},{8,12},{14,10},{9,13},{15,11},{16,20},{22,... | collective-permute-start | bytes 3145736 | tf_op jit(solution)/shard_map/ppermute | solution.py:195
  104.4 20.6 %collective-permute-start.11 = (f32[16,4,32,128]{3,2,1,0:T(8,128)}, f32[16,4,32,128]{3,2,1,0:T(8,128)}, u32[]{:S(2)}, u32[]{:S(2)}) collective-permute-start(f32[16,4,32,128]{3,2,1,0:T(8,128)} %copy-done.6), channel_id=1, source_target_pairs={{0,4},{6,2},{1,5},{7,3},{8,12},{14,10},{9,13},{15,11},{16,20},{22,... | collective-permute-start | bytes 3145736 | tf_op jit(solution)/shard_map/ppermute | solution.py:195
  105.7 34.6 %collective-permute-start.8 = (f32[16,4,32,128]{3,2,1,0:T(8,128)S(1)}, f32[16,4,32,128]{3,2,1,0:T(8,128)}, u32[]{:S(2)}, u32[]{:S(2)}) collective-permute-start(f32[16,4,32,128]{3,2,1,0:T(8,128)S(1)} %collective-permute-done.2.refs_3_), channel_id=1, source_target_pairs={{0,4},{6,2},{1,5},{7,3},{8,12},{14,10},{9,13},{15,11},{16,20},{22,... | collective-permute-start | bytes 3145736 | tf_op jit(solution)/shard_map/ppermute | solution.py:195
  121.8 1.0 copy-start.8
  122.7 17.5 %collective-permute-start.9 = (f32[16,4,32,128]{3,2,1,0:T(8,128)S(1)}, f32[16,4,32,128]{3,2,1,0:T(8,128)}, u32[]{:S(2)}, u32[]{:S(2)}) collective-permute-start(f32[16,4,32,128]{3,2,1,0:T(8,128)S(1)} %collective-permute-done.3.refs_4_), channel_id=1, source_target_pairs={{0,4},{6,2},{1,5},{7,3},{8,12},{14,10},{9,13},{15,11},{16,20},{22,... | collective-permute-start | bytes 3145736 | tf_op jit(solution)/shard_map/ppermute | solution.py:195
  125.1 1.2 copy-start.5
  126.3 1.2 copy-start.7
  127.5 1.2 copy-start.9
  140.3 11.7 %copy-start.13 = (f32[16,64,128]{2,1,0:T(8,128)}, f32[16,64,128]{2,1,0:T(8,128)S(1)}, u32[]{:S(2)}) copy-start(f32[16,64,128]{2,1,0:T(8,128)S(1)} %get-tuple-element.56.scaled) | copy-start | bytes 1572868
  152.0 0.8 copy-start.10
  152.7 21.3 %all-to-all-start = ((f32[8,5,8,128]{3,2,1,0:T(8,128)}), f32[8,5,8,128]{3,2,1,0:T(8,128)S(1)}, u32[]{:S(2)}, u32[]{:S(2)}) async-start(f32[8,5,8,128]{3,2,1,0:T(8,128)} %get-tuple-element.46), calls=%async_computation | async-start | bytes 327680 | tf_op jit(solution)/shard_map/all_to_all | solution.py:276
  167.9 1.6 copy-start.1
  174.0 12.4 %copy-start.2 = (bf16[16,384,128]{2,1,0:T(8,128)(2,1)S(1)}, bf16[16,384,128]{2,1,0:T(8,128)(2,1)}, u32[]{:S(2)}) copy-start(bf16[16,384,128]{2,1,0:T(8,128)(2,1)} %get-tuple-element.43.high) | copy-start | bytes 4718596
  174.0 12.4 %copy-start.11 = (f32[16,64,128]{2,1,0:T(8,128)S(1)}, f32[16,64,128]{2,1,0:T(8,128)}, u32[]{:S(2)}) copy-start(f32[16,64,128]{2,1,0:T(8,128)} %copy-done.10) | copy-start | bytes 1572868
  186.5 1.4 copy-start.3
  190.3 19.3 %collective-permute-start.14 = (f32[8,64,128]{2,1,0:T(8,128)S(1)}, f32[8,64,128]{2,1,0:T(8,128)S(1)}, u32[]{:S(2)}, u32[]{:S(2)}) collective-permute-start(f32[8,64,128]{2,1,0:T(8,128)S(1)} %get-tuple-element.53), channel_id=1, source_target_pairs={{0,0},{2,4},{4,2},{6,6},{1,1},{3,5},{5,3},{7,7},{8,8},{10,12},{12,... | collective-permute-start | bytes 786440 | tf_op jit(solution)/shard_map/ppermute | solution.py:189
  197.1 3.2 %copy-start.12 = (bf16[16,384,128]{2,1,0:T(8,128)(2,1)S(1)}, bf16[16,384,128]{2,1,0:T(8,128)(2,1)}, u32[]{:S(2)}) copy-start(bf16[16,384,128]{2,1,0:T(8,128)(2,1)} %get-tuple-element.54.high) | copy-start | bytes 4718596
  197.1 3.2 %copy-start.14 = (f32[16,64,128]{2,1,0:T(8,128)S(1)}, f32[16,64,128]{2,1,0:T(8,128)}, u32[]{:S(2)}) copy-start(f32[16,64,128]{2,1,0:T(8,128)} %copy-done.13) | copy-start | bytes 1572868
  203.5 20.0 %collective-permute-start.16 = (f32[17,64,128]{2,1,0:T(8,128)S(1)}, f32[17,64,128]{2,1,0:T(8,128)S(1)}, u32[]{:S(2)}, u32[]{:S(2)}) collective-permute-start(f32[17,64,128]{2,1,0:T(8,128)S(1)} %pad_maximum_fusion.4), channel_id=1, source_target_pairs={{0,0},{2,4},{4,2},{6,6},{1,1},{3,5},{5,3},{7,7},{8,8},{10,12},{12,... | collective-permute-start | bytes 1671176 | tf_op jit(solution)/shard_map/ppermute | solution.py:189
  209.6 16.7 %collective-permute-start.15 = (f32[8,64,128]{2,1,0:T(8,128)S(1)}, f32[8,64,128]{2,1,0:T(8,128)S(1)}, u32[]{:S(2)}, u32[]{:S(2)}) collective-permute-start(f32[8,64,128]{2,1,0:T(8,128)S(1)} %get-tuple-element.61), channel_id=1, source_target_pairs={{0,0},{2,4},{4,2},{6,6},{1,1},{3,5},{5,3},{7,7},{8,8},{10,12},{12,... | collective-permute-start | bytes 786440 | tf_op jit(solution)/shard_map/ppermute | solution.py:189
Sparse Core Ops, SparseCore 0:
  91.3 28.4 all-gather.2

commit v4 on v3

--- a/solution.py
+++ b/solution.py
@@ -217,7 +217,8 @@
     sides = swap(sides)
     far = [to_keeper(part) for part in parts]
     across = [keepers(after(sides, far[0]))] + [keepers(value) for value in far[1:]]
-    top, own_late, near_late = after(across[0], (top, own, near))
+    own_late, near_late = after(across[0], (own, near))
+    top = after(far[-1], top)
     own_passed, near_passed = to_trader(own_late), to_trader(near_late)
     top = jnp.stack([top, other(top, "zh")])
     top = jnp.concatenate([top, other(top, "zl")])

time: 235 us -> 224 us (0.953)
  starting transfers between devices: 74.1 us -> 61.2 us
  waiting for transfers between devices: 72.5 us -> 76 us
  local copies, waits for them, and re-layouts: 12.5 us -> 9.23 us
    ppermute x2, starting transfers between devices: 22.8 us -> 13.2 us  [other(): return lax.ppermute(value, axes, [(i, last - i) for i in range(last + 1)])]
    ppermute x6, waiting for transfers between devices: 14.8 us -> 7.33 us  [to_trader(): return lax.ppermute(value, ('core', 'zh'), [(0, 2), (3, 1)])]
    ppermute x2, waiting for transfers between devices: 1.67 us -> 7.64 us  [other(): return lax.ppermute(value, axes, [(i, last - i) for i in range(last + 1)])]
    ppermute x4, starting transfers between devices: 18.9 us -> 14.1 us  [swap(): return lax.ppermute(value, ('core', 'zh'), [(0, 0), (1, 2), (2, 1), (3, 3)])]
    ppermute x2, waiting for transfers between devices: 42.8 us -> 46.9 us  [to_keeper(): return lax.ppermute(value, ('core', 'zh'), [(1, 0), (2, 3)])]
    all_to_all x1, starting transfers between devices: 15.1 us -> 17.7 us  [local(): lax.all_to_all(results[4], ('xy', 'zh'), split_axis=0, concat_axis=0, til...]
    unnamed x36 -> x28, local copies, waits for them, and re-layouts: 8.49 us -> 6.87 us
  transfers between devices with their start and end apart: 19 -> 19, of which waited for: 7 -> 9; matrix products, arithmetic and copies ran while one was open for 4% -> 3% of each run, Pallas kernels for 16% -> 15%
where the time goes in v4:
time: 224 us; the launch traced here: 223 us
  waiting for transfers between devices  76 us (34%)
  starting transfers between devices  61.2 us (27%)
  Pallas kernels  41.9 us (19%)
  between operations  14.4 us (6%)
  blocking collectives  11.3 us (5%)
  local copies, waits for them, and re-layouts  9.23 us (4%)
  other arithmetic  9.21 us (4%)
    ppermute x2, waiting for transfers between devices, to_keeper(): return lax.ppermute(value, ('core', 'zh'), [(1, 0), (2, 3)])  46.9 us
    pallas_call x2, Pallas kernels, local(): pl.pallas_call(functools.partial(forward_kernel, k * steps, k == 0, last,...  23.6 us
    all_to_all x1, starting transfers between devices, local(): lax.all_to_all(results[4], ('xy', 'zh'), split_axis=0, concat_axis=0, til...  17.7 us
    ppermute x4, starting transfers between devices, swap(): return lax.ppermute(value, ('core', 'zh'), [(0, 0), (1, 2), (2, 1), (3, 3)])  14.1 us
    ppermute x2, starting transfers between devices, other(): return lax.ppermute(value, axes, [(i, last - i) for i in range(last + 1)])  13.2 us
    pallas_call x4, Pallas kernels, local(): pl.pallas_call(functools.partial(backward_kernel, k * steps, k == TURNS -...  12.8 us
    ppermute x4, waiting for transfers between devices, swap(): return lax.ppermute(value, ('core', 'zh'), [(0, 0), (1, 2), (2, 1), (3, 3)])  12.1 us
    all_to_all x1, blocking collectives, local(): lax.all_to_all(outgoing, ('xy', 'zh'), split_axis=0, concat_axis=0, tiled...  11.3 us
  transfers between devices with their start and end apart: 19, of which 9 were waited for; matrix products, arithmetic and copies ran while one was open for 3% of the time, Pallas kernels for 15%

profile of v4, /device:TPU:1, one launch (start us, length us, event | category | flops | bytes accessed | tf_op | source)
XLA Modules:
  0.0 223.1 jit_solution(317566209968174105)
XLA Ops:
  7.2 0.8 convert_bitcast_fusion
  8.0 2.3 %select_maximum_fusion = f32[2120,128]{1,0:T(8,128)} fusion(f32[3,32]{1,0:T(4,128)S(1)} %convert_bitcast_fusion, f32[64,128]{1,0:T(8,128)} %bitcast.38, f32[2048,128]{1,0:T(8,128)} %bitcast.33), kind=kLoop, calls=%fused_computation.2 | loop fusion | flops 1085440 | bytes 2167168 | tf_op jit(solution)/shard_map/concatenate | solution.py:210
  10.4 5.7 %collective-permute-start = (f32[2120,128]{1,0:T(8,128)}, f32[2120,128]{1,0:T(8,128)S(1)}, u32[]{:S(2)}, u32[]{:S(2)}) collective-permute-start(f32[2120,128]{1,0:T(8,128)} %select_maximum_fusion), channel_id=1, source_target_pairs={{0,0},{2,4},{4,2},{6,6},{1,1},{3,5},{5,3},{7,7},{8,8},{10,12},{12,... | collective-permute-start | bytes 3256328 | tf_op jit(solution)/shard_map/ppermute | solution.py:189
  16.3 1.1 pad_maximum_fusion.2
  17.4 2.3 %collective-permute-start.4 = (f32[16,4,32,128]{3,2,1,0:T(8,128)}, f32[16,4,32,128]{3,2,1,0:T(8,128)}, u32[]{:S(2)}, u32[]{:S(2)}) collective-permute-start(f32[16,4,32,128]{3,2,1,0:T(8,128)} %pad_maximum_fusion.2), channel_id=1, source_target_pairs={{2,0},{4,6},{3,1},{5,7},{10,8},{12,14},{11,9},{13,15},{18,16},{20,... | collective-permute-start | bytes 3145736 | tf_op jit(solution)/shard_map/ppermute | solution.py:192
  19.7 1.5 pad_maximum_fusion.refs_1_
  21.2 2.2 collective-permute-start.1
  23.4 1.5 collective-permute-start.2
  27.0 30.0 %collective-permute-done.4.refs_3_ = f32[16,4,32,128]{3,2,1,0:T(8,128)} collective-permute-done((f32[16,4,32,128]{3,2,1,0:T(8,128)}, f32[16,4,32,128]{3,2,1,0:T(8,128)}, u32[]{:S(2)}, u32[]{:S(2)}) %collective-permute-start.4) | collective-permute-done | bytes 1048608 | tf_op jit(solution)/shard_map/ppermute | solution.py:192
  57.0 1.6 collective-permute-start.5
  58.7 16.9 %collective-permute-done.2.refs_3_ = f32[16,4,32,128]{3,2,1,0:T(8,128)S(1)} collective-permute-done((f32[16,4,32,128]{3,2,1,0:T(8,128)S(1)}, f32[16,4,32,128]{3,2,1,0:T(8,128)S(1)}, u32[]{:S(2)}, u32[]{:S(2)}) %collective-permute-start.2) | collective-permute-done | bytes 1048608 | tf_op jit(solution)/shard_map/ppermute | solution.py:192
  75.6 2.8 %collective-permute-start.12 = (f32[4,32,128]{2,1,0:T(8,128)S(1)}, f32[4,32,128]{2,1,0:T(8,128)S(1)}, u32[]{:S(2)}, u32[]{:S(2)}) collective-permute-start(f32[4,32,128]{2,1,0:T(8,128)S(1)} %pad_maximum_fusion.7), channel_id=1, source_target_pairs={{0,2},{2,0},{1,3},{3,1},{4,6},{6,4},{5,7},{7,5},{8,10},{10,8},{9,1... | collective-permute-start | bytes 196616 | tf_op jit(solution)/shard_map/ppermute | solution.py:202
  78.4 3.4 %collective-permute-done.12 = f32[4,32,128]{2,1,0:T(8,128)S(1)} collective-permute-done((f32[4,32,128]{2,1,0:T(8,128)S(1)}, f32[4,32,128]{2,1,0:T(8,128)S(1)}, u32[]{:S(2)}, u32[]{:S(2)}) %collective-permute-start.12) | collective-permute-done | bytes 65568 | tf_op jit(solution)/shard_map/ppermute | solution.py:202
  81.8 10.4 %collective-permute-start.13 = (f32[2,4,32,128]{3,2,1,0:T(8,128)S(1)}, f32[2,4,32,128]{3,2,1,0:T(8,128)S(1)}, u32[]{:S(2)}, u32[]{:S(2)}) collective-permute-start(f32[2,4,32,128]{3,2,1,0:T(8,128)S(1)} %pad_maximum_fusion.6), channel_id=1, source_target_pairs={{0,1},{1,0},{2,3},{3,2},{4,5},{5,4},{6,7},{7,6},{8,9},{9,8},{10,11... | collective-permute-start | bytes 393224 | tf_op jit(solution)/shard_map/ppermute | solution.py:202
  92.2 4.2 %collective-permute-done.13 = f32[2,4,32,128]{3,2,1,0:T(8,128)S(1)} collective-permute-done((f32[2,4,32,128]{3,2,1,0:T(8,128)S(1)}, f32[2,4,32,128]{3,2,1,0:T(8,128)S(1)}, u32[]{:S(2)}, u32[]{:S(2)}) %collective-permute-start.13) | collective-permute-done | bytes 131104 | tf_op jit(solution)/shard_map/ppermute | solution.py:202
  96.5 0.7 pad_maximum_fusion.5
  97.2 1.3 collective-permute-start.6
  98.5 1.3 collective-permute-start.7
  99.8 1.3 collective-permute-start.10
  101.1 0.7 collective-permute-start.3
  101.9 1.3 collective-permute-start.11
  103.2 7.3 %collective-permute-done.10.refs_7_ = f32[16,4,32,128]{3,2,1,0:T(8,128)S(1)} collective-permute-done((f32[16,4,32,128]{3,2,1,0:T(8,128)}, f32[16,4,32,128]{3,2,1,0:T(8,128)S(1)}, u32[]{:S(2)}, u32[]{:S(2)}) %collective-permute-start.10) | collective-permute-done | bytes 1048608 | tf_op jit(solution)/shard_map/ppermute | solution.py:195
  110.5 1.0 copy-done.4
  111.5 1.3 collective-permute-start.8
  112.8 1.3 collective-permute-start.9
  115.1 1.2 copy-done.5
  116.3 12.1 %leaf_forward.2 = (f32[40,64,128]{2,1,0:T(8,128)}, bf16[16,384,128]{2,1,0:T(8,128)(2,1)}, bf16[16,384,128]{2,1,0:T(8,128)(2,1)}, f32[16,64,128]{2,1,0:T(8,128)S(1)}) custom-call(s32[105]{0:T(128)S(1)} %concatenate.31.refs_0_.meta, f32[32,4,32,128]{3,2,1,0:T(8,128)} %pad_maximum_fusion.refs_1_, f32[32,4,32,128]{3,2,1,0:T(8,128)} %collective-permute-done.1.refs_2_, ...), custom_call_target="tpu_custom_call" | custom-call | flops 4000000000 | bytes 8388608 | tf_op jit(solution)/shard_map/leaf_forward/pallas_call | solution.py:247
  128.4 0.8 copy-done.9
  129.3 11.5 %leaf_forward.3 = (f32[40,64,128]{2,1,0:T(8,128)}, bf16[16,384,128]{2,1,0:T(8,128)(2,1)}, bf16[16,384,128]{2,1,0:T(8,128)(2,1)}, f32[16,64,128]{2,1,0:T(8,128)S(1)}, f32[8,5,8,128]{3,2,1,0:T(8,128)}) custom-call(s32[105]{0:T(128)S(1)} %concatenate.31.refs_0_.meta, f32[32,4,32,128]{3,2,1,0:T(8,128)} %pad_maximum_fusion.refs_1_, ...), custom_call_target="tpu_custom_call" | custom-call | flops 4000000000 | bytes 8388608 | tf_op jit(solution)/shard_map/leaf_forward/pallas_call | solution.py:247
  140.8 0.8 copy-done.6
  141.6 17.7 %all-to-all-start = ((f32[8,5,8,128]{3,2,1,0:T(8,128)}), f32[8,5,8,128]{3,2,1,0:T(8,128)S(1)}, u32[]{:S(2)}, u32[]{:S(2)}) async-start(f32[8,5,8,128]{3,2,1,0:T(8,128)} %get-tuple-element.46), calls=%async_computation | async-start | bytes 327680 | tf_op jit(solution)/shard_map/all_to_all | solution.py:277
  159.3 1.6 copy-done.1
  160.9 2.8 %top_prepare.1 = (bf16[8,384,128]{2,1,0:T(8,128)(2,1)S(1)}, bf16[8,384,128]{2,1,0:T(8,128)(2,1)S(1)}, bf16[8,128,128]{2,1,0:T(8,128)(2,1)S(1)}, bf16[8,128,128]{2,1,0:T(8,128)(2,1)S(1)}) custom-call(s32[4]{0:T(128)S(1)} %pad_add_fusion.meta, f32[8,4,4,32,128]{4,3,2,1,0:T(8,128)S(1)} %bitcast.31), custom_call_target="tpu_custom_call" | custom-call | tf_op jit(solution)/shard_map/top_prepare/pallas_call | solution.py:265
  163.7 1.9 all-to-all-done.incoming
  165.6 2.7 %top_solve.1 = f32[8,5,8,128]{3,2,1,0:T(8,128)S(1)} custom-call(f32[8,5,8,128]{3,2,1,0:T(8,128)S(1)} %all-to-all-done.incoming, bf16[8,384,128]{2,1,0:T(8,128)(2,1)S(1)} %get-tuple-element.49.high, bf16[8,384,128]{2,1,0:T(8,128)(2,1)S(1)} %get-tuple-element.50.low, bf16[8,128,128]{2,1,0:T(8,128)(2,1)S(1)} %get-tuple-element.51.inverse_high, ...), custom_call_target="tpu_custom_call" | custom-call | tf_op jit(solution)/shard_map/top_solve/pallas_call | solution.py:278
  168.4 11.3 %all_to_all.10.state = f32[8,5,8,128]{3,2,1,0:T(8,128)S(1)} all-to-all(f32[8,5,8,128]{3,2,1,0:T(8,128)S(1)} %top_solve.1), channel_id=1, replica_groups=mesh['xy'=4,'core'=2,'zh'=2,'zl'=2] {'xy','zh'}, dimensions={0} | all-to-all | bytes 327680 | tf_op jit(solution)/shard_map/all_to_all | solution.py:286
  179.7 1.4 copy-done.3
  181.1 2.4 %leaf_backward.4 = (f32[8,64,128]{2,1,0:T(8,128)S(1)}, f32[40,64,128]{2,1,0:T(8,128)S(1)}) custom-call(s32[105]{0:T(128)S(1)} %concatenate.31.refs_0_.meta, bf16[16,384,128]{2,1,0:T(8,128)(2,1)S(1)} %copy-done.2, bf16[16,384,128]{2,1,0:T(8,128)(2,1)S(1)} %copy-done.3, f32[16,64,128]{2,1,0:T(8,128)S(1)} %copy-done.7, f32[8,5,8,128]{3,2,1,0:T(8,128)S(1)} %all_to_all.10.state), custom_call_target="tpu_custom_call" | custom-call | flops 4000000000 | bytes 8388608 | tf_op jit(solution)/shard_map/leaf_backward/pallas_call | solution.py:298
  183.5 3.2 %leaf_backward.5 = (f32[8,64,128]{2,1,0:T(8,128)S(1)}, f32[40,64,128]{2,1,0:T(8,128)S(1)}) custom-call(s32[105]{0:T(128)S(1)} %concatenate.31.refs_0_.meta, bf16[16,384,128]{2,1,0:T(8,128)(2,1)S(1)} %copy-done.2, bf16[16,384,128]{2,1,0:T(8,128)(2,1)} %get-tuple-element.44.low, f32[16,64,128]{2,1,0:T(8,128)S(1)} %copy-done.7, ...), custom_call_target="tpu_custom_call" | custom-call | flops 4000000000 | bytes 8388608 | tf_op jit(solution)/shard_map/leaf_backward/pallas_call | solution.py:298
  186.7 1.9 collective-permute-start.14
  188.7 3.0 %leaf_backward.6 = (f32[8,64,128]{2,1,0:T(8,128)S(1)}, f32[40,64,128]{2,1,0:T(8,128)S(1)}) custom-call(s32[105]{0:T(128)S(1)} %concatenate.31.refs_0_.meta, bf16[16,384,128]{2,1,0:T(8,128)(2,1)S(1)} %copy-done.8, bf16[16,384,128]{2,1,0:T(8,128)(2,1)} %get-tuple-element.55.low, f32[16,64,128]{2,1,0:T(8,128)S(1)} %copy-done.10, ...), custom_call_target="tpu_custom_call" | custom-call | flops 4000000000 | bytes 8388608 | tf_op jit(solution)/shard_map/leaf_backward/pallas_call | solution.py:298
  191.8 4.5 %collective-permute-start.16 = (f32[17,64,128]{2,1,0:T(8,128)S(1)}, f32[17,64,128]{2,1,0:T(8,128)S(1)}, u32[]{:S(2)}, u32[]{:S(2)}) collective-permute-start(f32[17,64,128]{2,1,0:T(8,128)S(1)} %pad_maximum_fusion.4), channel_id=1, source_target_pairs={{0,0},{2,4},{4,2},{6,6},{1,1},{3,5},{5,3},{7,7},{8,8},{10,12},{12,... | collective-permute-start | bytes 1671176 | tf_op jit(solution)/shard_map/ppermute | solution.py:189
  196.3 4.1 %leaf_backward.7 = (f32[8,64,128]{2,1,0:T(8,128)S(1)}, f32[40,64,128]{2,1,0:T(8,128)}) custom-call(s32[105]{0:T(128)S(1)} %concatenate.31.refs_0_.meta, bf16[16,384,128]{2,1,0:T(8,128)(2,1)S(1)} %copy-done.8, bf16[16,384,128]{2,1,0:T(8,128)(2,1)} %get-tuple-element.55.low, f32[16,64,128]{2,1,0:T(8,128)S(1)} %copy-done.10, ...), custom_call_target="tpu_custom_call" | custom-call | flops 4000000000 | bytes 8388608 | tf_op jit(solution)/shard_map/leaf_backward/pallas_call | solution.py:298
  200.5 3.1 %collective-permute-done.14 = f32[8,64,128]{2,1,0:T(8,128)S(1)} collective-permute-done((f32[8,64,128]{2,1,0:T(8,128)S(1)}, f32[8,64,128]{2,1,0:T(8,128)S(1)}, u32[]{:S(2)}, u32[]{:S(2)}) %collective-permute-start.14) | collective-permute-done | bytes 262176 | tf_op jit(solution)/shard_map/ppermute | solution.py:189
  203.6 1.9 collective-permute-start.15
  205.5 6.9 %collective-permute-done.16 = f32[17,64,128]{2,1,0:T(8,128)S(1)} collective-permute-done((f32[17,64,128]{2,1,0:T(8,128)S(1)}, f32[17,64,128]{2,1,0:T(8,128)S(1)}, u32[]{:S(2)}, u32[]{:S(2)}) %collective-permute-start.16) | collective-permute-done | bytes 557088 | tf_op jit(solution)/shard_map/ppermute | solution.py:189
  213.0 2.1 collective-permute-done.15
  215.2 1.1 pad_maximum_fusion.3
  (54 shorter events, 4.2 us)
Async XLA Ops:
  7.2 18.5 %copy-start = (f32[8,1,32,128]{3,2,1,0:T(8,128)S(1)}, f32[8,1,32,128]{3,2,1,0:T(8,128)}, u32[]{:S(2)}) copy-start(f32[8,1,32,128]{3,2,1,0:T(8,128)} %param.16) | copy-start | bytes 393220
  7.2 8.9 %copy-start.11 = (f32[32,3,32,128]{3,2,1,0:T(8,128)S(1)}, f32[32,3,32,128]{3,2,1,0:T(8,128)}, u32[]{:S(2)}) copy-start(f32[32,3,32,128]{3,2,1,0:T(8,128)} %param.13) | copy-start | bytes 4718596
  7.2 152.2 %all-gather.3.cloned.1.call-start = ((), (), s32[]{:S(2)}) async-start(), calls=%async_computation.2 | async-start | bytes 2359296 | tf_op jit(solution)/shard_map/all_gather | solution.py:225
  10.4 5.9 %copy-start.12 = (f32[32,32,128]{2,1,0:T(8,128)S(1)}, f32[32,32,128]{2,1,0:T(8,128)}, u32[]{:S(2)}) copy-start(f32[32,32,128]{2,1,0:T(8,128)} %param.14) | copy-start | bytes 1572868
  10.4 46.7 %collective-permute-start = (f32[2120,128]{1,0:T(8,128)}, f32[2120,128]{1,0:T(8,128)S(1)}, u32[]{:S(2)}, u32[]{:S(2)}) collective-permute-start(f32[2120,128]{1,0:T(8,128)} %select_maximum_fusion), channel_id=1, source_target_pairs={{0,0},{2,4},{4,2},{6,6},{1,1},{3,5},{5,3},{7,7},{8,8},{10,12},{12,... | collective-permute-start | bytes 3256328 | tf_op jit(solution)/shard_map/ppermute | solution.py:189
  17.4 39.7 %collective-permute-start.4 = (f32[16,4,32,128]{3,2,1,0:T(8,128)}, f32[16,4,32,128]{3,2,1,0:T(8,128)}, u32[]{:S(2)}, u32[]{:S(2)}) collective-permute-start(f32[16,4,32,128]{3,2,1,0:T(8,128)} %pad_maximum_fusion.2), channel_id=1, source_target_pairs={{2,0},{4,6},{3,1},{5,7},{10,8},{12,14},{11,9},{13,15},{18,16},{20,... | collective-permute-start | bytes 3145736 | tf_op jit(solution)/shard_map/ppermute | solution.py:192
  21.2 37.5 %copy-start.13 = (f32[1,32,128]{2,1,0:T(8,128)S(1)}, f32[1,32,128]{2,1,0:T(8,128)}, u32[]{:S(2)}) copy-start(f32[1,32,128]{2,1,0:T(8,128)} %param.17) | copy-start | bytes 49156
  21.2 76.1 %collective-permute-start.1 = (f32[32,4,32,128]{3,2,1,0:T(8,128)}, f32[32,4,32,128]{3,2,1,0:T(8,128)}, u32[]{:S(2)}, u32[]{:S(2)}) collective-permute-start(f32[32,4,32,128]{3,2,1,0:T(8,128)} %pad_maximum_fusion.refs_1_), channel_id=1, source_target_pairs={{0,1},{1,0},{6,7},{7,6},{8,9},{9,8},{14,15},{15,14},{16,17},{17,16... | collective-permute-start | bytes 6291464 | tf_op jit(solution)/shard_map/ppermute | solution.py:198
  23.4 52.2 %collective-permute-start.2 = (f32[16,4,32,128]{3,2,1,0:T(8,128)S(1)}, f32[16,4,32,128]{3,2,1,0:T(8,128)S(1)}, u32[]{:S(2)}, u32[]{:S(2)}) collective-permute-start(f32[16,4,32,128]{3,2,1,0:T(8,128)S(1)} %pad_maximum_fusion.1), channel_id=1, source_target_pairs={{2,0},{4,6},{3,1},{5,7},{10,8},{12,14},{11,9},{13,15},{18,16},{20,... | collective-permute-start | bytes 3145736 | tf_op jit(solution)/shard_map/ppermute | solution.py:192
  57.0 40.2 %collective-permute-start.5 = (f32[16,4,32,128]{3,2,1,0:T(8,128)}, f32[16,4,32,128]{3,2,1,0:T(8,128)}, u32[]{:S(2)}, u32[]{:S(2)}) collective-permute-start(f32[16,4,32,128]{3,2,1,0:T(8,128)} %collective-permute-done.4.refs_3_), channel_id=1, source_target_pairs={{0,1},{1,0},{6,7},{7,6},{8,9},{9,8},{14,15},{15,14},{16,17},{17,16... | collective-permute-start | bytes 3145736 | tf_op jit(solution)/shard_map/ppermute | solution.py:198
  75.6 6.2 %collective-permute-start.12 = (f32[4,32,128]{2,1,0:T(8,128)S(1)}, f32[4,32,128]{2,1,0:T(8,128)S(1)}, u32[]{:S(2)}, u32[]{:S(2)}) collective-permute-start(f32[4,32,128]{2,1,0:T(8,128)S(1)} %pad_maximum_fusion.7), channel_id=1, source_target_pairs={{0,2},{2,0},{1,3},{3,1},{4,6},{6,4},{5,7},{7,5},{8,10},{10,8},{9,1... | collective-permute-start | bytes 196616 | tf_op jit(solution)/shard_map/ppermute | solution.py:202
  81.8 14.7 %collective-permute-start.13 = (f32[2,4,32,128]{3,2,1,0:T(8,128)S(1)}, f32[2,4,32,128]{3,2,1,0:T(8,128)S(1)}, u32[]{:S(2)}, u32[]{:S(2)}) collective-permute-start(f32[2,4,32,128]{3,2,1,0:T(8,128)S(1)} %pad_maximum_fusion.6), channel_id=1, source_target_pairs={{0,1},{1,0},{2,3},{3,2},{4,5},{5,4},{6,7},{7,6},{8,9},{9,8},{10,11... | collective-permute-start | bytes 393224 | tf_op jit(solution)/shard_map/ppermute | solution.py:202
  97.2 17.8 %collective-permute-start.6 = (f32[32,4,32,128]{3,2,1,0:T(8,128)}, f32[32,4,32,128]{3,2,1,0:T(8,128)}, u32[]{:S(2)}, u32[]{:S(2)}) collective-permute-start(f32[32,4,32,128]{3,2,1,0:T(8,128)} %pad_maximum_fusion.refs_1_), channel_id=1, source_target_pairs={{0,4},{6,2},{1,5},{7,3},{8,12},{14,10},{9,13},{15,11},{16,20},{22,... | collective-permute-start | bytes 6291464 | tf_op jit(solution)/shard_map/ppermute | solution.py:195
  98.5 16.5 %collective-permute-start.7 = (f32[32,4,32,128]{3,2,1,0:T(8,128)}, f32[32,4,32,128]{3,2,1,0:T(8,128)}, u32[]{:S(2)}, u32[]{:S(2)}) collective-permute-start(f32[32,4,32,128]{3,2,1,0:T(8,128)} %collective-permute-done.1.refs_2_), channel_id=1, source_target_pairs={{0,4},{6,2},{1,5},{7,3},{8,12},{14,10},{9,13},{15,11},{16,20},{22,... | collective-permute-start | bytes 6291464 | tf_op jit(solution)/shard_map/ppermute | solution.py:195
  99.8 10.6 %collective-permute-start.10 = (f32[16,4,32,128]{3,2,1,0:T(8,128)}, f32[16,4,32,128]{3,2,1,0:T(8,128)S(1)}, u32[]{:S(2)}, u32[]{:S(2)}) collective-permute-start(f32[16,4,32,128]{3,2,1,0:T(8,128)} %collective-permute-done.4.refs_3_), channel_id=1, source_target_pairs={{0,4},{6,2},{1,5},{7,3},{8,12},{14,10},{9,13},{15,11},{16,20},{22,... | collective-permute-start | bytes 3145736 | tf_op jit(solution)/shard_map/ppermute | solution.py:195
  101.1 11.6 %collective-permute-start.3 = (f32[16,4,32,128]{3,2,1,0:T(8,128)S(1)}, f32[16,4,32,128]{3,2,1,0:T(8,128)S(1)}, u32[]{:S(2)}, u32[]{:S(2)}) collective-permute-start(f32[16,4,32,128]{3,2,1,0:T(8,128)S(1)} %collective-permute-done.2.refs_3_), channel_id=1, source_target_pairs={{0,1},{1,0},{6,7},{7,6},{8,9},{9,8},{14,15},{15,14},{16,17},{17,16... | collective-permute-start | bytes 3145736 | tf_op jit(solution)/shard_map/ppermute | solution.py:198
  101.9 13.2 %collective-permute-start.11 = (f32[16,4,32,128]{3,2,1,0:T(8,128)}, f32[16,4,32,128]{3,2,1,0:T(8,128)}, u32[]{:S(2)}, u32[]{:S(2)}) collective-permute-start(f32[16,4,32,128]{3,2,1,0:T(8,128)} %collective-permute-done.5.refs_4_), channel_id=1, source_target_pairs={{0,4},{6,2},{1,5},{7,3},{8,12},{14,10},{9,13},{15,11},{16,20},{22,... | collective-permute-start | bytes 3145736 | tf_op jit(solution)/shard_map/ppermute | solution.py:195
  110.5 1.0 copy-start.4
  111.5 17.8 %collective-permute-start.8 = (f32[16,4,32,128]{3,2,1,0:T(8,128)S(1)}, f32[16,4,32,128]{3,2,1,0:T(8,128)}, u32[]{:S(2)}, u32[]{:S(2)}) collective-permute-start(f32[16,4,32,128]{3,2,1,0:T(8,128)S(1)} %collective-permute-done.2.refs_3_), channel_id=1, source_target_pairs={{0,4},{6,2},{1,5},{7,3},{8,12},{14,10},{9,13},{15,11},{16,20},{22,... | collective-permute-start | bytes 3145736 | tf_op jit(solution)/shard_map/ppermute | solution.py:195
  112.8 16.5 %collective-permute-start.9 = (f32[16,4,32,128]{3,2,1,0:T(8,128)S(1)}, f32[16,4,32,128]{3,2,1,0:T(8,128)}, u32[]{:S(2)}, u32[]{:S(2)}) collective-permute-start(f32[16,4,32,128]{3,2,1,0:T(8,128)S(1)} %collective-permute-done.3.refs_4_), channel_id=1, source_target_pairs={{0,4},{6,2},{1,5},{7,3},{8,12},{14,10},{9,13},{15,11},{16,20},{22,... | collective-permute-start | bytes 3145736 | tf_op jit(solution)/shard_map/ppermute | solution.py:195
  115.1 1.2 copy-start.5
  128.4 0.8 copy-start.9
  140.8 0.8 copy-start.6
  141.6 24.1 %all-to-all-start = ((f32[8,5,8,128]{3,2,1,0:T(8,128)}), f32[8,5,8,128]{3,2,1,0:T(8,128)S(1)}, u32[]{:S(2)}, u32[]{:S(2)}) async-start(f32[8,5,8,128]{3,2,1,0:T(8,128)} %get-tuple-element.46), calls=%async_computation | async-start | bytes 327680 | tf_op jit(solution)/shard_map/all_to_all | solution.py:277
  159.3 1.6 copy-start.1
  165.6 14.0 %copy-start.2 = (bf16[16,384,128]{2,1,0:T(8,128)(2,1)S(1)}, bf16[16,384,128]{2,1,0:T(8,128)(2,1)}, u32[]{:S(2)}) copy-start(bf16[16,384,128]{2,1,0:T(8,128)(2,1)} %get-tuple-element.43.high) | copy-start | bytes 4718596
  165.6 14.0 %copy-start.7 = (f32[16,64,128]{2,1,0:T(8,128)S(1)}, f32[16,64,128]{2,1,0:T(8,128)}, u32[]{:S(2)}) copy-start(f32[16,64,128]{2,1,0:T(8,128)} %copy-done.6) | copy-start | bytes 1572868
  179.7 1.4 copy-start.3
  183.5 5.1 %copy-start.8 = (bf16[16,384,128]{2,1,0:T(8,128)(2,1)S(1)}, bf16[16,384,128]{2,1,0:T(8,128)(2,1)}, u32[]{:S(2)}) copy-start(bf16[16,384,128]{2,1,0:T(8,128)(2,1)} %get-tuple-element.54.high) | copy-start | bytes 4718596
  183.5 5.1 %copy-start.10 = (f32[16,64,128]{2,1,0:T(8,128)S(1)}, f32[16,64,128]{2,1,0:T(8,128)}, u32[]{:S(2)}) copy-start(f32[16,64,128]{2,1,0:T(8,128)} %copy-done.9) | copy-start | bytes 1572868
  186.7 16.9 %collective-permute-start.14 = (f32[8,64,128]{2,1,0:T(8,128)S(1)}, f32[8,64,128]{2,1,0:T(8,128)S(1)}, u32[]{:S(2)}, u32[]{:S(2)}) collective-permute-start(f32[8,64,128]{2,1,0:T(8,128)S(1)} %get-tuple-element.53), channel_id=1, source_target_pairs={{0,0},{2,4},{4,2},{6,6},{1,1},{3,5},{5,3},{7,7},{8,8},{10,12},{12,... | collective-permute-start | bytes 786440 | tf_op jit(solution)/shard_map/ppermute | solution.py:189
  191.8 20.6 %collective-permute-start.16 = (f32[17,64,128]{2,1,0:T(8,128)S(1)}, f32[17,64,128]{2,1,0:T(8,128)S(1)}, u32[]{:S(2)}, u32[]{:S(2)}) collective-permute-start(f32[17,64,128]{2,1,0:T(8,128)S(1)} %pad_maximum_fusion.4), channel_id=1, source_target_pairs={{0,0},{2,4},{4,2},{6,6},{1,1},{3,5},{5,3},{7,7},{8,8},{10,12},{12,... | collective-permute-start | bytes 1671176 | tf_op jit(solution)/shard_map/ppermute | solution.py:189
  203.6 11.6 %collective-permute-start.15 = (f32[8,64,128]{2,1,0:T(8,128)S(1)}, f32[8,64,128]{2,1,0:T(8,128)S(1)}, u32[]{:S(2)}, u32[]{:S(2)}) collective-permute-start(f32[8,64,128]{2,1,0:T(8,128)S(1)} %get-tuple-element.61), channel_id=1, source_target_pairs={{0,0},{2,4},{4,2},{6,6},{1,1},{3,5},{5,3},{7,7},{8,8},{10,12},{12,... | collective-permute-start | bytes 786440 | tf_op jit(solution)/shard_map/ppermute | solution.py:189
Sparse Core Ops, SparseCore 0:
  97.3 33.4 all-gather.2
